TPU v7x, 32 devices: a whole 2x2x4 slice. The times are simulated.
32 devices in a mesh: dp: 16 (over z, x, core), tensor: 2 (over y).
Axes of the slice: x: 2, y: 2, z: 4, core: 2. Of those that a mesh axis runs over, the one named last changes fastest.
Arguments:
- clean_images: bfloat16 [64, 256, 768], P(('dp', 'tensor')), may hold values from -6 to 6
- noise_draw: bfloat16 [64, 256, 768], P(('dp', 'tensor')), may hold values from -6 to 6
- levels: int32 [64], P(('dp', 'tensor')), may hold values from 0 to 999
- labels: int32 [64], P(('dp', 'tensor')), may hold values from 0 to 999
- dropped: int32 [64], P(('dp', 'tensor')), may hold values 0 or 1
- groups: int32 [64], P(('dp', 'tensor')), may hold values from 0 to 3
- step_count: int32 [1], replicated, may hold values from 1 to 20
- inward: float32 [1024, 3, 1024], P('dp', None, 'tensor'), may hold values from -0.1875 to 0.1875
- first_inward: float32 [1024, 3, 1024], P('dp', None, 'tensor'), may hold values from -2.744419e-06 to 2.744419e-06, as said below
- second_inward: float32 [1024, 3, 1024], P('dp', None, 'tensor'), may hold values from 3.347482e-12 to 1.3389928e-11
- outward: float32 [1024, 1024], P('tensor', 'dp'), may hold values from -0.75 to 0.75
- first_outward: float32 [1024, 1024], P('tensor', 'dp'), may hold values from -1.3722094e-06 to 1.3722094e-06, as said below
- second_outward: float32 [1024, 1024], P('tensor', 'dp'), may hold values from 8.368705e-13 to 3.347482e-12
- expand: float32 [1024, 2, 3072], P('dp', None, 'tensor'), may hold values from -0.1875 to 0.1875
- first_expand: float32 [1024, 2, 3072], P('dp', None, 'tensor'), may hold values from -1.029157e-06 to 1.029157e-06, as said below
- second_expand: float32 [1024, 2, 3072], P('dp', None, 'tensor'), may hold values from 4.7073966e-13 to 1.8829586e-12
- shrink: float32 [3072, 1024], P('tensor', 'dp'), may hold values from -0.109375 to 0.109375
- first_shrink: float32 [3072, 1024], P('tensor', 'dp'), may hold values from -2.744419e-06 to 2.744419e-06, as said below
- second_shrink: float32 [3072, 1024], P('tensor', 'dp'), may hold values from 3.347482e-12 to 1.3389928e-11
- patches: float32 [2, 768, 1024], P(None, ('dp', 'tensor')), may hold values from -0.1875 to 0.1875
- first_patches: float32 [2, 768, 1024], P(None, ('dp', 'tensor')), may hold values from -6.861047e-06 to 6.861047e-06, as said below
- second_patches: float32 [2, 768, 1024], P(None, ('dp', 'tensor')), may hold values from 2.0921763e-11 to 8.368705e-11
- classes: float32 [1001, 768], P(None, ('dp', 'tensor')), may hold values from -0.21875 to 0.21875
- first_classes: float32 [1001, 768], P(None, ('dp', 'tensor')), may hold values from -6.861047e-06 to 6.861047e-06, as said below
- second_classes: float32 [1001, 768], P(None, ('dp', 'tensor')), may hold values from 2.0921763e-11 to 8.368705e-11
- mapping: float32 [768, 4096], P(('dp', 'tensor')), may hold values from -0.21875 to 0.21875
- first_mapping: float32 [768, 4096], P(('dp', 'tensor')), may hold values from -6.861047e-06 to 6.861047e-06, as said below
- second_mapping: float32 [768, 4096], P(('dp', 'tensor')), may hold values from 2.0921763e-11 to 8.368705e-11
Outputs:
- total_loss: float32 [], replicated
- grad_norm: float32 [], replicated
- inward_next: float32 [1024, 3, 1024], P('dp', None, 'tensor')
- moment_inward: float32 [1024, 3, 1024], P('dp', None, 'tensor')
- square_inward: float32 [1024, 3, 1024], P('dp', None, 'tensor')
- outward_next: float32 [1024, 1024], P('tensor', 'dp')
- moment_outward: float32 [1024, 1024], P('tensor', 'dp')
- square_outward: float32 [1024, 1024], P('tensor', 'dp')
- expand_next: float32 [1024, 2, 3072], P('dp', None, 'tensor')
- moment_expand: float32 [1024, 2, 3072], P('dp', None, 'tensor')
- square_expand: float32 [1024, 2, 3072], P('dp', None, 'tensor')
- shrink_next: float32 [3072, 1024], P('tensor', 'dp')
- moment_shrink: float32 [3072, 1024], P('tensor', 'dp')
- square_shrink: float32 [3072, 1024], P('tensor', 'dp')
- patches_next: float32 [2, 768, 1024], P(None, ('dp', 'tensor'))
- moment_patches: float32 [2, 768, 1024], P(None, ('dp', 'tensor'))
- square_patches: float32 [2, 768, 1024], P(None, ('dp', 'tensor'))
- classes_next: float32 [1001, 768], P(None, ('dp', 'tensor'))
- moment_classes: float32 [1001, 768], P(None, ('dp', 'tensor'))
- square_classes: float32 [1001, 768], P(None, ('dp', 'tensor'))
- mapping_next: float32 [768, 4096], P(('dp', 'tensor'))
- moment_mapping: float32 [768, 4096], P(('dp', 'tensor'))
- square_mapping: float32 [768, 4096], P(('dp', 'tensor'))
Inputs may be any that keep to these rules, and one draw needn't show every extreme that they name: `first_inward`: entries of both signs. `first_outward`: entries of both signs. `first_expand`: entries of both signs. `first_shrink`: entries of both signs. `first_patches`: entries of both signs. `first_classes`: entries of both signs. `first_mapping`: entries of both signs.
All inputs are finite; a program needn't handle non-finite values. No bound on the sum of `dropped` on one device may be relied on, other than what follows from the above.
Results may differ from a plain program's by a relative error of at most 0.012.
Values may be sent and summed in bfloat16 or wider, within the bound.
No kernel may reach another device: no remote copies, remote signals or barrier semaphores. Data moves between devices by JAX's collectives and lax.ppermute only.
A program may use at most 256 MiB of HBM per device.

v0:
```python
import math

import jax
import jax.numpy as jnp
from jax import lax
from jax.sharding import PartitionSpec as P

D = 1024
HEAD_DIM = 64
CD = 768
CLASSES = 1001
PD = 768
FOUR = 256
SEQ = 256
GROUPS = 4
NLEVELS = 1000


HIGH = lax.Precision.HIGHEST
SIGMA_DATA = 0.5
LEARN_RATE = 0.05
DECAY = 0.1
BETA_ONE = 0.5
BETA_TWO = 0.5
ADAM_EPS = 1e-08
CLIP = 0.02
NORM_EPS = 1e-06


def to_low(value):
    return value.astype(jnp.bfloat16).astype(jnp.float32)


def rms_norm(value):
    return value * lax.rsqrt(jnp.mean(value * value, axis=-1, keepdims=True) + NORM_EPS)


def einsum_low(form, left, right):
    return jnp.einsum(form, left, right, preferred_element_type=jnp.float32)


def outer_sum(left, right):
    return jnp.dot(left.T, right, precision=HIGH)


def noise_terms(levels):
    log_sigma = -3.0 + 6.0 * levels.astype(jnp.float32) / (NLEVELS - 1)
    sigma = jnp.exp(log_sigma)
    radius = jnp.sqrt(sigma * sigma + SIGMA_DATA * SIGMA_DATA)
    half = FOUR // 2
    freqs = jnp.exp(-2.0 + 4.0 * jnp.arange(half, dtype=jnp.float32) / (half - 1))
    angles = 2.0 * math.pi * (log_sigma / 4.0)[:, None] * freqs[None, :]
    return (sigma, radius, jnp.concatenate([jnp.cos(angles), jnp.sin(angles)], axis=1))


def map_forward(feats, onehot, table, mats):
    feats_low = to_low(feats)
    cond_zero = jnp.dot(onehot, table, precision=HIGH) + jnp.dot(
        feats_low, mats[:, :FOUR].T, precision=HIGH
    )
    normed = to_low(rms_norm(cond_zero))
    inner = jnp.dot(normed, mats[:, FOUR : FOUR + CD], precision=HIGH)
    cond_low = to_low(cond_zero + jax.nn.gelu(inner))
    scales = 1.0 + jnp.dot(cond_low, mats[:, FOUR + CD :], precision=HIGH)
    return (scales, (feats_low, cond_zero, normed, inner, cond_low))


def map_backward(mats, kept, grad_scales):
    feats_low, cond_zero, normed, inner, cond_low = kept
    grad_cond = jnp.dot(grad_scales, mats[:, FOUR + CD :].T, precision=HIGH)
    _, pull_gelu = jax.vjp(jax.nn.gelu, inner)
    (grad_inner,) = pull_gelu(grad_cond)
    grad_normed = jnp.dot(grad_inner, mats[:, FOUR : FOUR + CD].T, precision=HIGH)
    _, pull_norm = jax.vjp(rms_norm, cond_zero)
    (grad_zero,) = pull_norm(grad_normed)
    return (grad_zero + grad_cond, grad_inner)


def scale_norm(hidden, scale):
    return rms_norm(hidden) * scale[:, None, :]


def norm_back(hidden, scale, grad):
    _, pull = jax.vjp(scale_norm, hidden, scale)
    return pull(grad)


def pair_rows(value):
    return lax.all_gather(value, "tensor", axis=0, tiled=True)


def pair_sum(value):
    return lax.psum_scatter(value, "tensor", scatter_dimension=0, tiled=True)


def split_heads(project):
    images, tokens = (project.shape[0], project.shape[1])
    heads = project.shape[3] // HEAD_DIM
    return tuple(
        (project[:, :, part].reshape(images, tokens, heads, HEAD_DIM) for part in range(3))
    )


def attention_probs(queries, keys, totals):
    scores = einsum_low("iqhe,ikhe->ihqk", queries, keys) * (1.0 / math.sqrt(HEAD_DIM))
    return jnp.exp(scores - totals)


def layer_forward(big, patch_pair, inputs, scales):
    attn_in, attn_out, gate_up, down = big
    resid_zero = einsum_low("isp,pd->isd", inputs, patch_pair[0])
    rows_zero = pair_rows(scale_norm(resid_zero, scales[:, 0]).astype(jnp.bfloat16))
    project = einsum_low("isd,dke->iske", rows_zero, attn_in).astype(jnp.bfloat16)
    queries, keys, values = split_heads(project)
    scores = einsum_low("iqhe,ikhe->ihqk", queries, keys) * (1.0 / math.sqrt(HEAD_DIM))
    totals = jax.nn.logsumexp(scores, axis=-1, keepdims=True)
    probs = jnp.exp(scores - totals).astype(jnp.bfloat16)
    mixed = einsum_low("ihqk,ikhe->iqhe", probs, values).astype(jnp.bfloat16)
    mixed = mixed.reshape(mixed.shape[0], mixed.shape[1], -1)
    resid_one = resid_zero + pair_sum(einsum_low("isd,de->ise", mixed, attn_out))
    rows_one = pair_rows(scale_norm(resid_one, scales[:, 1]).astype(jnp.bfloat16))
    gated = einsum_low("isd,dkf->iskf", rows_one, gate_up)
    hidden = (jax.nn.gelu(gated[:, :, 0]) * gated[:, :, 1]).astype(jnp.bfloat16)
    resid_two = resid_one + pair_sum(einsum_low("isf,fd->isd", hidden, down))
    last = scale_norm(resid_two, scales[:, 2]).astype(jnp.bfloat16)
    output = einsum_low("isd,pd->isp", last, patch_pair[1])
    return (
        resid_zero,
        rows_zero,
        project,
        totals,
        mixed,
        resid_one,
        rows_one,
        gated,
        hidden,
        resid_two,
        last,
        output,
    )


def layer_backward(big, patch_pair, inputs, scales, kept, grad_out):
    attn_in, attn_out, gate_up, down = big
    (
        resid_zero,
        rows_zero,
        project,
        totals,
        mixed,
        resid_one,
        rows_one,
        gated,
        hidden,
        resid_two,
        last,
        output,
    ) = kept
    grad_low = grad_out.astype(jnp.bfloat16)
    grad_last = einsum_low("isp,pd->isd", grad_low, patch_pair[1])
    grad_patch_out = einsum_low("isp,isd->pd", grad_low, last)
    grad_two, scale_two = norm_back(resid_two, scales[:, 2], grad_last)
    rows_grad = pair_rows(grad_two.astype(jnp.bfloat16))
    grad_hidden = einsum_low("isd,fd->isf", rows_grad, down)
    grad_down = einsum_low("isf,isd->fd", hidden, rows_grad)
    _, pull_gate = jax.vjp(
        lambda gate, upper: jax.nn.gelu(gate) * upper, gated[:, :, 0], gated[:, :, 1]
    )
    grad_gate, grad_up = pull_gate(grad_hidden)
    grad_gated = jnp.stack([grad_gate, grad_up], axis=2).astype(jnp.bfloat16)
    grad_gate_up = einsum_low("isd,iskf->dkf", rows_one, grad_gated)
    part_one, scale_one = norm_back(
        resid_one, scales[:, 1], pair_sum(einsum_low("iskf,dkf->isd", grad_gated, gate_up))
    )
    grad_one = grad_two + part_one
    rows_grad = pair_rows(grad_one.astype(jnp.bfloat16))
    queries, keys, values = split_heads(project)
    grad_mixed = (
        einsum_low("isd,ed->ise", rows_grad, attn_out).astype(jnp.bfloat16).reshape(queries.shape)
    )
    grad_attn_out = einsum_low("ise,isd->ed", mixed, rows_grad)
    probs = attention_probs(queries, keys, totals)
    grad_values = einsum_low("ihqk,iqhe->ikhe", probs.astype(jnp.bfloat16), grad_mixed)
    grad_probs = einsum_low("iqhe,ikhe->ihqk", grad_mixed, values)
    grad_scores = (
        probs * (grad_probs - jnp.sum(grad_probs * probs, axis=-1, keepdims=True))
    ).astype(jnp.bfloat16)
    inverse_root = 1.0 / math.sqrt(HEAD_DIM)
    grad_queries = einsum_low("ihqk,ikhe->iqhe", grad_scores, keys) * inverse_root
    grad_keys = einsum_low("ihqk,iqhe->ikhe", grad_scores, queries) * inverse_root
    grad_project = jnp.stack([grad_queries, grad_keys, grad_values], axis=2)
    grad_project = grad_project.reshape(project.shape).astype(jnp.bfloat16)
    grad_attn_in = einsum_low("isd,iske->dke", rows_zero, grad_project)
    part_zero, scale_zero = norm_back(
        resid_zero, scales[:, 0], pair_sum(einsum_low("iske,dke->isd", grad_project, attn_in))
    )
    grad_zero = (grad_one + part_zero).astype(jnp.bfloat16)
    grad_patch_in = einsum_low("isp,isd->pd", inputs, grad_zero)
    grad_scales = jnp.stack([scale_zero, scale_one, scale_two], axis=1)
    return (
        (grad_attn_in, grad_attn_out, grad_gate_up, grad_down),
        jnp.stack([grad_patch_in, grad_patch_out]),
        grad_scales,
    )


def body(
    clean_images,
    noise_draw,
    levels,
    labels,
    dropped,
    groups,
    step_count,
    inward,
    first_inward,
    second_inward,
    outward,
    first_outward,
    second_outward,
    expand,
    first_expand,
    second_expand,
    shrink,
    first_shrink,
    second_shrink,
    patches,
    first_patches,
    second_patches,
    classes,
    first_classes,
    second_classes,
    mapping,
    first_mapping,
    second_mapping,
):
    masters = (inward, outward, expand, shrink, patches, classes, mapping)
    firsts = (
        first_inward,
        first_outward,
        first_expand,
        first_shrink,
        first_patches,
        first_classes,
        first_mapping,
    )
    seconds = (
        second_inward,
        second_outward,
        second_expand,
        second_shrink,
        second_patches,
        second_classes,
        second_mapping,
    )
    big = (
        lax.all_gather(inward.astype(jnp.bfloat16), "dp", axis=0, tiled=True),
        lax.all_gather(outward.astype(jnp.bfloat16), "dp", axis=1, tiled=True),
        lax.all_gather(expand.astype(jnp.bfloat16), "dp", axis=0, tiled=True),
        lax.all_gather(shrink.astype(jnp.bfloat16), "dp", axis=1, tiled=True),
    )
    small = (
        lax.all_gather(patches.astype(jnp.bfloat16), ("dp", "tensor"), axis=1, tiled=True),
        lax.all_gather(classes.astype(jnp.bfloat16), ("dp", "tensor"), axis=1, tiled=True),
        lax.all_gather(mapping.astype(jnp.bfloat16), ("dp", "tensor"), axis=0, tiled=True),
    )
    sigma, radius, feats = noise_terms(levels)
    chosen = jnp.where(dropped == 1, CLASSES - 1, labels)
    onehot = (chosen[:, None] == jnp.arange(CLASSES)[None, :]).astype(jnp.float32)
    map_mats = small[2].astype(jnp.float32)
    scale_flat, map_kept = map_forward(feats, onehot, small[1].astype(jnp.float32), map_mats)
    scales = scale_flat.reshape(-1, 3, D)
    sig = sigma[:, None, None]
    rad = radius[:, None, None]
    clean_float = clean_images.astype(jnp.float32)
    noise_float = noise_draw.astype(jnp.float32)
    inputs = ((clean_float + sig * noise_float) / rad).astype(jnp.bfloat16)
    target = (sig * clean_float - SIGMA_DATA * SIGMA_DATA * noise_float) / (SIGMA_DATA * rad)
    kept = layer_forward(big, small[0], inputs, scales)
    output = kept[-1]
    counts = jnp.sum((groups[:, None] == groups[None, :]).astype(jnp.float32), axis=1)
    weight = 1.0 / (GROUPS * counts)
    local_loss = jnp.sum(weight * jnp.mean((output - target) ** 2, axis=(1, 2)))
    total_loss = lax.psum(local_loss, ("dp", "tensor"))
    grad_out = 2.0 * (output - target) * (weight / (SEQ * PD))[:, None, None]
    backward_big = (
        lax.all_gather(inward.astype(jnp.bfloat16), "dp", axis=0, tiled=True),
        lax.all_gather(outward.astype(jnp.bfloat16), "dp", axis=1, tiled=True),
        lax.all_gather(expand.astype(jnp.bfloat16), "dp", axis=0, tiled=True),
        lax.all_gather(shrink.astype(jnp.bfloat16), "dp", axis=1, tiled=True),
    )
    big_grads, patch_grads, scale_grads = layer_backward(
        backward_big, small[0], inputs, scales, kept, grad_out
    )
    grad_scales = scale_grads.reshape(-1, 3 * D)
    grad_zero, grad_inner = map_backward(map_mats, map_kept, grad_scales)
    feats_low, cond_zero, normed, inner, cond_low = map_kept
    big_shards = (
        lax.psum_scatter(big_grads[0], "dp", scatter_dimension=0, tiled=True),
        lax.psum_scatter(big_grads[1], "dp", scatter_dimension=1, tiled=True),
        lax.psum_scatter(big_grads[2], "dp", scatter_dimension=0, tiled=True),
        lax.psum_scatter(big_grads[3], "dp", scatter_dimension=1, tiled=True),
    )
    table_grad = outer_sum(onehot, grad_zero)
    mapping_grad = jnp.concatenate(
        [
            outer_sum(grad_zero, feats_low),
            outer_sum(normed, grad_inner),
            outer_sum(cond_low, grad_scales),
        ],
        axis=1,
    )
    small_shards = (
        lax.psum_scatter(patch_grads, ("dp", "tensor"), scatter_dimension=1, tiled=True),
        lax.psum_scatter(table_grad, ("dp", "tensor"), scatter_dimension=1, tiled=True),
        lax.psum_scatter(mapping_grad, ("dp", "tensor"), scatter_dimension=0, tiled=True),
    )
    grads = tuple(big_shards) + tuple(small_shards)
    squares = sum((jnp.sum(grad * grad) for grad in grads))
    squares_total = lax.psum(squares, ("dp", "tensor"))
    grad_norm = jnp.sqrt(squares_total)
    factor = CLIP / (grad_norm + NORM_EPS)
    count = step_count[0].astype(jnp.float32)
    fix_one = 1.0 - jnp.power(BETA_ONE, count)
    fix_two = 1.0 - jnp.power(BETA_TWO, count)
    results = [total_loss, grad_norm]
    for master, first, second, grad in zip(masters, firsts, seconds, grads):
        clipped = grad * factor
        moment = BETA_ONE * first + (1.0 - BETA_ONE) * clipped
        square = BETA_TWO * second + (1.0 - BETA_TWO) * clipped * clipped
        step_size = moment / fix_one / (jnp.sqrt(square / fix_two) + ADAM_EPS)
        results.extend([master - LEARN_RATE * (step_size + DECAY * master), moment, square])
    return tuple(results)


def solution(mesh):
    in_specs = (
        P(("dp", "tensor"), None, None),
        P(("dp", "tensor"), None, None),
        P(("dp", "tensor")),
        P(("dp", "tensor")),
        P(("dp", "tensor")),
        P(("dp", "tensor")),
        P(),
        P("dp", None, "tensor"),
        P("dp", None, "tensor"),
        P("dp", None, "tensor"),
        P("tensor", "dp"),
        P("tensor", "dp"),
        P("tensor", "dp"),
        P("dp", None, "tensor"),
        P("dp", None, "tensor"),
        P("dp", None, "tensor"),
        P("tensor", "dp"),
        P("tensor", "dp"),
        P("tensor", "dp"),
        P(None, ("dp", "tensor"), None),
        P(None, ("dp", "tensor"), None),
        P(None, ("dp", "tensor"), None),
        P(None, ("dp", "tensor")),
        P(None, ("dp", "tensor")),
        P(None, ("dp", "tensor")),
        P(("dp", "tensor"), None),
        P(("dp", "tensor"), None),
        P(("dp", "tensor"), None),
    )
    out_specs = (
        P(),
        P(),
        P("dp", None, "tensor"),
        P("dp", None, "tensor"),
        P("dp", None, "tensor"),
        P("tensor", "dp"),
        P("tensor", "dp"),
        P("tensor", "dp"),
        P("dp", None, "tensor"),
        P("dp", None, "tensor"),
        P("dp", None, "tensor"),
        P("tensor", "dp"),
        P("tensor", "dp"),
        P("tensor", "dp"),
        P(None, ("dp", "tensor"), None),
        P(None, ("dp", "tensor"), None),
        P(None, ("dp", "tensor"), None),
        P(None, ("dp", "tensor")),
        P(None, ("dp", "tensor")),
        P(None, ("dp", "tensor")),
        P(("dp", "tensor"), None),
        P(("dp", "tensor"), None),
        P(("dp", "tensor"), None),
    )
    return jax.shard_map(body, mesh=mesh, in_specs=in_specs, out_specs=out_specs, check_vma=False)
```

profile of v0, /device:TPU:0, one launch (start us, length us, event | category | flops | bytes accessed | tf_op | source)
XLA Modules:
  0.0 1666.4 jit_solution(6635196143196874810)
XLA Ops:
  16.0 57.3 %all-gather.12.cloned.1.call-done = bf16[2,768,1024]{2,1,0:T(8,128)(2,1)} async-done(((bf16[2,24,1024]{2,1,0:T(8,128)(2,1)}), bf16[2,768,1024]{2,1,0:T(8,128)(2,1)}) %all-gather.12.cloned.1.call-update) | async-done | bytes 3145744 | tf_op jit(solution)/shard_map/all_gather | solution.py:263
  76.4 68.7 %all-gather.16.cloned.1.call-done = bf16[768,4096]{1,0:T(8,128)(2,1)} async-done(((bf16[24,4096]{1,0:T(8,128)(2,1)}), bf16[768,4096]{1,0:T(8,128)(2,1)}) %all-gather.16.cloned.1.call-update) | async-done | bytes 6291472 | tf_op jit(solution)/shard_map/all_gather | solution.py:265
  146.3 55.9 %all-gather.14.cloned.1.call-done = bf16[1001,768]{0,1:T(8,128)(2,1)} async-done(((bf16[1001,24]{0,1:T(8,128)(2,1)}), bf16[1001,768]{0,1:T(8,128)(2,1)}) %all-gather.14.cloned.1.call-update) | async-done | bytes 1537552 | tf_op jit(solution)/shard_map/all_gather | solution.py:264
  212.2 36.7 %all-gather.20.cloned.1.call-done = bf16[1024,3,512]{2,0,1:T(8,128)(2,1)} async-done(((bf16[64,3,512]{2,0,1:T(8,128)(2,1)}), bf16[1024,3,512]{2,0,1:T(8,128)(2,1)}) %all-gather.20.cloned.1.call-update) | async-done | bytes 3145744 | tf_op jit(solution)/shard_map/all_gather | solution.py:257
  248.9 33.4 %all-gather.18.cloned.1.call-done = bf16[4,256,1024]{2,1,0:T(8,128)(2,1)} async-done(((bf16[2,256,1024]{2,1,0:T(8,128)(2,1)}), bf16[4,256,1024]{2,1,0:T(8,128)(2,1)}) %all-gather.18.cloned.1.call-update) | async-done | bytes 2097168 | tf_op jit(solution)/shard_map/all_gather | solution.py:89
  298.6 24.3 %all-gather.22.cloned.1.call-done = bf16[512,1024]{0,1:T(8,128)(2,1)} async-done(((bf16[512,64]{0,1:T(8,128)(2,1)}), bf16[512,1024]{0,1:T(8,128)(2,1)}) %all-gather.22.cloned.1.call-update) | async-done | bytes 1048592 | tf_op jit(solution)/shard_map/all_gather | solution.py:258
  329.9 50.9 %reduce-scatter.12.cloned.1.call-done = f32[2,256,1024]{2,1,0:T(8,128)} async-done(((f32[4,256,1024]{2,1,0:T(8,128)}), f32[2,256,1024]{2,1,0:T(8,128)}) %reduce-scatter.12.cloned.1.call-update) | async-done | bytes 2097168 | tf_op jit(solution)/shard_map/reduce_scatter | solution.py:93
  386.5 59.3 %all-gather.26.cloned.1.call-done = bf16[1024,2,1536]{2,0,1:T(8,128)(2,1)} async-done(((bf16[64,2,1536]{2,0,1:T(8,128)(2,1)}), bf16[1024,2,1536]{2,0,1:T(8,128)(2,1)}) %all-gather.26.cloned.1.call-update) | async-done | bytes 6291472 | tf_op jit(solution)/shard_map/all_gather | solution.py:259
  445.9 33.4 %all-gather.24.cloned.1.call-done = bf16[4,256,1024]{2,1,0:T(8,128)(2,1)} async-done(((bf16[2,256,1024]{2,1,0:T(8,128)(2,1)}), bf16[4,256,1024]{2,1,0:T(8,128)(2,1)}) %all-gather.24.cloned.1.call-update) | async-done | bytes 2097168 | tf_op jit(solution)/shard_map/all_gather | solution.py:89
  479.2 9.4 fusion.9
  496.6 31.1 %all-gather.28.cloned.1.call-done = bf16[1536,1024]{0,1:T(8,128)(2,1)} async-done(((bf16[1536,64]{0,1:T(8,128)(2,1)}), bf16[1536,1024]{0,1:T(8,128)(2,1)}) %all-gather.28.cloned.1.call-update) | async-done | bytes 3145744 | tf_op jit(solution)/shard_map/all_gather | solution.py:260
  527.6 8.4 fusion.24
  536.9 52.4 %reduce-scatter.14.cloned.1.call-done = f32[2,256,1024]{2,1,0:T(8,128)} async-done(((f32[4,256,1024]{2,1,0:T(8,128)}), f32[2,256,1024]{2,1,0:T(8,128)}) %reduce-scatter.14.cloned.1.call-update) | async-done | bytes 2097168 | tf_op jit(solution)/shard_map/reduce_scatter | solution.py:93
  597.9 33.2 %all-gather.30.cloned.1.call-done = bf16[4,256,1024]{2,1,0:T(8,128)(2,1)} async-done(((bf16[2,256,1024]{2,1,0:T(8,128)(2,1)}), bf16[4,256,1024]{2,1,0:T(8,128)(2,1)}) %all-gather.30.cloned.1.call-update) | async-done | bytes 2097168 | tf_op jit(solution)/shard_map/all_gather | solution.py:89
  631.1 11.2 fusion.28
  645.1 10.2 fusion.32
  655.3 54.4 %reduce-scatter.16.cloned.1.call-done = f32[2,256,1024]{2,1,0:T(8,128)} async-done(((f32[4,256,1024]{2,1,0:T(8,128)}), f32[2,256,1024]{2,1,0:T(8,128)}) %reduce-scatter.16.cloned.1.call-update) | async-done | bytes 2097168 | tf_op jit(solution)/shard_map/reduce_scatter | solution.py:93
  717.0 33.0 %all-gather.32.cloned.1.call-done = bf16[4,256,1024]{2,1,0:T(8,128)(2,1)} async-done(((bf16[2,256,1024]{2,1,0:T(8,128)(2,1)}), bf16[4,256,1024]{2,1,0:T(8,128)(2,1)}) %all-gather.32.cloned.1.call-update) | async-done | bytes 2097168 | tf_op jit(solution)/shard_map/all_gather | solution.py:89
  772.4 7.6 fusion.35
  781.9 7.1 convolution_bitcast_fusion.1
  794.5 12.8 convolution_bitcast_fusion
  809.1 7.1 convolution_bitcast_fusion.2
  816.3 18.1 %reduce-scatter.26.cloned.1.call-done = f32[2,256,1024]{2,1,0:T(8,128)} async-done(((f32[4,256,1024]{2,1,0:T(8,128)}), f32[2,256,1024]{2,1,0:T(8,128)}) %reduce-scatter.26.cloned.1.call-update) | async-done | bytes 2097168 | tf_op jit(solution)/shard_map/reduce_scatter | solution.py:93
  836.7 6.1 fusion.12
  872.1 51.5 %reduce-scatter.24.cloned.1.call-done = f32[1536,64]{0,1:T(8,128)} async-done(((f32[1536,1024]{0,1:T(8,128)}), f32[1536,64]{0,1:T(8,128)}) %reduce-scatter.24.cloned.1.call-update) | async-done | bytes 393232 | tf_op jit(solution)/shard_map/reduce_scatter | solution.py:302
  925.3 63.1 %reduce-scatter.20.cloned.1.call-done = f32[512,64]{0,1:T(8,128)} async-done(((f32[512,1024]{0,1:T(8,128)}), f32[512,64]{0,1:T(8,128)}) %reduce-scatter.20.cloned.1.call-update) | async-done | bytes 131088 | tf_op jit(solution)/shard_map/reduce_scatter | solution.py:300
  989.9 136.0 %reduce-scatter.22.cloned.1.call-done = f32[64,2,1536]{2,0,1:T(8,128)} async-done(((f32[1024,2,1536]{2,0,1:T(8,128)}), f32[64,2,1536]{2,0,1:T(8,128)}) %reduce-scatter.22.cloned.1.call-update) | async-done | bytes 786448 | tf_op jit(solution)/shard_map/reduce_scatter | solution.py:301
  1127.9 86.4 %reduce-scatter.18.cloned.1.call-done = f32[64,3,512]{2,0,1:T(8,128)} async-done(((f32[1024,3,512]{2,0,1:T(8,128)}), f32[64,3,512]{2,0,1:T(8,128)}) %reduce-scatter.18.cloned.1.call-update) | async-done | bytes 393232 | tf_op jit(solution)/shard_map/reduce_scatter | solution.py:299
  1218.6 102.8 %reduce-scatter.30.cloned.1.call-done = f32[1001,24]{0,1:T(8,128)} async-done(((f32[1001,768]{0,1:T(8,128)}), f32[1001,24]{0,1:T(8,128)}) %reduce-scatter.30.cloned.1.call-update) | async-done | bytes 96112 | tf_op jit(solution)/shard_map/reduce_scatter | solution.py:315
  1322.9 118.4 %reduce-scatter.28.cloned.1.call-done = f32[2,24,1024]{2,1,0:T(8,128)} async-done(((f32[2,768,1024]{2,1,0:T(8,128)}), f32[2,24,1024]{2,1,0:T(8,128)}) %reduce-scatter.28.cloned.1.call-update) | async-done | bytes 196624 | tf_op jit(solution)/shard_map/reduce_scatter | solution.py:314
  1444.1 158.1 %reduce-scatter.32.cloned.1.call-done = f32[24,4096]{1,0:T(8,128)} async-done(((f32[768,4096]{1,0:T(8,128)}), f32[24,4096]{1,0:T(8,128)}) %reduce-scatter.32.cloned.1.call-update) | async-done | bytes 393232 | tf_op jit(solution)/shard_map/reduce_scatter | solution.py:316
  1604.6 40.2 %all-reduce = (f32[]{:T(128)}, f32[]{:T(128)}) all-reduce(f32[]{:T(128)} %multiply_reduce_fusion.21, f32[]{:T(128)S(6)} %add.296), channel_id=1, replica_groups=mesh['dp'=16,'tensor'=2] {'dp','tensor'}, use_global_device_ids=true, to_apply=%region_11.12 | all-reduce | flops 2 | bytes 16 | tf_op jit(solution)/shard_map/psum | solution.py:284
  (327 shorter events, 165.2 us)
Async XLA Ops:
  7.2 66.2 %all-gather.12.cloned.1.call-start = ((), (), s32[]{:S(2)}) async-start(), calls=%async_computation.11 | async-start | bytes 3244032 | tf_op jit(solution)/shard_map/all_gather | solution.py:263
  8.8 136.3 %all-gather.16.cloned.1.call-start = ((), (), s32[]{:S(2)}) async-start(), calls=%async_computation.13 | async-start | bytes 6488064 | tf_op jit(solution)/shard_map/all_gather | solution.py:265
  10.6 191.6 %all-gather.14.cloned.1.call-start = ((), (), s32[]{:S(2)}) async-start(), calls=%async_computation.12 | async-start | bytes 1622016 | tf_op jit(solution)/shard_map/all_gather | solution.py:264
  12.2 236.7 %all-gather.20.cloned.1.call-start = ((), (), s32[]{:S(2)}) async-start(), calls=%async_computation.15 | async-start | bytes 3342336 | tf_op jit(solution)/shard_map/all_gather | solution.py:257
  14.0 268.3 %all-gather.18.cloned.1.call-start = ((), (), s32[]{:S(2)}) async-start(), calls=%async_computation.14 | async-start | bytes 3145728 | tf_op jit(solution)/shard_map/all_gather | solution.py:89
  14.7 187.5 %copy-start.76 = (s32[2]{0:T(128)}, s32[2]{0:T(128)S(1)}, u32[]{:S(2)}) copy-start(s32[2]{0:T(128)S(1)} %compare_select_fusion) | copy-start | bytes 28
  15.9 60.5 %copy-start.82 = (f32[2]{0:T(128)}, f32[2]{0:T(128)S(1)}, u32[]{:S(2)}) copy-start(f32[2]{0:T(128)S(1)} %get-tuple-element.165) | copy-start | bytes 28
  16.0 129.1 %copy-start.72 = (bf16[2,128]{1,0:T(2,128)(2,1)}, bf16[2,128]{1,0:T(2,128)(2,1)S(1)}, u32[]{:S(2)}) copy-start(bf16[2,128]{1,0:T(2,128)(2,1)S(1)} %get-tuple-element.162) | copy-start | bytes 1540
  16.0 129.1 %copy-start.74 = (bf16[2,128]{1,0:T(2,128)(2,1)}, bf16[2,128]{1,0:T(2,128)(2,1)S(1)}, u32[]{:S(2)}) copy-start(bf16[2,128]{1,0:T(2,128)(2,1)S(1)} %get-tuple-element.163) | copy-start | bytes 1540
  76.4 68.7 %copy-start.68 = (f32[2,256]{1,0:T(2,128)}, f32[2,256]{1,0:T(2,128)S(1)}, u32[]{:S(2)}) copy-start(f32[2,256]{1,0:T(2,128)S(1)} %get-tuple-element.168) | copy-start | bytes 6148
  76.4 133.8 %copy-start.4 = (f32[2,256,1024]{2,1,0:T(8,128)}, f32[2,256,1024]{2,1,0:T(8,128)S(1)}, u32[]{:S(2)}) copy-start(f32[2,256,1024]{2,1,0:T(8,128)S(1)} %get-tuple-element.169) | copy-start | bytes 6291460
  76.4 133.8 %copy-start.64 = (f32[2,256]{1,0:T(2,128)}, f32[2,256]{1,0:T(2,128)S(1)}, u32[]{:S(2)}) copy-start(f32[2,256]{1,0:T(2,128)S(1)} %fusion.85) | copy-start | bytes 6148
  211.5 111.4 %all-gather.22.cloned.1.call-start = ((), (), s32[]{:S(2)}) async-start(), calls=%async_computation.16 | async-start | bytes 1114112 | tf_op jit(solution)/shard_map/all_gather | solution.py:258
  212.2 168.6 %reduce-scatter.12.cloned.1.call-start = ((), (), s32[]{:S(2)}) async-start(), calls=%async_computation.17 | async-start | bytes 6291456 | tf_op jit(solution)/shard_map/reduce_scatter | solution.py:93
  327.4 118.5 %all-gather.26.cloned.1.call-start = ((), (), s32[]{:S(2)}) async-start(), calls=%async_computation.19 | async-start | bytes 6684672 | tf_op jit(solution)/shard_map/all_gather | solution.py:259
  329.4 149.8 %all-gather.24.cloned.1.call-start = ((), (), s32[]{:S(2)}) async-start(), calls=%async_computation.18 | async-start | bytes 3145728 | tf_op jit(solution)/shard_map/all_gather | solution.py:89
  385.7 141.9 %all-gather.28.cloned.1.call-start = ((), (), s32[]{:S(2)}) async-start(), calls=%async_computation.20 | async-start | bytes 3342336 | tf_op jit(solution)/shard_map/all_gather | solution.py:260
  386.5 202.8 %reduce-scatter.14.cloned.1.call-start = ((), (), s32[]{:S(2)}) async-start(), calls=%async_computation.21 | async-start | bytes 6291456 | tf_op jit(solution)/shard_map/reduce_scatter | solution.py:93
  536.0 95.1 %all-gather.30.cloned.1.call-start = ((), (), s32[]{:S(2)}) async-start(), calls=%async_computation.22 | async-start | bytes 3145728 | tf_op jit(solution)/shard_map/all_gather | solution.py:89
  597.8 111.9 %reduce-scatter.16.cloned.1.call-start = ((), (), s32[]{:S(2)}) async-start(), calls=%async_computation.23 | async-start | bytes 6291456 | tf_op jit(solution)/shard_map/reduce_scatter | solution.py:93
  655.3 94.8 %all-gather.32.cloned.1.call-start = ((), (), s32[]{:S(2)}) async-start(), calls=%async_computation.24 | async-start | bytes 3145728 | tf_op jit(solution)/shard_map/all_gather | solution.py:89
  716.8 117.6 %reduce-scatter.26.cloned.1.call-start = ((), (), s32[]{:S(2)}) async-start(), calls=%async_computation.29 | async-start | bytes 6291456 | tf_op jit(solution)/shard_map/reduce_scatter | solution.py:93
  780.0 143.6 %reduce-scatter.24.cloned.1.call-start = ((), (), s32[]{:S(2)}) async-start(), calls=%async_computation.28 | async-start | bytes 6684672 | tf_op jit(solution)/shard_map/reduce_scatter | solution.py:302
  789.0 199.4 %reduce-scatter.20.cloned.1.call-start = ((), (), s32[]{:S(2)}) async-start(), calls=%async_computation.26 | async-start | bytes 2228224 | tf_op jit(solution)/shard_map/reduce_scatter | solution.py:300
  794.5 331.5 %reduce-scatter.22.cloned.1.call-start = ((), (), s32[]{:S(2)}) async-start(), calls=%async_computation.27 | async-start | bytes 13369344 | tf_op jit(solution)/shard_map/reduce_scatter | solution.py:301
  807.3 407.0 %reduce-scatter.18.cloned.1.call-start = ((), (), s32[]{:S(2)}) async-start(), calls=%async_computation.25 | async-start | bytes 6684672 | tf_op jit(solution)/shard_map/reduce_scatter | solution.py:299
  816.3 505.1 %reduce-scatter.30.cloned.1.call-start = ((), (), s32[]{:S(2)}) async-start(), calls=%async_computation.31 | async-start | bytes 3244032 | tf_op jit(solution)/shard_map/reduce_scatter | solution.py:315
  848.7 592.5 %reduce-scatter.28.cloned.1.call-start = ((), (), s32[]{:S(2)}) async-start(), calls=%async_computation.30 | async-start | bytes 6488064 | tf_op jit(solution)/shard_map/reduce_scatter | solution.py:314
  859.2 743.1 %reduce-scatter.32.cloned.1.call-start = ((), (), s32[]{:S(2)}) async-start(), calls=%async_computation.32 | async-start | bytes 12976128 | tf_op jit(solution)/shard_map/reduce_scatter | solution.py:316
  870.6 774.9 %copy-start.17 = (f32[64,2,1536]{2,1,0:T(2,128)S(1)}, f32[64,2,1536]{2,1,0:T(2,128)}, u32[]{:S(2)}) copy-start(f32[64,2,1536]{2,1,0:T(2,128)} %param.41) | copy-start | bytes 2359300
  870.6 774.9 %copy-start.38 = (f32[64,2,1536]{2,1,0:T(2,128)S(1)}, f32[64,2,1536]{2,1,0:T(2,128)}, u32[]{:S(2)}) copy-start(f32[64,2,1536]{2,1,0:T(2,128)} %param.43) | copy-start | bytes 2359300
  870.6 775.0 %copy-start.39 = (f32[64,2,1536]{2,1,0:T(2,128)S(1)}, f32[64,2,1536]{2,1,0:T(2,128)}, u32[]{:S(2)}) copy-start(f32[64,2,1536]{2,1,0:T(2,128)} %param.42) | copy-start | bytes 2359300
  (85 other events, 632.4 us)
Sparse Core Ops, SparseCore 0:
  11.5 61.7 all-gather.11
  76.8 68.2 all-gather.15
  148.6 53.5 all-gather.13
  204.8 44.0 all-gather.19
  250.3 31.9 all-gather.17
  284.9 37.9 all-gather.21
  327.5 53.2 reduce-scatter.11
  383.9 61.9 all-gather.25
  447.5 31.6 all-gather.23
  482.2 45.4 all-gather.27
  536.2 53.0 reduce-scatter.13
  597.9 33.1 all-gather.29
  655.4 54.2 reduce-scatter.15
  716.9 33.1 all-gather.31
  780.1 54.2 reduce-scatter.25
  838.2 85.3 reduce-scatter.23
  927.7 60.6 reduce-scatter.19
  992.3 133.5 reduce-scatter.21
  1129.9 84.3 reduce-scatter.17
  1220.4 100.8 reduce-scatter.29
  1327.9 113.2 reduce-scatter.27
  1447.3 154.9 reduce-scatter.31
where the time goes:
time: 1680 us; the launch traced here: 1670 us
  waiting for transfers between devices  1360 us (81%)
  matrix products  143 us (9%)
  other arithmetic  62.7 us (4%)
  blocking collectives  40.2 us (2%)
  local copies, waits for them, and re-layouts  36.4 us (2%)
  between operations  23 us (1%)
    reduce_scatter x4, waiting for transfers between devices, pair_sum(): return lax.psum_scatter(value, 'tensor', scatter_dimension=0, tiled=True)  176 us
    reduce_scatter x1, waiting for transfers between devices, body(): lax.psum_scatter(mapping_grad, ('dp', 'tensor'), scatter_dimension=0, til...  158 us
    reduce_scatter x1, waiting for transfers between devices, body(): lax.psum_scatter(big_grads[2], 'dp', scatter_dimension=0, tiled=True)  136 us
    all_gather x4, waiting for transfers between devices, pair_rows(): return lax.all_gather(value, 'tensor', axis=0, tiled=True)  133 us
    reduce_scatter x1, waiting for transfers between devices, body(): lax.psum_scatter(patch_grads, ('dp', 'tensor'), scatter_dimension=1, tile...  118 us
    dot_general x23, matrix products, einsum_low(): return jnp.einsum(form, left, right, preferred_element_type=jnp.float32)  118 us
    reduce_scatter x1, waiting for transfers between devices, body(): lax.psum_scatter(table_grad, ('dp', 'tensor'), scatter_dimension=1, tiled...  103 us
    reduce_scatter x1, waiting for transfers between devices, body(): lax.psum_scatter(big_grads[0], 'dp', scatter_dimension=0, tiled=True)  86.4 us
  transfers between devices with their start and end apart: 22, of which 22 were waited for; matrix products, arithmetic and copies ran while one was open for 8% of the time, Pallas kernels for 0%

commit v1 on v0

v1 whole, which is shorter than its diff:
```python
import math

import jax
import jax.numpy as jnp
from jax import lax
from jax.sharding import PartitionSpec as P

D = 1024
HEAD_DIM = 64
CD = 768
CLASSES = 1001
PD = 768
FOUR = 256
SEQ = 256
GROUPS = 4
NLEVELS = 1000
LOW = jnp.bfloat16


HIGH = lax.Precision.HIGHEST
SIGMA_DATA = 0.5
LEARN_RATE = 0.05
DECAY = 0.1
BETA_ONE = 0.5
BETA_TWO = 0.5
ADAM_EPS = 1e-08
CLIP = 0.02
NORM_EPS = 1e-06


def to_low(value):
    return value.astype(LOW).astype(jnp.float32)


def rms_norm(value):
    return value * lax.rsqrt(jnp.mean(value * value, axis=-1, keepdims=True) + NORM_EPS)


def einsum_low(form, left, right):
    return jnp.einsum(form, left, right, preferred_element_type=jnp.float32)


def outer_sum(left, right):
    return jnp.dot(left.T, right, precision=HIGH)


def noise_terms(levels):
    log_sigma = -3.0 + 6.0 * levels.astype(jnp.float32) / (NLEVELS - 1)
    sigma = jnp.exp(log_sigma)
    radius = jnp.sqrt(sigma * sigma + SIGMA_DATA * SIGMA_DATA)
    half = FOUR // 2
    freqs = jnp.exp(-2.0 + 4.0 * jnp.arange(half, dtype=jnp.float32) / (half - 1))
    angles = 2.0 * math.pi * (log_sigma / 4.0)[:, None] * freqs[None, :]
    return (sigma, radius, jnp.concatenate([jnp.cos(angles), jnp.sin(angles)], axis=1))


def map_forward(feats, onehot, table, mats):
    feats_low = to_low(feats)
    cond_zero = jnp.dot(onehot, table, precision=HIGH) + jnp.dot(
        feats_low, mats[:, :FOUR].T, precision=HIGH
    )
    normed = to_low(rms_norm(cond_zero))
    inner = jnp.dot(normed, mats[:, FOUR : FOUR + CD], precision=HIGH)
    cond_low = to_low(cond_zero + jax.nn.gelu(inner))
    scales = 1.0 + jnp.dot(cond_low, mats[:, FOUR + CD :], precision=HIGH)
    return (scales, (feats_low, cond_zero, normed, inner, cond_low))


def map_backward(mats, kept, grad_scales):
    feats_low, cond_zero, normed, inner, cond_low = kept
    grad_cond = jnp.dot(grad_scales, mats[:, FOUR + CD :].T, precision=HIGH)
    _, pull_gelu = jax.vjp(jax.nn.gelu, inner)
    (grad_inner,) = pull_gelu(grad_cond)
    grad_normed = jnp.dot(grad_inner, mats[:, FOUR : FOUR + CD].T, precision=HIGH)
    _, pull_norm = jax.vjp(rms_norm, cond_zero)
    (grad_zero,) = pull_norm(grad_normed)
    return (grad_zero + grad_cond, grad_inner)


def scale_norm(hidden, scale):
    return rms_norm(hidden) * scale[:, None, :]


def norm_back(hidden, scale, grad):
    _, pull = jax.vjp(scale_norm, hidden, scale)
    return pull(grad)


class Links:
    def __init__(self, size):
        self.size = size
        self.bits = size.bit_length() - 1
        assert 1 << self.bits == size
        self.upper = list(range(self.bits - 1, 1, -1))

    def flip(self, value, bit):
        return lax.ppermute(value, "dp", [(i, i ^ (1 << bit)) for i in range(self.size)])

    def flip_pair(self, value):
        return lax.ppermute(value, "tensor", [(0, 1), (1, 0)])

    def grow(self, value, bit, axis=0):
        return jnp.concatenate([value, self.flip(value, bit)], axis=axis)

    def grow_pair(self, value, axis):
        return jnp.concatenate([value, self.flip_pair(value)], axis=axis)

    def gather_pair_last(self, value):
        for bit in self.upper + [1]:
            value = self.grow(value, bit)
        other = self.flip_pair(value)
        return (self.grow(value, 0), self.grow(other, 0))

    def gather_pair_first(self, value, axis):
        for bit in self.upper:
            value = self.grow(value, bit)
        value = self.grow_pair(value, axis)
        return self.grow(self.grow(value, 1), 0)

    def halve(self, value, bit):
        half = value.shape[0] // 2
        return value[:half] + self.flip(value[half:], bit)

    def halve_pair(self, value, axis):
        half = value.shape[axis] // 2
        own = lax.slice_in_dim(value, 0, half, axis=axis)
        other = lax.slice_in_dim(value, half, 2 * half, axis=axis)
        return own + self.flip_pair(other)

    def reduce(self, own, other, axis, pair_first):
        value = own + self.flip(other, 0)
        if pair_first:
            value = self.halve(self.halve_pair(value, axis), 1)
        else:
            value = self.halve_pair(self.halve(value, 1), axis)
        for bit in reversed(self.upper):
            value = self.halve(value, bit)
        return value

    def gather_rows(self, value):
        for bit in self.upper + [1]:
            value = self.grow(value, bit)
        return self.grow(self.grow_pair(value, 0), 0)

    def total(self, value):
        value = value + self.flip(value, 0)
        value = value + self.flip_pair(value)
        for bit in [1] + self.upper[::-1]:
            value = value + self.flip(value, bit)
        return value


def reverse_bits(value, bits):
    result = 0
    for bit in range(bits):
        result |= ((value >> bit) & 1) << (bits - 1 - bit)
    return result


def relative_order(size, bits, own):
    block = size >> bits
    order = jnp.array([reverse_bits(i, bits) for i in range(1 << bits)], jnp.int32)
    return ((order ^ own)[:, None] * block + jnp.arange(block)[None, :]).reshape(-1)


def order_matrix(size, order):
    return jnp.arange(size)[:, None] == order[None, :]


def split_heads(project):
    images, tokens = (project.shape[0], project.shape[1])
    return tuple(
        (project[:, :, :, part].reshape(images, tokens, -1, HEAD_DIM) for part in range(3))
    )


def attention_probs(queries, keys, totals):
    scores = einsum_low("iqhe,ikhe->ihqk", queries, keys) * (1.0 / math.sqrt(HEAD_DIM))
    return jnp.exp(scores - totals)


def body(
    clean_images,
    noise_draw,
    levels,
    labels,
    dropped,
    groups,
    step_count,
    inward,
    first_inward,
    second_inward,
    outward,
    first_outward,
    second_outward,
    expand,
    first_expand,
    second_expand,
    shrink,
    first_shrink,
    second_shrink,
    patches,
    first_patches,
    second_patches,
    classes,
    first_classes,
    second_classes,
    mapping,
    first_mapping,
    second_mapping,
):
    masters = (inward, outward, expand, shrink, patches, classes, mapping)
    firsts = (
        first_inward,
        first_outward,
        first_expand,
        first_shrink,
        first_patches,
        first_classes,
        first_mapping,
    )
    seconds = (
        second_inward,
        second_outward,
        second_expand,
        second_shrink,
        second_patches,
        second_classes,
        second_mapping,
    )
    links = Links(lax.axis_size("dp"))
    me, pair = lax.axis_index("dp"), lax.axis_index("tensor")
    images = clean_images.shape[0]
    rows = images * SEQ
    heads_width = inward.shape[2]
    ff_width = expand.shape[2]

    all_axes = ("dp", "tensor")
    table = lax.all_gather(classes.astype(LOW), all_axes, axis=1, tiled=True)
    map_mats = lax.all_gather(mapping.astype(LOW), all_axes, axis=0, tiled=True)
    patch_rows = patches.shape[1]
    patch_flat = jnp.concatenate([patches[0], patches[1]], axis=1).astype(LOW)
    patch_all = links.gather_pair_first(patch_flat, 0)
    attn_in = links.gather_pair_first(inward.reshape(inward.shape[0], -1).astype(LOW), 1)
    attn_out = links.gather_pair_last(outward.T.astype(LOW))
    gate_up = links.gather_pair_last(expand.reshape(expand.shape[0], -1).astype(LOW))
    down = links.gather_pair_first(shrink.T.astype(LOW), 1)

    order_d = relative_order(D, links.bits, me)
    to_own = order_matrix(D, order_d).astype(LOW)
    n_up = len(links.upper)
    pos = []
    for i in range(1 << (links.bits + 1)):
        place, bit = 0, 0
        for step in links.upper:
            place |= ((i >> bit) & 1) << (step + 1)
            bit += 1
        place |= ((i >> bit) & 1) << 0
        place |= ((i >> (bit + 1)) & 1) << 2
        place |= ((i >> (bit + 2)) & 1) << 1
        pos.append(place)
    own_place = me * 2 + pair
    order_p = (
        (jnp.array(pos, jnp.int32) ^ own_place)[:, None] * patch_rows + jnp.arange(patch_rows)[None, :]
    ).reshape(-1)
    to_own_p = order_matrix(PD, order_p).astype(LOW)

    def pick_p(value):
        return jnp.dot(
            value.reshape(rows, PD), to_own_p, preferred_element_type=jnp.float32
        ).reshape(value.shape)

    sigma, radius, feats = noise_terms(levels)
    chosen = jnp.where(dropped == 1, CLASSES - 1, labels)
    onehot = (chosen[:, None] == jnp.arange(CLASSES)[None, :]).astype(jnp.float32)
    map_mats = map_mats.astype(jnp.float32)
    scale_flat, map_kept = map_forward(feats, onehot, table.astype(jnp.float32), map_mats)
    feats_low, cond_zero, normed, inner, cond_low = map_kept
    scales = jnp.dot(
        scale_flat.reshape(images * 3, D), to_own.astype(jnp.float32), precision=HIGH
    ).reshape(images, 3, D)

    sig = sigma[:, None, None]
    rad = radius[:, None, None]
    clean_float = pick_p(clean_images)
    noise_float = pick_p(noise_draw)
    inputs = ((clean_float + sig * noise_float) / rad).astype(LOW)
    target = (sig * clean_float - SIGMA_DATA * SIGMA_DATA * noise_float) / (SIGMA_DATA * rad)

    patch_in = jnp.dot(patch_all[:, :D], to_own, preferred_element_type=jnp.float32).astype(LOW)
    patch_out = jnp.dot(patch_all[:, D:], to_own, preferred_element_type=jnp.float32).astype(LOW)

    resid_zero = einsum_low("isp,pd->isd", inputs, patch_in)
    rows_zero = scale_norm(resid_zero, scales[:, 0]).astype(LOW)
    project = einsum_low("isd,dn->isn", rows_zero, attn_in).astype(LOW)
    project = project.reshape(images, SEQ, 2, 3, heads_width)
    queries, keys, values = split_heads(project)
    scores = einsum_low("iqhe,ikhe->ihqk", queries, keys) * (1.0 / math.sqrt(HEAD_DIM))
    totals = jax.nn.logsumexp(scores, axis=-1, keepdims=True)
    probs = jnp.exp(scores - totals).astype(LOW)
    mixed = einsum_low("ihqk,ikhe->iqhe", probs, values).astype(LOW)
    mixed = mixed.reshape(images, SEQ, -1)
    halves = (mixed[:, :, :heads_width], mixed[:, :, heads_width:])
    resid_one = (
        resid_zero
        + einsum_low("ish,dh->isd", halves[0], attn_out[0])
        + einsum_low("ish,dh->isd", halves[1], attn_out[1])
    )
    rows_one = scale_norm(resid_one, scales[:, 1]).astype(LOW)
    gates, uppers, hiddens = [], [], []
    for part in range(2):
        gates.append(einsum_low("isd,df->isf", rows_one, gate_up[part][:, :ff_width]))
        uppers.append(einsum_low("isd,df->isf", rows_one, gate_up[part][:, ff_width:]))
        hiddens.append((jax.nn.gelu(gates[part]) * uppers[part]).astype(LOW))
    hidden = jnp.concatenate(hiddens, axis=2)
    resid_two = resid_one + einsum_low("isf,df->isd", hidden, down)
    last = scale_norm(resid_two, scales[:, 2]).astype(LOW)
    output = einsum_low("isd,pd->isp", last, patch_out)

    counts = jnp.sum((groups[:, None] == groups[None, :]).astype(jnp.float32), axis=1)
    weight = 1.0 / (GROUPS * counts)
    diff = output - target
    local_loss = jnp.sum(weight * jnp.mean(diff**2, axis=(1, 2)))
    grad_low = (2.0 * diff * (weight / (SEQ * PD))[:, None, None]).astype(LOW)

    half = D // 2

    def weight_grad(form, left, right):
        return einsum_low(form, left, right).astype(LOW)

    grad_last = einsum_low("isp,pd->isd", grad_low, patch_out)
    last_canon = einsum_low("isd,cd->isc", last, to_own).astype(LOW)
    half_p = PD // 2
    out_own = weight_grad("isp,isd->pd", grad_low[:, :, :half_p], last_canon)
    out_other = weight_grad("isp,isd->pd", grad_low[:, :, half_p:], last_canon)
    grad_two, scale_two = norm_back(resid_two, scales[:, 2], grad_last)
    rows_grad = grad_two.astype(LOW)
    grad_hidden = einsum_low("isd,df->isf", rows_grad, down)
    down_own = weight_grad("isd,isf->df", rows_grad[:, :, :half], hidden)
    down_other = weight_grad("isd,isf->df", rows_grad[:, :, half:], hidden)
    shard_down = links.reduce(down_own, down_other, 1, False)

    part_one = 0.0
    gated_grads = []
    for part in range(2):
        _, pull_gate = jax.vjp(
            lambda gate, upper: jax.nn.gelu(gate) * upper, gates[part], uppers[part]
        )
        grad_gate, grad_up = pull_gate(
            grad_hidden[:, :, part * ff_width : (part + 1) * ff_width]
        )
        gated_grads.append(jnp.concatenate([grad_gate, grad_up], axis=2).astype(LOW))
        part_one = part_one + einsum_low("isf,df->isd", gated_grads[part], gate_up[part])
    gated_grad = jnp.concatenate(gated_grads, axis=2)
    up_own = weight_grad("isd,isf->df", rows_one[:, :, :half], gated_grad)
    up_other = weight_grad("isd,isf->df", rows_one[:, :, half:], gated_grad)
    shard_up = links.reduce(up_own, up_other, 1, True)

    part_one, scale_one = norm_back(resid_one, scales[:, 1], part_one)
    grad_one = grad_two + part_one
    rows_grad = grad_one.astype(LOW)
    grad_mixed = jnp.concatenate(
        [
            einsum_low("isd,dh->ish", rows_grad, attn_out[0]),
            einsum_low("isd,dh->ish", rows_grad, attn_out[1]),
        ],
        axis=2,
    ).astype(LOW)
    attn_own = weight_grad("isd,ish->dh", rows_grad[:, :, :half], mixed)
    attn_other = weight_grad("isd,ish->dh", rows_grad[:, :, half:], mixed)
    shard_out = links.reduce(attn_own, attn_other, 1, True)
    grad_mixed = grad_mixed.reshape(queries.shape)

    probs = attention_probs(queries, keys, totals)
    grad_values = einsum_low("ihqk,iqhe->ikhe", probs.astype(LOW), grad_mixed)
    grad_probs = einsum_low("iqhe,ikhe->ihqk", grad_mixed, values)
    grad_scores = (
        probs * (grad_probs - jnp.sum(grad_probs * probs, axis=-1, keepdims=True))
    ).astype(LOW)
    inverse_root = 1.0 / math.sqrt(HEAD_DIM)
    grad_queries = einsum_low("ihqk,ikhe->iqhe", grad_scores, keys) * inverse_root
    grad_keys = einsum_low("ihqk,iqhe->ikhe", grad_scores, queries) * inverse_root
    grad_project = jnp.stack(
        [
            part.reshape(images, SEQ, 2, heads_width).astype(LOW)
            for part in (grad_queries, grad_keys, grad_values)
        ],
        axis=3,
    ).reshape(images, SEQ, -1)
    in_own = weight_grad("isd,isn->dn", rows_zero[:, :, :half], grad_project)
    in_other = weight_grad("isd,isn->dn", rows_zero[:, :, half:], grad_project)
    shard_in = links.reduce(in_own, in_other, 1, False)

    part_zero, scale_zero = norm_back(
        resid_zero, scales[:, 0], einsum_low("isn,dn->isd", grad_project, attn_in)
    )
    grad_zero = (grad_one + part_zero).astype(LOW)
    zero_canon = einsum_low("isd,cd->isc", grad_zero, to_own).astype(LOW)
    patch_own = jnp.concatenate(
        [weight_grad("isp,isd->pd", inputs[:, :, :half_p], zero_canon), out_own], axis=1
    )
    patch_other = jnp.concatenate(
        [weight_grad("isp,isd->pd", inputs[:, :, half_p:], zero_canon), out_other], axis=1
    )
    shard_patch = links.reduce(patch_own, patch_other, 0, False)

    grad_scales = jnp.stack([scale_zero, scale_one, scale_two], axis=1)
    grad_scales = jnp.dot(
        grad_scales.reshape(images * 3, D), to_own.astype(jnp.float32).T, precision=HIGH
    ).reshape(images, 3 * D)
    map_grad_zero, map_grad_inner = map_backward(map_mats, map_kept, grad_scales)
    kept_rows = jnp.concatenate([feats_low, normed, cond_low], axis=1).astype(LOW)
    kept_rows = links.gather_rows(kept_rows).astype(jnp.float32)
    chosen_rows = links.gather_rows(jnp.broadcast_to(chosen[:, None], (images, 128)))[:, :1]
    grad_rows = links.gather_rows(
        jnp.concatenate([grad_scales, map_grad_inner, map_grad_zero], axis=1)
    )
    own = own_place * mapping.shape[0]

    def own_columns(value):
        return lax.dynamic_slice_in_dim(value, own, mapping.shape[0], axis=1)

    zero_own = own_columns(grad_rows[:, 3 * D + CD :])
    onehot_rows = (chosen_rows == jnp.arange(CLASSES)[None, :]).astype(jnp.float32)
    table_grad = outer_sum(onehot_rows, zero_own)
    mapping_grad = jnp.concatenate(
        [
            outer_sum(zero_own, kept_rows[:, :FOUR]),
            outer_sum(own_columns(kept_rows[:, FOUR : FOUR + CD]), grad_rows[:, 3 * D : 3 * D + CD]),
            outer_sum(own_columns(kept_rows[:, FOUR + CD :]), grad_rows[:, : 3 * D]),
        ],
        axis=1,
    )

    shard_patch = shard_patch.astype(jnp.float32)
    grads = (
        shard_in.astype(jnp.float32).reshape(inward.shape),
        shard_out.astype(jnp.float32).T,
        shard_up.astype(jnp.float32).reshape(expand.shape),
        shard_down.astype(jnp.float32).T,
        jnp.stack([shard_patch[:, :D], shard_patch[:, D:]]),
        table_grad,
        mapping_grad,
    )
    squares = sum((jnp.sum(grad * grad) for grad in grads))
    sums = links.total(jnp.stack([local_loss, squares]))
    total_loss = sums[0]
    grad_norm = jnp.sqrt(sums[1])
    factor = CLIP / (grad_norm + NORM_EPS)
    count = step_count[0].astype(jnp.float32)
    fix_one = 1.0 - jnp.power(BETA_ONE, count)
    fix_two = 1.0 - jnp.power(BETA_TWO, count)
    results = [total_loss, grad_norm]
    for master, first, second, grad in zip(masters, firsts, seconds, grads):
        clipped = grad * factor
        moment = BETA_ONE * first + (1.0 - BETA_ONE) * clipped
        square = BETA_TWO * second + (1.0 - BETA_TWO) * clipped * clipped
        step_size = moment / fix_one / (jnp.sqrt(square / fix_two) + ADAM_EPS)
        results.extend([master - LEARN_RATE * (step_size + DECAY * master), moment, square])
    return tuple(results)


def solution(mesh):
    in_specs = (
        P(("dp", "tensor"), None, None),
        P(("dp", "tensor"), None, None),
        P(("dp", "tensor")),
        P(("dp", "tensor")),
        P(("dp", "tensor")),
        P(("dp", "tensor")),
        P(),
        P("dp", None, "tensor"),
        P("dp", None, "tensor"),
        P("dp", None, "tensor"),
        P("tensor", "dp"),
        P("tensor", "dp"),
        P("tensor", "dp"),
        P("dp", None, "tensor"),
        P("dp", None, "tensor"),
        P("dp", None, "tensor"),
        P("tensor", "dp"),
        P("tensor", "dp"),
        P("tensor", "dp"),
        P(None, ("dp", "tensor"), None),
        P(None, ("dp", "tensor"), None),
        P(None, ("dp", "tensor"), None),
        P(None, ("dp", "tensor")),
        P(None, ("dp", "tensor")),
        P(None, ("dp", "tensor")),
        P(("dp", "tensor"), None),
        P(("dp", "tensor"), None),
        P(("dp", "tensor"), None),
    )
    out_specs = (
        P(),
        P(),
        P("dp", None, "tensor"),
        P("dp", None, "tensor"),
        P("dp", None, "tensor"),
        P("tensor", "dp"),
        P("tensor", "dp"),
        P("tensor", "dp"),
        P("dp", None, "tensor"),
        P("dp", None, "tensor"),
        P("dp", None, "tensor"),
        P("tensor", "dp"),
        P("tensor", "dp"),
        P("tensor", "dp"),
        P(None, ("dp", "tensor"), None),
        P(None, ("dp", "tensor"), None),
        P(None, ("dp", "tensor"), None),
        P(None, ("dp", "tensor")),
        P(None, ("dp", "tensor")),
        P(None, ("dp", "tensor")),
        P(("dp", "tensor"), None),
        P(("dp", "tensor"), None),
        P(("dp", "tensor"), None),
    )
    return jax.shard_map(body, mesh=mesh, in_specs=in_specs, out_specs=out_specs, check_vma=False)
```

time: 1680 us -> 792 us (0.47)
  waiting for transfers between devices: 1360 us -> 384 us
  starting transfers between devices: 2.17 us -> 67.7 us
  blocking collectives: 40.2 us -> 0 us
  matrix products: 143 us -> 174 us
  local copies, waits for them, and re-layouts: 36.4 us -> 66.7 us
    reduce_scatter x11 -> x0, waiting for transfers between devices: 892 us -> none  [the longest x4 176 us: pair_sum(): return lax.psum_scatter(value, 'tensor', scatter_dimension=0, tiled=True)]
    all_gather x11 -> x2, waiting for transfers between devices: 466 us -> 0.01 us  [the longest x1 0.01 us: body(): map_mats = lax.all_gather(mapping.astype(LOW), all_axes, axis=0, tiled=True)]
    ppermute x0 -> x72, waiting for transfers between devices: none -> 384 us  [the longest x58 224 us: flip(): lax.ppermute(value, 'dp', [(i, i ^ 1 << bit) for i in range(self.size)])]
    ppermute x0 -> x72, starting transfers between devices: none -> 67.7 us  [the longest x58 50.1 us: flip(): lax.ppermute(value, 'dp', [(i, i ^ 1 << bit) for i in range(self.size)])]
    psum x1 -> x0, blocking collectives: 40.2 us -> none  [body(): total_loss = lax.psum(local_loss, ('dp', 'tensor'))]
    concatenate x0 -> x13, local copies, waits for them, and re-layouts: none -> 29.4 us  [the longest x10 22.9 us: grow(): return jnp.concatenate([value, self.flip(value, bit)], axis=axis)]
    dot_general x23 -> x37, matrix products: 118 us -> 142 us  [einsum_low(): return jnp.einsum(form, left, right, preferred_element_type=jnp.float32)]
  transfers between devices with their start and end apart: 22 -> 74, of which waited for: 22 -> 34; matrix products, arithmetic and copies ran while one was open for 8% -> 25% of each run, Pallas kernels for 0% -> 0%
where the time goes in v1:
time: 792 us; the launch traced here: 785 us
  waiting for transfers between devices  384 us (48%)
  matrix products  174 us (22%)
  other arithmetic  68.7 us (9%)
  starting transfers between devices  67.7 us (9%)
  local copies, waits for them, and re-layouts  66.7 us (8%)
  between operations  23.6 us (3%)
    ppermute x58, waiting for transfers between devices, flip(): lax.ppermute(value, 'dp', [(i, i ^ 1 << bit) for i in range(self.size)])  224 us
    ppermute x14, waiting for transfers between devices, flip_pair(): return lax.ppermute(value, 'tensor', [(0, 1), (1, 0)])  160 us
    dot_general x37, matrix products, einsum_low(): return jnp.einsum(form, left, right, preferred_element_type=jnp.float32)  142 us
    ppermute x58, starting transfers between devices, flip(): lax.ppermute(value, 'dp', [(i, i ^ 1 << bit) for i in range(self.size)])  50.1 us
    unnamed x282, local copies, waits for them, and re-layouts  23.5 us
    concatenate x10, local copies, waits for them, and re-layouts, grow(): return jnp.concatenate([value, self.flip(value, bit)], axis=axis)  22.9 us
    ppermute x14, starting transfers between devices, flip_pair(): return lax.ppermute(value, 'tensor', [(0, 1), (1, 0)])  17.5 us
  transfers between devices with their start and end apart: 74, of which 34 were waited for; matrix products, arithmetic and copies ran while one was open for 25% of the time, Pallas kernels for 0%

profile of v1, /device:TPU:0, one launch (start us, length us, event | category | flops | bytes accessed | tf_op | source)
XLA Modules:
  0.0 784.6 jit_solution(15581906526241912492)
XLA Ops:
  31.2 22.4 %collective-permute-done.52 = s32[2,128]{1,0:T(2,128)S(1)} collective-permute-done((s32[2,128]{1,0:T(2,128)S(1)}, s32[2,128]{1,0:T(2,128)S(1)}, u32[]{:S(2)}, u32[]{:S(2)}) %collective-permute-start.52) | collective-permute-done | bytes 1056 | tf_op jit(solution)/shard_map/ppermute | solution.py:97
  73.2 35.3 %collective-permute-done.11 = bf16[128,512]{1,0:T(8,128)(2,1)S(1)} collective-permute-done((bf16[128,512]{1,0:T(8,128)(2,1)S(1)}, bf16[128,512]{1,0:T(8,128)(2,1)S(1)}, u32[]{:S(2)}, u32[]{:S(2)}) %collective-permute-start.11) | collective-permute-done | bytes 131104 | tf_op jit(solution)/shard_map/ppermute | solution.py:97
  119.8 31.0 %collective-permute-done.18 = bf16[256,3072]{1,0:T(8,128)(2,1)S(1)} collective-permute-done((bf16[256,3072]{1,0:T(8,128)(2,1)S(1)}, bf16[256,3072]{1,0:T(8,128)(2,1)S(1)}, u32[]{:S(2)}, u32[]{:S(2)}) %collective-permute-start.18) | collective-permute-done | bytes 1572896 | tf_op jit(solution)/shard_map/ppermute | solution.py:97
  160.8 83.1 %collective-permute-done.7 = bf16[256,1536]{1,0:T(8,128)(2,1)S(1)} collective-permute-done((bf16[256,1536]{1,0:T(8,128)(2,1)S(1)}, bf16[256,1536]{1,0:T(8,128)(2,1)S(1)}, u32[]{:S(2)}, u32[]{:S(2)}) %collective-permute-start.7) | collective-permute-done | bytes 786464 | tf_op jit(solution)/shard_map/ppermute | solution.py:100
  247.8 9.9 %collective-permute-done.24 = bf16[256,1536]{1,0:T(8,128)(2,1)S(1)} collective-permute-done((bf16[256,1536]{1,0:T(8,128)(2,1)S(1)}, bf16[256,1536]{1,0:T(8,128)(2,1)S(1)}, u32[]{:S(2)}, u32[]{:S(2)}) %collective-permute-start.24) | collective-permute-done | bytes 786464 | tf_op jit(solution)/shard_map/ppermute | solution.py:100
  285.0 19.4 %collective-permute-done.25 = bf16[256,3072]{1,0:T(8,128)(2,1)} collective-permute-done((bf16[256,3072]{1,0:T(8,128)(2,1)}, bf16[256,3072]{1,0:T(8,128)(2,1)}, u32[]{:S(2)}, u32[]{:S(2)}) %collective-permute-start.25) | collective-permute-done | bytes 1572896 | tf_op jit(solution)/shard_map/ppermute | solution.py:97
  304.4 6.1 pad_maximum_fusion.3
  318.3 5.2 fusion.62
  346.3 11.3 %convolution_convert_fusion = bf16[2,256,3072]{2,1,0:T(8,128)(2,1)} fusion(bf16[2,256,1024]{2,1,0:T(8,128)(2,1)S(1)} %multiply_convert_fusion.9, bf16[512,3072]{1,0:T(8,128)(2,1)} %collective-permute-done.9, bf16[256,3072]{1,0:T(8,128)(2,1)} %collective-permute-done.8, bf16[256,1536]{1,0:T(8,128)(2,1)S(1)} %copy-done.19, bf16[256,1536]{1,0:T(8,128)(2,1)S(1)} %copy-done.13), kind=kOutput, calls=%fused_computation.24 | convolution fusion | flops 3247964160 | bytes 10485760 | tf_op jit(solution)/shard_map/isd,dn->isn/dot_general | solution.py:40
  357.6 4.9 copy.231
  381.4 5.3 multiply_convert_fusion.3
  390.9 6.8 multiply_reduce_fusion.8
  405.4 8.5 %fusion.87 = f32[2,256,3072]{2,1,0:T(8,128)S(1)} fusion(bf16[2,256,1024]{2,1,0:T(8,128)(2,1)S(1)} %fusion.120, bf16[512,3072]{1,0:T(8,128)(2,1)} %collective-permute-done.26, bf16[256,3072]{1,0:T(8,128)(2,1)} %collective-permute-done.25, bf16[256,1536]{1,0:T(8,128)(2,1)S(1)} %copy-done.23, bf16[128,1536]{1,0:T(8,128)(2,1)S(1)} %collective-permute-done.23, ...), kind=kOutput, calls=%fused_computation.150 | convolution fusion | flops 3258974208 | bytes 13631488 | tf_op jit(solution)/shard_map/isd,df->isf/dot_general | solution.py:40
  414.0 5.9 fusion.38
  419.9 6.9 fusion.3
  426.9 6.6 multiply_reduce_fusion.3
  440.7 5.1 convolution_convert_fusion.1
  457.7 8.4 %bitcast_convert_fusion = bf16[512,6144]{1,0:T(8,128)(2,1)} fusion(bf16[2,256,1536]{2,1,0:T(8,128)(2,1)S(1)} %copy-done.31, bf16[2,256,1536]{2,1,0:T(8,128)(2,1)S(1)} %copy-done.28, bf16[2,256,1536]{2,1,0:T(8,128)(2,1)S(1)} %copy-done.34, bf16[2,256,1536]{2,1,0:T(8,128)(2,1)S(1)} %copy-done.37, bf16[2,256,1024]{2,1,0:T(8,128)(2,1)} %copy-done.59), kind=kOutput, calls=%fused_computation | convolution fusion | flops 3249537024 | bytes 13107200 | tf_op jit(solution)/shard_map/isd,isf->df/dot_general | solution.py:40
  466.2 5.1 bitcast_convert_fusion.2
  479.4 10.6 %multiply_reduce_fusion.4 = (f32[2,1024]{1,0:T(2,128)S(1)}, f32[2,256]{1,0:T(2,128)S(1)}, f32[2,256,1024]{2,1,0:T(8,128)S(1)}) fusion(f32[2,256,1024]{2,1,0:T(8,128)S(1)} %copy-done.7, f32[2,256]{1,0:T(2,128)S(1)} %fusion.159, f32[2,1024]{1,0:T(2,128)S(1)} %bitcast.278, bf16[2,256,3072]{1,2,0:T(8,128)(2,1)S(1)} %bitcast.260, ...), kind=kOutput, calls=%fused_computation.93 | convolution fusion | flops 3249534464 | bytes 13651968 | tf_op jit(solution)/shard_map/isn,dn->isd/dot_general | solution.py:40
  495.9 6.2 fusion.156
  543.3 7.4 collective-permute-done.33
  568.6 7.8 collective-permute-done.48
  577.5 8.2 %fusion = bf16[512,6144]{1,0:T(8,128)(2,1)S(1)} fusion(bf16[512,6144]{1,0:T(8,128)(2,1)} %collective-permute-done.37, bf16[2,256,1536]{2,1,0:T(8,128)(2,1)S(1)} %copy-done.32, bf16[2,256,1536]{2,1,0:T(8,128)(2,1)S(1)} %copy-done.29, bf16[2,256,1536]{2,1,0:T(8,128)(2,1)S(1)} %copy-done.35, bf16[2,256,1536]{2,1,0:T(8,128)(2,1)} %copy-done.36, ...), kind=kOutput, calls=%fused_computation.6 | convolution fusion | flops 3252682752 | bytes 19398656 | tf_op jit(solution)/shard_map/isd,isf->df/dot_general | solution.py:40
  605.0 24.2 %collective-permute-done.28 = bf16[256,3072]{1,0:T(8,128)(2,1)S(1)} collective-permute-done((bf16[256,3072]{1,0:T(8,128)(2,1)S(1)}, bf16[256,3072]{1,0:T(8,128)(2,1)S(1)}, u32[]{:S(2)}, u32[]{:S(2)}) %collective-permute-start.28) | collective-permute-done | bytes 1572896 | tf_op jit(solution)/shard_map/ppermute | solution.py:97
  630.7 26.4 %collective-permute-done.38 = bf16[512,3072]{1,0:T(8,128)(2,1)S(1)} collective-permute-done((bf16[512,3072]{1,0:T(8,128)(2,1)S(1)}, bf16[512,3072]{1,0:T(8,128)(2,1)S(1)}, u32[]{:S(2)}, u32[]{:S(2)}) %collective-permute-start.38) | collective-permute-done | bytes 3145760 | tf_op jit(solution)/shard_map/ppermute | solution.py:100
  664.4 9.5 %collective-permute-done.29 = bf16[256,1536]{1,0:T(8,128)(2,1)S(1)} collective-permute-done((bf16[256,1536]{1,0:T(8,128)(2,1)S(1)}, bf16[256,1536]{1,0:T(8,128)(2,1)S(1)}, u32[]{:S(2)}, u32[]{:S(2)}) %collective-permute-start.29) | collective-permute-done | bytes 786464 | tf_op jit(solution)/shard_map/ppermute | solution.py:100
  674.4 13.4 %collective-permute-done.44 = bf16[256,1536]{1,0:T(8,128)(2,1)S(1)} collective-permute-done((bf16[256,1536]{1,0:T(8,128)(2,1)S(1)}, bf16[256,1536]{1,0:T(8,128)(2,1)S(1)}, u32[]{:S(2)}, u32[]{:S(2)}) %collective-permute-start.44) | collective-permute-done | bytes 786464 | tf_op jit(solution)/shard_map/ppermute | solution.py:100
  688.3 5.4 collective-permute-done.39
  696.5 8.4 %collective-permute-done.45 = bf16[128,1536]{1,0:T(8,128)(2,1)S(1)} collective-permute-done((bf16[128,1536]{1,0:T(8,128)(2,1)S(1)}, bf16[128,1536]{1,0:T(8,128)(2,1)S(1)}, u32[]{:S(2)}, u32[]{:S(2)}) %collective-permute-start.45) | collective-permute-done | bytes 393248 | tf_op jit(solution)/shard_map/ppermute | solution.py:97
  705.1 16.4 %collective-permute-done.40 = bf16[128,3072]{1,0:T(8,128)(2,1)S(1)} collective-permute-done((bf16[128,3072]{1,0:T(8,128)(2,1)S(1)}, bf16[128,3072]{1,0:T(8,128)(2,1)S(1)}, u32[]{:S(2)}, u32[]{:S(2)}) %collective-permute-start.40) | collective-permute-done | bytes 786464 | tf_op jit(solution)/shard_map/ppermute | solution.py:97
  725.8 13.2 %collective-permute-done.41 = bf16[64,3072]{1,0:T(8,128)(2,1)S(1)} collective-permute-done((bf16[64,3072]{1,0:T(8,128)(2,1)S(1)}, bf16[64,3072]{1,0:T(8,128)(2,1)S(1)}, u32[]{:S(2)}, u32[]{:S(2)}) %collective-permute-start.41) | collective-permute-done | bytes 393248 | tf_op jit(solution)/shard_map/ppermute | solution.py:97
  (616 shorter events, 316.4 us)
Async XLA Ops:
  7.3 327.7 %all-gather.5.cloned.1.call-start = ((), (), s32[]{:S(2)}) async-start(), calls=%async_computation.1 | async-start | bytes 6488064 | tf_op jit(solution)/shard_map/all_gather | solution.py:240
  9.1 327.0 %all-gather.3.cloned.1.call-start = ((), (), s32[]{:S(2)}) async-start(), calls=%async_computation | async-start | bytes 1622016 | tf_op jit(solution)/shard_map/all_gather | solution.py:239
  10.8 58.6 %collective-permute-start.10 = (bf16[64,512]{1,0:T(8,128)(2,1)}, bf16[64,512]{1,0:T(8,128)(2,1)}, u32[]{:S(2)}, u32[]{:S(2)}) collective-permute-start(bf16[64,512]{1,0:T(8,128)(2,1)} %get-tuple-element.149), channel_id=1, source_target_pairs={{0,16},{2,18},{4,20},{6,22},{8,24},{10,26},{12,28},{14,30},{16,0},... | collective-permute-start | bytes 196616 | tf_op jit(solution)/shard_map/ppermute | solution.py:97
  16.5 54.7 %collective-permute-start = (bf16[24,2048]{1,0:T(8,128)(2,1)}, bf16[24,2048]{1,0:T(8,128)(2,1)S(1)}, u32[]{:S(2)}, u32[]{:S(2)}) collective-permute-start(bf16[24,2048]{1,0:T(8,128)(2,1)} %get-tuple-element.181), channel_id=1, source_target_pairs={{0,16},{2,18},{4,20},{6,22},{8,24},{10,26},{12,28},{14,30},{16,0},... | collective-permute-start | bytes 294920 | tf_op jit(solution)/shard_map/ppermute | solution.py:97
  17.5 94.2 %collective-permute-start.5 = (bf16[64,1536]{1,0:T(8,128)(2,1)S(1)}, bf16[64,1536]{1,0:T(8,128)(2,1)}, u32[]{:S(2)}, u32[]{:S(2)}) collective-permute-start(bf16[64,1536]{1,0:T(8,128)(2,1)S(1)} %bitcast.262), channel_id=1, source_target_pairs={{0,16},{2,18},{4,20},{6,22},{8,24},{10,26},{12,28},{14,30},{16,0},... | collective-permute-start | bytes 589832 | tf_op jit(solution)/shard_map/ppermute | solution.py:97
  20.8 41.7 %collective-permute-start.16 = (bf16[64,3072]{1,0:T(8,128)(2,1)S(1)}, bf16[64,3072]{1,0:T(8,128)(2,1)S(1)}, u32[]{:S(2)}, u32[]{:S(2)}) collective-permute-start(bf16[64,3072]{1,0:T(8,128)(2,1)S(1)} %bitcast.244), channel_id=1, source_target_pairs={{0,16},{2,18},{4,20},{6,22},{8,24},{10,26},{12,28},{14,30},{16,0},... | collective-permute-start | bytes 1179656 | tf_op jit(solution)/shard_map/ppermute | solution.py:97
  63.5 47.5 %collective-permute-start.17 = (bf16[128,3072]{1,0:T(8,128)(2,1)}, bf16[128,3072]{1,0:T(8,128)(2,1)S(1)}, u32[]{:S(2)}, u32[]{:S(2)}) collective-permute-start(bf16[128,3072]{1,0:T(8,128)(2,1)} %pad_maximum_fusion.16), channel_id=1, source_target_pairs={{0,8},{2,10},{4,12},{6,14},{8,0},{10,2},{12,4},{14,6},{16,24},{18,... | collective-permute-start | bytes 2359304 | tf_op jit(solution)/shard_map/ppermute | solution.py:97
  64.7 48.0 %collective-permute-start.22 = (bf16[64,1536]{1,0:T(8,128)(2,1)S(1)}, bf16[64,1536]{1,0:T(8,128)(2,1)S(1)}, u32[]{:S(2)}, u32[]{:S(2)}) collective-permute-start(bf16[64,1536]{1,0:T(8,128)(2,1)S(1)} %convert_bitcast_fusion), channel_id=1, source_target_pairs={{0,16},{2,18},{4,20},{6,22},{8,24},{10,26},{12,28},{14,30},{16,0},... | collective-permute-start | bytes 589832 | tf_op jit(solution)/shard_map/ppermute | solution.py:97
  71.2 44.6 %collective-permute-start.1 = (bf16[48,2048]{1,0:T(8,128)(2,1)S(1)}, bf16[48,2048]{1,0:T(8,128)(2,1)S(1)}, u32[]{:S(2)}, u32[]{:S(2)}) collective-permute-start(bf16[48,2048]{1,0:T(8,128)(2,1)S(1)} %pad_maximum_fusion.27), channel_id=1, source_target_pairs={{0,8},{2,10},{4,12},{6,14},{8,0},{10,2},{12,4},{14,6},{16,24},{18,... | collective-permute-start | bytes 589832 | tf_op jit(solution)/shard_map/ppermute | solution.py:97
  109.4 46.5 %collective-permute-start.12 = (bf16[256,512]{1,0:T(8,128)(2,1)S(1)}, bf16[256,512]{1,0:T(8,128)(2,1)S(1)}, u32[]{:S(2)}, u32[]{:S(2)}) collective-permute-start(bf16[256,512]{1,0:T(8,128)(2,1)S(1)} %pad_maximum_fusion.26), channel_id=1, source_target_pairs={{0,4},{2,6},{4,0},{6,2},{8,12},{10,14},{12,8},{14,10},{16,20},{18,... | collective-permute-start | bytes 786440 | tf_op jit(solution)/shard_map/ppermute | solution.py:97
  112.8 44.9 %collective-permute-start.23 = (bf16[128,1536]{1,0:T(8,128)(2,1)S(1)}, bf16[128,1536]{1,0:T(8,128)(2,1)S(1)}, u32[]{:S(2)}, u32[]{:S(2)}) collective-permute-start(bf16[128,1536]{1,0:T(8,128)(2,1)S(1)} %pad_maximum_fusion.23), channel_id=1, source_target_pairs={{0,8},{2,10},{4,12},{6,14},{8,0},{10,2},{12,4},{14,6},{16,24},{18,... | collective-permute-start | bytes 1179656 | tf_op jit(solution)/shard_map/ppermute | solution.py:97
  115.8 43.4 %collective-permute-start.2 = (bf16[96,2048]{1,0:T(8,128)(2,1)S(1)}, bf16[96,2048]{1,0:T(8,128)(2,1)S(1)}, u32[]{:S(2)}, u32[]{:S(2)}) collective-permute-start(bf16[96,2048]{1,0:T(8,128)(2,1)S(1)} %pad_maximum_fusion.21), channel_id=1, source_target_pairs={{0,1},{1,0},{2,3},{3,2},{4,5},{5,4},{6,7},{7,6},{8,9},{9,8},{10,11... | collective-permute-start | bytes 1179656 | tf_op jit(solution)/shard_map/ppermute | solution.py:100
  153.0 126.3 %collective-permute-start.20 = (bf16[512,3072]{1,0:T(8,128)(2,1)}, bf16[512,3072]{1,0:T(8,128)(2,1)}, u32[]{:S(2)}, u32[]{:S(2)}) collective-permute-start(bf16[512,3072]{1,0:T(8,128)(2,1)} %get-tuple-element.159), channel_id=1, source_target_pairs={{0,1},{1,0},{2,3},{3,2},{4,5},{5,4},{6,7},{7,6},{8,9},{9,8},{10,11... | collective-permute-start | bytes 9437192 | tf_op jit(solution)/shard_map/ppermute | solution.py:100
  154.4 89.5 %collective-permute-start.7 = (bf16[256,1536]{1,0:T(8,128)(2,1)S(1)}, bf16[256,1536]{1,0:T(8,128)(2,1)S(1)}, u32[]{:S(2)}, u32[]{:S(2)}) collective-permute-start(bf16[256,1536]{1,0:T(8,128)(2,1)S(1)} %constant_dynamic-update-slice_fusion.11), channel_id=1, source_target_pairs={{0,1},{1,0},{2,3},{3,2},{4,5},{5,4},{6,7},{7,6},{8,9},{9,8},{10,11... | collective-permute-start | bytes 2359304 | tf_op jit(solution)/shard_map/ppermute | solution.py:100
  155.9 104.6 %collective-permute-start.56 = (s32[32,128]{1,0:T(8,128)S(1)}, s32[32,128]{1,0:T(8,128)S(1)}, u32[]{:S(2)}, u32[]{:S(2)}) collective-permute-start(s32[32,128]{1,0:T(8,128)S(1)} %copy-done.100), channel_id=1, source_target_pairs={{0,2},{2,0},{4,6},{6,4},{8,10},{10,8},{12,14},{14,12},{16,18},{18,... | collective-permute-start | bytes 49160 | tf_op jit(solution)/shard_map/ppermute | solution.py:97
  157.8 99.9 %collective-permute-start.24 = (bf16[256,1536]{1,0:T(8,128)(2,1)S(1)}, bf16[256,1536]{1,0:T(8,128)(2,1)S(1)}, u32[]{:S(2)}, u32[]{:S(2)}) collective-permute-start(bf16[256,1536]{1,0:T(8,128)(2,1)S(1)} %pad_maximum_fusion.17), channel_id=1, source_target_pairs={{0,1},{1,0},{2,3},{3,2},{4,5},{5,4},{6,7},{7,6},{8,9},{9,8},{10,11... | collective-permute-start | bytes 2359304 | tf_op jit(solution)/shard_map/ppermute | solution.py:100
  159.3 101.3 %collective-permute-start.3 = (bf16[192,2048]{1,0:T(8,128)(2,1)S(1)}, bf16[192,2048]{1,0:T(8,128)(2,1)S(1)}, u32[]{:S(2)}, u32[]{:S(2)}) collective-permute-start(bf16[192,2048]{1,0:T(8,128)(2,1)S(1)} %pad_maximum_fusion.15), channel_id=1, source_target_pairs={{0,4},{2,6},{4,0},{6,2},{8,12},{10,14},{12,8},{14,10},{16,20},{18,... | collective-permute-start | bytes 2359304 | tf_op jit(solution)/shard_map/ppermute | solution.py:97
  260.6 43.8 %collective-permute-start.25 = (bf16[256,3072]{1,0:T(8,128)(2,1)}, bf16[256,3072]{1,0:T(8,128)(2,1)}, u32[]{:S(2)}, u32[]{:S(2)}) collective-permute-start(bf16[256,3072]{1,0:T(8,128)(2,1)} %pad_maximum_fusion.7), channel_id=1, source_target_pairs={{0,4},{2,6},{4,0},{6,2},{8,12},{10,14},{12,8},{14,10},{16,20},{18,... | collective-permute-start | bytes 4718600 | tf_op jit(solution)/shard_map/ppermute | solution.py:97
  267.2 43.4 %collective-permute-start.4 = (bf16[384,2048]{1,0:T(8,128)(2,1)}, bf16[384,2048]{1,0:T(8,128)(2,1)}, u32[]{:S(2)}, u32[]{:S(2)}) collective-permute-start(bf16[384,2048]{1,0:T(8,128)(2,1)} %get-tuple-element.163), channel_id=1, source_target_pairs={{0,2},{2,0},{4,6},{6,4},{8,10},{10,8},{12,14},{14,12},{16,18},{18,... | collective-permute-start | bytes 4718600 | tf_op jit(solution)/shard_map/ppermute | solution.py:97
  276.0 51.3 %collective-permute-start.19 = (bf16[512,3072]{1,0:T(8,128)(2,1)}, bf16[512,3072]{1,0:T(8,128)(2,1)}, u32[]{:S(2)}, u32[]{:S(2)}) collective-permute-start(bf16[512,3072]{1,0:T(8,128)(2,1)} %get-tuple-element.159), channel_id=1, source_target_pairs={{0,2},{2,0},{4,6},{6,4},{8,10},{10,8},{12,14},{14,12},{16,18},{18,... | collective-permute-start | bytes 9437192 | tf_op jit(solution)/shard_map/ppermute | solution.py:97
  279.3 51.8 %collective-permute-start.21 = (bf16[512,3072]{1,0:T(8,128)(2,1)}, bf16[512,3072]{1,0:T(8,128)(2,1)}, u32[]{:S(2)}, u32[]{:S(2)}) collective-permute-start(bf16[512,3072]{1,0:T(8,128)(2,1)} %collective-permute-done.20), channel_id=1, source_target_pairs={{0,2},{2,0},{4,6},{6,4},{8,10},{10,8},{12,14},{14,12},{16,18},{18,... | collective-permute-start | bytes 9437192 | tf_op jit(solution)/shard_map/ppermute | solution.py:97
  281.2 90.5 %collective-permute-start.15 = (bf16[512,512]{1,0:T(8,128)(2,1)}, bf16[512,512]{1,0:T(8,128)(2,1)}, u32[]{:S(2)}, u32[]{:S(2)}) collective-permute-start(bf16[512,512]{1,0:T(8,128)(2,1)} %collective-permute-done.14), channel_id=1, source_target_pairs={{0,2},{2,0},{4,6},{6,4},{8,10},{10,8},{12,14},{14,12},{16,18},{18,... | collective-permute-start | bytes 1572872 | tf_op jit(solution)/shard_map/ppermute | solution.py:97
  310.6 80.3 %collective-permute-start.26 = (bf16[512,3072]{1,0:T(8,128)(2,1)}, bf16[512,3072]{1,0:T(8,128)(2,1)}, u32[]{:S(2)}, u32[]{:S(2)}) collective-permute-start(bf16[512,3072]{1,0:T(8,128)(2,1)} %pad_maximum_fusion.3), channel_id=1, source_target_pairs={{0,2},{2,0},{4,6},{6,4},{8,10},{10,8},{12,14},{14,12},{16,18},{18,... | collective-permute-start | bytes 9437192 | tf_op jit(solution)/shard_map/ppermute | solution.py:97
  478.2 54.4 %collective-permute-start.32 = (bf16[512,1024]{1,0:T(8,128)(2,1)}, bf16[512,1024]{1,0:T(8,128)(2,1)}, u32[]{:S(2)}, u32[]{:S(2)}) collective-permute-start(bf16[512,1024]{1,0:T(8,128)(2,1)} %bitcast_convert_fusion.6), channel_id=1, source_target_pairs={{0,2},{2,0},{4,6},{6,4},{8,10},{10,8},{12,14},{14,12},{16,18},{18,... | collective-permute-start | bytes 3145736 | tf_op jit(solution)/shard_map/ppermute | solution.py:97
  478.3 99.2 %collective-permute-start.37 = (bf16[512,6144]{1,0:T(8,128)(2,1)}, bf16[512,6144]{1,0:T(8,128)(2,1)}, u32[]{:S(2)}, u32[]{:S(2)}) collective-permute-start(bf16[512,6144]{1,0:T(8,128)(2,1)} %bitcast_convert_fusion), channel_id=1, source_target_pairs={{0,2},{2,0},{4,6},{6,4},{8,10},{10,8},{12,14},{14,12},{16,18},{18,... | collective-permute-start | bytes 18874376 | tf_op jit(solution)/shard_map/ppermute | solution.py:97
  493.7 59.3 %collective-permute-start.47 = (bf16[384,2048]{1,0:T(8,128)(2,1)}, bf16[384,2048]{1,0:T(8,128)(2,1)}, u32[]{:S(2)}, u32[]{:S(2)}) collective-permute-start(bf16[384,2048]{1,0:T(8,128)(2,1)} %pad_maximum_fusion.8), channel_id=1, source_target_pairs={{0,2},{2,0},{4,6},{6,4},{8,10},{10,8},{12,14},{14,12},{16,18},{18,... | collective-permute-start | bytes 4718600 | tf_op jit(solution)/shard_map/ppermute | solution.py:97
  539.8 47.3 %collective-permute-start.27 = (bf16[512,3072]{1,0:T(8,128)(2,1)}, bf16[512,3072]{1,0:T(8,128)(2,1)}, u32[]{:S(2)}, u32[]{:S(2)}) collective-permute-start(bf16[512,3072]{1,0:T(8,128)(2,1)} %bitcast_convert_fusion.4), channel_id=1, source_target_pairs={{0,2},{2,0},{4,6},{6,4},{8,10},{10,8},{12,14},{14,12},{16,18},{18,... | collective-permute-start | bytes 9437192 | tf_op jit(solution)/shard_map/ppermute | solution.py:97
  539.9 59.7 %collective-permute-start.42 = (bf16[512,3072]{1,0:T(8,128)(2,1)}, bf16[512,3072]{1,0:T(8,128)(2,1)}, u32[]{:S(2)}, u32[]{:S(2)}) collective-permute-start(bf16[512,3072]{1,0:T(8,128)(2,1)} %bitcast_convert_fusion.2), channel_id=1, source_target_pairs={{0,2},{2,0},{4,6},{6,4},{8,10},{10,8},{12,14},{14,12},{16,18},{18,... | collective-permute-start | bytes 9437192 | tf_op jit(solution)/shard_map/ppermute | solution.py:97
  585.9 71.1 %collective-permute-start.38 = (bf16[512,3072]{1,0:T(8,128)(2,1)S(1)}, bf16[512,3072]{1,0:T(8,128)(2,1)S(1)}, u32[]{:S(2)}, u32[]{:S(2)}) collective-permute-start(bf16[512,3072]{1,0:T(8,128)(2,1)S(1)} %slice.387), channel_id=1, source_target_pairs={{0,1},{1,0},{2,3},{3,2},{4,5},{5,4},{6,7},{7,6},{8,9},{9,8},{10,11... | collective-permute-start | bytes 9437192 | tf_op jit(solution)/shard_map/ppermute | solution.py:100
  599.2 65.2 %collective-permute-start.51 = (bf16[24,2048]{1,0:T(8,128)(2,1)S(1)}, bf16[24,2048]{1,0:T(8,128)(2,1)S(1)}, u32[]{:S(2)}, u32[]{:S(2)}) collective-permute-start(bf16[24,2048]{1,0:T(8,128)(2,1)S(1)} %slice.415), channel_id=1, source_target_pairs={{0,16},{2,18},{4,20},{6,22},{8,24},{10,26},{12,28},{14,30},{16,0},... | collective-permute-start | bytes 294920 | tf_op jit(solution)/shard_map/ppermute | solution.py:97
  603.5 59.4 %collective-permute-start.43 = (bf16[256,3072]{1,0:T(8,128)(2,1)S(1)}, bf16[256,3072]{1,0:T(8,128)(2,1)S(1)}, u32[]{:S(2)}, u32[]{:S(2)}) collective-permute-start(bf16[256,3072]{1,0:T(8,128)(2,1)S(1)} %slice.397), channel_id=1, source_target_pairs={{0,4},{2,6},{4,0},{6,2},{8,12},{10,14},{12,8},{14,10},{16,20},{18,... | collective-permute-start | bytes 4718600 | tf_op jit(solution)/shard_map/ppermute | solution.py:97
  629.4 44.5 %collective-permute-start.29 = (bf16[256,1536]{1,0:T(8,128)(2,1)S(1)}, bf16[256,1536]{1,0:T(8,128)(2,1)S(1)}, u32[]{:S(2)}, u32[]{:S(2)}) collective-permute-start(bf16[256,1536]{1,0:T(8,128)(2,1)S(1)} %slice.369), channel_id=1, source_target_pairs={{0,1},{1,0},{2,3},{3,2},{4,5},{5,4},{6,7},{7,6},{8,9},{9,8},{10,11... | collective-permute-start | bytes 2359304 | tf_op jit(solution)/shard_map/ppermute | solution.py:100
  (175 other events, 2292.7 us)
Sparse Core Ops, SparseCore 0:
  11.6 103.9 all-gather.4
  119.1 59.5 all-gather.2

commit v2 on v0

v2 whole, which is shorter than its diff:
```python
import math
import types

import jax
import jax.numpy as jnp
from jax import lax
from jax.experimental import pallas as pl
from jax.experimental.pallas import tpu as pltpu
from jax.sharding import PartitionSpec as P

D = 1024
HEAD_DIM = 64
CD = 768
CLASSES = 1001
PD = 768
FOUR = 256
SEQ = 256
GROUPS = 4
NLEVELS = 1000
LOW = jnp.bfloat16
F32 = jnp.float32
TILE = 512
TABLE = 1024


HIGH = lax.Precision.HIGHEST
SIGMA_DATA = 0.5
LEARN_RATE = 0.05
DECAY = 0.1
BETA_ONE = 0.5
BETA_TWO = 0.5
ADAM_EPS = 1e-08
CLIP = 0.02
NORM_EPS = 1e-06
MIB = 1 << 20


def rms_norm(value):
    return value * lax.rsqrt(jnp.mean(value * value, axis=-1, keepdims=True) + NORM_EPS)


def dot_f32(left, right):
    return jnp.dot(left, right, preferred_element_type=F32)


def dot_nt(left, right):
    return lax.dot_general(left, right, (((1,), (1,)), ((), ())), preferred_element_type=F32)


def dot_tn(left, right):
    return lax.dot_general(left, right, (((0,), (0,)), ((), ())), preferred_element_type=F32)


def noise_terms(levels):
    log_sigma = -3.0 + 6.0 * levels.astype(F32) / (NLEVELS - 1)
    sigma = jnp.exp(log_sigma)
    radius = jnp.sqrt(sigma * sigma + SIGMA_DATA * SIGMA_DATA)
    half = FOUR // 2
    freqs = jnp.exp(-2.0 + 4.0 * jnp.arange(half, dtype=F32) / (half - 1))
    angles = 2.0 * math.pi * (log_sigma / 4.0)[:, None] * freqs[None, :]
    return (sigma, radius, jnp.concatenate([jnp.cos(angles), jnp.sin(angles)], axis=1))


class Rounds:
    def __init__(self, have):
        self.token = jnp.zeros((8, 128), F32)
        self.have, self.tied = have, set()

    def __call__(self, runs, works, held=()):
        fields = {name: value for name, value in vars(self.have).items() if name not in self.tied}
        values, form = jax.tree.flatten((fields, [run.waiting for run in (*runs, *held)]))
        *values, self.token = lax.optimization_barrier((*values, self.token))
        fields, waiting = jax.tree.unflatten(form, values)
        vars(self.have).update(fields)
        self.tied.update(fields)
        for run, value in zip(held, waiting[len(runs) :]):
            run.waiting = value
        for run, value in zip(runs, waiting):
            run.go_on(value)
        for work in works:
            work()


def params(vmem=40):
    return pltpu.CompilerParams(vmem_limit_bytes=vmem * MIB)


def cost(*_):
    return pl.CostEstimate(flops=1, bytes_accessed=1, transcendentals=0)


def simple(kernel, columns, in_specs, args, out_rows, out_lead=()):
    width = columns
    while width > 1024 and width % 256 == 0:
        width //= 2
    return pl.pallas_call(
        kernel,
        grid=(columns // width,),
        in_specs=[spec(width) for spec in in_specs],
        out_specs=[pl.BlockSpec((rows, width), lambda j: (0, j)) for rows in out_rows],
        out_shape=[jax.ShapeDtypeStruct((rows, columns), LOW) for rows in out_rows],
        compiler_params=params(),
        cost_estimate=cost(),
    )(*args)


def rows_spec(rows, at=0):
    return lambda width: pl.BlockSpec((rows, width), lambda j: (at, j))


def part_spec(pair, half, at):
    return lambda width: pl.BlockSpec((1, half, width), lambda j: (pair, at, j))


def even(*rows):
    return all(row % 16 == 0 for row in rows)


def one_below_other(*parts):
    rows, columns = parts[0].shape
    if not even(rows):
        return jnp.concatenate(parts, axis=0)

    def kernel(*refs):
        *refs, out_ref = refs
        for i, ref in enumerate(refs):
            out_ref[i * rows : (i + 1) * rows, :] = ref[...]

    specs = [rows_spec(rows)] * len(parts)
    return simple(kernel, columns, specs, parts, (len(parts) * rows,))[0]


def top_and_bottom(first, second):
    rows, columns = first.shape
    half = rows // 2
    if not even(half):
        return first[:half], second[half:]

    def kernel(first_ref, second_ref, top_ref, bottom_ref):
        top_ref[...] = first_ref[...]
        bottom_ref[...] = second_ref[...]

    specs = [rows_spec(half), rows_spec(half, 1)]
    return simple(kernel, columns, specs, (first, second), (half, half))


def add(*terms):
    return sum(term.astype(F32) for term in terms).astype(LOW)


def add_corners(own, came):
    _, rows, columns = own.shape
    half = rows // 2
    quarter = half // 2
    if not even(quarter):
        total = add(own[1, half:], came)
        return total[:quarter], total[quarter:]

    def kernel(own_ref, came_ref, x_ref, pair_ref):
        x_ref[...] = add(own_ref[0, :quarter], came_ref[:quarter])
        pair_ref[...] = add(own_ref[0, quarter:], came_ref[quarter:])

    specs = [part_spec(1, half, 1), rows_spec(half)]
    return simple(kernel, columns, specs, (own, came), (quarter, quarter))


def add_sides(own, came_pair, came_x, from_x, from_pair):
    _, rows, columns = own.shape
    half = rows // 2
    quarter = half // 2
    if not even(quarter):
        to_pair = add(own[1, :half], came_pair, jnp.pad(from_x, ((0, half - quarter), (0, 0))))
        to_x = add(own[0, half:], came_x, jnp.pad(from_pair, ((quarter, 0), (0, 0))))
        return to_pair, to_x

    def kernel(own_a, came_a, own_b, came_b, x_ref, pair_ref, to_pair, to_x):
        to_pair[:quarter, :] = add(own_a[0, :quarter], came_a[:quarter], x_ref[...])
        to_pair[quarter:, :] = add(own_a[0, quarter:], came_a[quarter:])
        to_x[:quarter, :] = add(own_b[0, :quarter], came_b[:quarter])
        to_x[quarter:, :] = add(own_b[0, quarter:], came_b[quarter:], pair_ref[...])

    first, second = part_spec(1, half, 0), part_spec(0, half, 1)
    side, corner = rows_spec(half), rows_spec(quarter)
    specs = [first, side, second, side, corner, corner]
    args = (own, came_pair, own, came_x, from_x, from_pair)
    return simple(kernel, columns, specs, args, (half, half))


def add_parts(count, *terms):
    columns = terms[0].shape[-1]
    rows = terms[-1].shape[0]
    size = rows // count
    cuts = [slice(i * size, (i + 1) * size) for i in range(count)]
    if not even(size):
        terms = [term[0, :rows] if term.ndim == 3 else term for term in terms]
        return tuple(add(*(term[cut] for term in terms)) for cut in cuts)

    def kernel(*refs):
        refs, outs = refs[: len(terms)], refs[len(terms) :]
        parts = [ref.at[0] if len(ref.shape) == 3 else ref for ref in refs]
        for cut, out in zip(cuts, outs):
            out[...] = add(*(part[cut, :] for part in parts))

    specs = [part_spec(0, rows, 0) if term.ndim == 3 else rows_spec(rows) for term in terms]
    return simple(kernel, columns, specs, terms, (size,) * count)


class Links:
    def __init__(self, size):
        self.size = size
        self.bits = size.bit_length() - 1
        assert 1 << self.bits == size
        self.upper = list(range(self.bits - 1, 1, -1))

    def swap(self, value, mask):
        return lax.ppermute(value, "dp", [(i, i ^ mask) for i in range(self.size)])

    def flip(self, value, bit):
        return self.swap(value, 1 << bit)

    def far(self):
        if len(self.upper) != 2:
            return None
        first, second = (1 << bit for bit in self.upper)
        return (first, second, first | second)

    def flip_pair(self, value):
        return lax.ppermute(value, "tensor", [(0, 1), (1, 0)])

    def gather(self, value, groups=((0, 1, 2),)):
        if self.far():
            (value,) = yield (value,)
            parts = [value]
            for group in groups:
                parts = [*parts] + [self.swap(value, self.far()[i]) for i in group]
                parts = yield tuple(parts)
            value = one_below_other(*parts)
        else:
            for bit in self.upper:
                (value,) = yield (value,)
                value = one_below_other(value, self.flip(value, bit))
            (value,) = yield (value,)
        by_x, by_pair = self.flip(value, 1), self.flip_pair(value)
        by_x, by_pair = yield (by_x, by_pair)
        top, bottom = top_and_bottom(by_pair, by_x)
        corner = (self.flip(top, 1), self.flip_pair(bottom))
        pieces = [value, by_x, by_pair, *corner]
        pieces = yield tuple(pieces)
        pieces = list(pieces)
        return pieces + [self.flip(piece, 0) for piece in pieces]

    def gather_rows(self, value):
        for bit in (1, None, 0):
            (value,) = yield (value,)
            other = self.flip_pair(value) if bit is None else self.flip(value, bit)
            value = jnp.concatenate([value, other], axis=0)
        return value


    def place(self, index):
        return sum(((index >> i) & 1) << (bit - 2) for i, bit in enumerate(self.upper))

    def index(self, place):
        return sum(((place >> (bit - 2)) & 1) << i for i, bit in enumerate(self.upper))

    def along(self, values):
        others = [
            self.swap(value, self.place(i + 1) << 2) for i, value in enumerate(values[1:])
        ]
        return [values[0], *others]

    def seen_from_here(self, value, index):
        order = [i ^ index for i in range(value.shape[0])]
        return jnp.concatenate([value[i : i + 1] for i in order], axis=0)

    def reduce(self, own, *others):
        others = yield others
        corner, side, across, kept = (self.flip(others[i], 0) for i in (3, 2, 1, 0))
        (corner,) = yield (corner,)
        corner_x, corner_pair = add_corners(own, corner)
        from_x, from_pair = self.flip(corner_x, 1), self.flip_pair(corner_pair)
        from_x, from_pair, side, across = yield (from_x, from_pair, side, across)
        to_pair, to_x = add_sides(own, side, across, from_x, from_pair)
        came = kept
        terms = (own, came, self.flip_pair(to_pair), self.flip(to_x, 1))
        if self.far():
            terms = yield terms
            kept, *sent = add_parts(4, *terms)
            terms = (kept, *(self.swap(part, mask) for part, mask in zip(sent, self.far())))
        else:
            for bit in reversed(self.upper):
                terms = yield terms
                kept, sent = add_parts(2, *terms)
                terms = (kept, self.flip(sent, bit))
        terms = yield terms
        return sum(term.astype(F32) for term in terms)

    def total(self, value):
        value = value + self.flip(value, 0)
        value = value + self.flip_pair(value)
        for bit in [1] + self.upper[::-1]:
            value = value + self.flip(value, bit)
        return value


class Run:
    def __init__(self, steps=None):
        self.result = None
        if steps is not None:
            self.begin(steps)

    def begin(self, steps):
        self.steps, self.waiting = steps, next(steps)

    def go_on(self, values):
        assert self.result is None
        try:
            self.waiting = self.steps.send(values)
        except StopIteration as stop:
            self.result = stop.value

    def finish(self):
        while self.result is None:
            self.go_on(self.waiting)
        return self.result


def reverse_bits(value, bits):
    result = 0
    for bit in range(bits):
        result |= ((value >> bit) & 1) << (bits - 1 - bit)
    return result


def spread(places, own, block):
    order = jnp.array(places, jnp.int32) ^ own
    return (order[:, None] * block + jnp.arange(block)[None, :]).reshape(-1)


def order_matrix(size, order):
    return (jnp.arange(size)[:, None] == order[None, :]).astype(LOW)


def whole(shape):
    return pl.BlockSpec(shape, lambda *_: (0,) * len(shape))


def piece_specs(pieces, width, at):
    return [pl.BlockSpec((piece.shape[0], width), lambda j: (0, at + j)) for piece in pieces]


def both_spec(rows, width, at=0):
    return pl.BlockSpec((2, rows, width), lambda j: (0, 0, at + j))


def assemble(pieces):
    starts = [0]
    for piece in pieces:
        starts.append(starts[-1] + piece.shape[0])
    columns = pieces[0].shape[1]

    def kernel(*refs):
        *refs, out_ref = refs
        for ref, start in zip(refs, starts):
            out_ref[start : start + ref.shape[0], :] = ref[...]

    return pl.pallas_call(
        kernel,
        grid=(columns // (2 * TILE),),
        in_specs=piece_specs(pieces, 2 * TILE, 0),
        out_specs=pl.BlockSpec((starts[-1], 2 * TILE), lambda j: (0, j)),
        out_shape=jax.ShapeDtypeStruct((starts[-1], columns), LOW),
        compiler_params=params(),
        cost_estimate=cost(),
    )(*pieces)


def rows_matmul(x, matrix, columns, at):
    rows = x.shape[0]

    def kernel(x_ref, matrix_ref, out_ref):
        for pair in range(2):
            out_ref[pair] = dot_f32(x_ref[...], matrix_ref[pair]).astype(LOW)

    return pl.pallas_call(
        kernel,
        grid=(columns // TILE,),
        in_specs=[whole(x.shape), both_spec(D, TILE, at)],
        out_specs=both_spec(rows, TILE),
        out_shape=jax.ShapeDtypeStruct((2, rows, columns), LOW),
        compiler_params=params(),
        cost_estimate=cost(),
    )(x, matrix)


def expand_forward(x, matrix, columns):
    rows = x.shape[0]

    def kernel(x_ref, matrix_ref, gated_ref, hidden_ref):
        for pair in range(2):
            gate = dot_f32(x_ref[...], matrix_ref[pair, :, :TILE])
            upper = dot_f32(x_ref[...], matrix_ref[pair, :, TILE:])
            gated_ref[pair, :, :TILE] = gate.astype(LOW)
            gated_ref[pair, :, TILE:] = upper.astype(LOW)
            hidden_ref[pair] = (jax.nn.gelu(gate) * upper).astype(LOW)

    return pl.pallas_call(
        kernel,
        grid=(columns // (2 * TILE),),
        in_specs=[whole(x.shape), both_spec(D, 2 * TILE)],
        out_specs=[both_spec(rows, 2 * TILE), both_spec(rows, TILE)],
        out_shape=[
            jax.ShapeDtypeStruct((2, rows, columns), LOW),
            jax.ShapeDtypeStruct((2, rows, columns // 2), LOW),
        ],
        compiler_params=params(),
        cost_estimate=cost(),
    )(x, matrix)


def gelu_parts(gate):
    root, cube = math.sqrt(2.0 / math.pi), 0.044715
    square = gate * gate
    slope = jnp.tanh(root * (gate + cube * gate * square))
    half = 0.5 * (1.0 + slope)
    turn = 0.5 * gate * (1.0 - slope * slope) * root * (1.0 + 3.0 * cube * square)
    return gate * half, half + turn


def shrink_backward(x, matrix, at, gated):
    rows = x.shape[0]
    columns = gated.shape[2] // 2

    def kernel(x_ref, gated_ref, matrix_ref, out_ref):
        for pair in range(2):
            grad = dot_f32(x_ref[...], matrix_ref[pair])
            gate = gated_ref[pair, :, :TILE].astype(F32)
            upper = gated_ref[pair, :, TILE:].astype(F32)
            value, slope = gelu_parts(gate)
            out_ref[pair, :, :TILE] = (grad * upper * slope).astype(LOW)
            out_ref[pair, :, TILE:] = (grad * value).astype(LOW)

    both = both_spec(rows, 2 * TILE)
    return pl.pallas_call(
        kernel,
        grid=(columns // TILE,),
        in_specs=[whole(x.shape), both, both_spec(D, TILE, at)],
        out_specs=both,
        out_shape=jax.ShapeDtypeStruct(gated.shape, LOW),
        compiler_params=params(),
        cost_estimate=cost(),
    )(x, gated, matrix)


def cols_sum(value_ref, matrix_ref):
    return dot_nt(value_ref[0], matrix_ref[0]) + dot_nt(value_ref[1], matrix_ref[1])


def norm_out(value, scale_ref, resid_ref, rows_ref):
    images = scale_ref.shape[0]
    resid_ref[...] = value
    for i in range(images):
        span = slice(i * SEQ, (i + 1) * SEQ)
        part = resid_ref[span, :]
        rows_ref[span, :] = (rms_norm(part) * scale_ref[i : i + 1, :]).astype(LOW)


def norm_grad(resid, scale, grad):
    root = lax.rsqrt(jnp.mean(resid * resid, axis=-1, keepdims=True) + NORM_EPS)
    normed = resid * root
    inner = grad * scale
    back = root * (inner - normed * jnp.mean(inner * normed, axis=-1, keepdims=True))
    return back, jnp.sum(grad * normed, axis=0, keepdims=True)


def cols_forward(value, matrix, width, at, resid, scale):
    _, rows, columns = value.shape
    steps = columns // width

    def kernel(value_ref, resid_ref, scale_ref, matrix_ref, out_ref, rows_ref, acc_ref):
        @pl.when(pl.program_id(0) == 0)
        def _():
            acc_ref[...] = resid_ref[...]

        acc_ref[...] += cols_sum(value_ref, matrix_ref)

        @pl.when(pl.program_id(0) == steps - 1)
        def _():
            norm_out(acc_ref[...], scale_ref, out_ref, rows_ref)

    return pl.pallas_call(
        kernel,
        grid=(steps,),
        in_specs=[
            both_spec(rows, width),
            whole(resid.shape),
            whole(scale.shape),
            both_spec(D, width, at),
        ],
        out_specs=[whole(resid.shape), whole(resid.shape)],
        out_shape=[
            jax.ShapeDtypeStruct(resid.shape, F32),
            jax.ShapeDtypeStruct(resid.shape, LOW),
        ],
        scratch_shapes=[pltpu.VMEM(resid.shape, F32)],
        compiler_params=params(),
        cost_estimate=cost(),
    )(value, resid, scale, matrix)


def cols_backward(value, matrix, width, at, resid, scale, grad, types):
    _, rows, columns = value.shape
    steps = columns // width

    def kernel(value_ref, resid_ref, scale_ref, grad_ref, matrix_ref, scale_out, *outs):
        *outs, acc_ref = outs

        @pl.when(pl.program_id(0) == 0)
        def _():
            acc_ref[...] = cols_sum(value_ref, matrix_ref)

        @pl.when(pl.program_id(0) > 0)
        def _():
            acc_ref[...] += cols_sum(value_ref, matrix_ref)

        @pl.when(pl.program_id(0) == steps - 1)
        def _():
            for i in range(scale_ref.shape[0]):
                span = slice(i * SEQ, (i + 1) * SEQ)
                back, scale_out[i : i + 1, :] = norm_grad(
                    resid_ref[span, :], scale_ref[i : i + 1, :], acc_ref[span, :]
                )
                back = back + grad_ref[span, :]
                for out in outs:
                    out[span, :] = back.astype(out.dtype)

    return pl.pallas_call(
        kernel,
        grid=(steps,),
        in_specs=[
            both_spec(rows, width),
            whole(resid.shape),
            whole(scale.shape),
            whole(resid.shape),
            both_spec(D, width, at),
        ],
        out_specs=[whole(scale.shape)] + [whole(resid.shape)] * len(types),
        out_shape=[jax.ShapeDtypeStruct(scale.shape, F32)]
        + [jax.ShapeDtypeStruct(resid.shape, kind) for kind in types],
        scratch_shapes=[pltpu.VMEM(resid.shape, F32)],
        compiler_params=params(),
        cost_estimate=cost(),
    )(value, resid, scale, grad, matrix)


def weight_grads(from_own, first, *pairs):
    rows, depth = pairs[0][0].shape
    half = depth // 2
    quarter = half // 2
    tiles = [value.shape[2] // TILE for _, value in pairs]
    starts = [sum(tiles[:i]) for i in range(len(tiles))]
    columns = sum(tiles) * TILE

    def kernel(*refs):
        count = len(pairs)
        order_ref, first_ref, *refs = refs
        x_refs, value_refs = refs[:count], refs[count : 2 * count]
        own_ref, *parts = refs[2 * count : 2 * count + 5]
        turned = refs[2 * count + 5 :]
        step = pl.program_id(0)
        for i in range(count):

            @pl.when(step == starts[i])
            def _():
                turned[i][...] = dot_nt(order_ref[...], x_refs[i][...]).astype(LOW)

            @pl.when((step >= starts[i]) & (step < starts[i] + tiles[i]))
            def _():
                for pair in range(2):
                    value = value_refs[i][first_ref[0] ^ pair]
                    own_ref[pair] = dot_f32(turned[i][:half, :], value).astype(LOW)
                    other = dot_f32(turned[i][half:, :], value).astype(LOW)
                    parts[2 * pair][...] = other[:quarter]
                    parts[2 * pair + 1][...] = other[quarter:]

    def value_spec(i):
        return pl.BlockSpec(
            (2, rows, TILE), lambda j: (0, 0, jnp.clip(j - starts[i], 0, tiles[i] - 1))
        )

    return pl.pallas_call(
        kernel,
        grid=(columns // TILE,),
        in_specs=[whole(from_own.shape), pl.BlockSpec(memory_space=pltpu.SMEM)]
        + [whole(x.shape) for x, _ in pairs]
        + [value_spec(i) for i in range(len(pairs))],
        out_specs=[pl.BlockSpec((2, half, TILE), lambda j: (0, 0, j))]
        + [pl.BlockSpec((quarter, TILE), lambda j: (0, j))] * 4,
        out_shape=[jax.ShapeDtypeStruct((2, half, columns), LOW)]
        + [jax.ShapeDtypeStruct((quarter, columns), LOW)] * 4,
        scratch_shapes=[pltpu.VMEM((depth, rows), LOW) for _ in pairs],
        compiler_params=params(),
        cost_estimate=cost(),
    )(from_own, first, *(x for x, _ in pairs), *(value for _, value in pairs))


def head_part(ref, part):
    return ref[0, :, part * HEAD_DIM : (part + 1) * HEAD_DIM]


def softmax_turned(queries, keys):
    scores = dot_nt(keys, queries) * (1.0 / math.sqrt(HEAD_DIM))
    scores = jnp.exp(scores - jnp.max(scores, axis=0, keepdims=True))
    return scores * (1.0 / jnp.sum(scores, axis=0, keepdims=True))


def attention_specs(width):
    return [
        pl.BlockSpec((1, SEQ, width), lambda i, j, part=part: (i, j, part)) for part in range(3)
    ]


def attention_forward(project, width):
    rows = project.shape[1]

    def kernel(q_ref, k_ref, v_ref, out_ref):
        for part in range(width // HEAD_DIM):
            scores = dot_nt(head_part(q_ref, part), head_part(k_ref, part))
            scores = scores * (1.0 / math.sqrt(HEAD_DIM))
            scores = jnp.exp(scores - jnp.max(scores, axis=-1, keepdims=True))
            probs = scores * (1.0 / jnp.sum(scores, axis=-1, keepdims=True))
            mixed = dot_f32(probs.astype(LOW), head_part(v_ref, part))
            out_ref[0, :, part * HEAD_DIM : (part + 1) * HEAD_DIM] = mixed.astype(LOW)

    return pl.pallas_call(
        kernel,
        grid=(2, rows // SEQ),
        in_specs=attention_specs(width),
        out_specs=pl.BlockSpec((1, SEQ, width), lambda i, j: (i, j, 0)),
        out_shape=jax.ShapeDtypeStruct((2, rows, width), LOW),
        compiler_params=params(),
        cost_estimate=cost(8 * rows * SEQ * width, 16 * rows * width),
    )(project, project, project)


def attention_backward(project, grad, width):
    rows = project.shape[1]
    inverse_root = 1.0 / math.sqrt(HEAD_DIM)

    def kernel(q_ref, k_ref, v_ref, grad_ref, out_ref):
        for part in range(width // HEAD_DIM):
            queries, keys = head_part(q_ref, part), head_part(k_ref, part)
            values, grad = head_part(v_ref, part), head_part(grad_ref, part)
            probs = softmax_turned(queries, keys)
            grad_values = dot_f32(probs.astype(LOW), grad)
            grad_probs = dot_nt(values, grad)
            inner = jnp.sum(grad_probs * probs, axis=0, keepdims=True)
            grad_scores = (probs * (grad_probs - inner)).astype(LOW)
            grad_queries = dot_tn(keys, grad_scores).T * inverse_root
            grad_keys = dot_f32(grad_scores, queries) * inverse_root
            for place, value in enumerate((grad_queries, grad_keys, grad_values)):
                start = place * width + part * HEAD_DIM
                out_ref[0, :, start : start + HEAD_DIM] = value.astype(LOW)

    return pl.pallas_call(
        kernel,
        grid=(2, rows // SEQ),
        in_specs=attention_specs(width) + [pl.BlockSpec((1, SEQ, width), lambda i, j: (i, j, 0))],
        out_specs=pl.BlockSpec((1, SEQ, 3 * width), lambda i, j: (i, j, 0)),
        out_shape=jax.ShapeDtypeStruct((2, rows, 3 * width), LOW),
        compiler_params=params(),
        cost_estimate=cost(20 * rows * SEQ * width, 28 * rows * width),
    )(project, project, project, grad)


def loss_kernel(last, patch_out, target, coef, resid, scale):
    rows = last.shape[0]
    images = scale.shape[0]

    def kernel(
        last_ref, out_ref, target_ref, coef_ref, resid_ref, scale_ref,
        loss_ref, low_ref, grad_ref, rows_ref, scale_out,
    ):
        for i in range(images):
            span = slice(i * SEQ, (i + 1) * SEQ)
            diff = dot_nt(last_ref[span, :], out_ref[...]) - target_ref[span, :]
            total = jnp.sum(jnp.sum(diff * diff, axis=1, keepdims=True), axis=0, keepdims=True)
            loss_ref[i : i + 1, :] = jnp.broadcast_to(total, (1, 128))
            low = (diff * coef_ref[i : i + 1, :1]).astype(LOW)
            low_ref[span, :] = low
            back, scale_out[i : i + 1, :] = norm_grad(
                resid_ref[span, :], scale_ref[i : i + 1, :], dot_f32(low, out_ref[...])
            )
            grad_ref[span, :] = back
            rows_ref[span, :] = back.astype(LOW)

    return pl.pallas_call(
        kernel,
        out_shape=[
            jax.ShapeDtypeStruct((images, 128), F32),
            jax.ShapeDtypeStruct((rows, PD), LOW),
            jax.ShapeDtypeStruct((rows, D), F32),
            jax.ShapeDtypeStruct((rows, D), LOW),
            jax.ShapeDtypeStruct((images, D), F32),
        ],
        compiler_params=params(),
        cost_estimate=cost(4 * rows * D * PD, 16 * rows * D),
    )(last, patch_out, target, coef, resid, scale)


def body(
    clean_images,
    noise_draw,
    levels,
    labels,
    dropped,
    groups,
    step_count,
    inward,
    first_inward,
    second_inward,
    outward,
    first_outward,
    second_outward,
    expand,
    first_expand,
    second_expand,
    shrink,
    first_shrink,
    second_shrink,
    patches,
    first_patches,
    second_patches,
    classes,
    first_classes,
    second_classes,
    mapping,
    first_mapping,
    second_mapping,
):
    masters = (inward, outward, expand, shrink, patches, classes, mapping)
    firsts = (
        first_inward,
        first_outward,
        first_expand,
        first_shrink,
        first_patches,
        first_classes,
        first_mapping,
    )
    seconds = (
        second_inward,
        second_outward,
        second_expand,
        second_shrink,
        second_patches,
        second_classes,
        second_mapping,
    )
    links = Links(lax.axis_size("dp"))
    me, pair = lax.axis_index("dp"), lax.axis_index("tensor")
    own_place = me * 2 + pair
    images = clean_images.shape[0]
    rows = images * SEQ
    width = inward.shape[2]
    ff_width = expand.shape[2]
    ff_tiles = ff_width // TILE
    map_rows = mapping.shape[0]

    have = types.SimpleNamespace()
    rounds = Rounds(have)

    def turn(*values):
        return values[0] if len(values) == 1 else values

    flat_patch = jnp.concatenate([patches[0], patches[1]], axis=1).astype(LOW)
    table = jnp.pad(classes.T, ((0, 0), (0, TABLE - CLASSES)))
    flat_map = jnp.concatenate([table, mapping], axis=1).astype(LOW)
    flat_up = expand.reshape(-1, 2, ff_tiles, TILE).transpose(0, 2, 1, 3)
    flat = jnp.concatenate(
        [
            flat_up.reshape(expand.shape[0], -1),
            shrink.T,
            inward.reshape(inward.shape[0], -1),
            outward.T,
        ],
        axis=1,
    ).astype(LOW)
    block = lax.all_gather(flat, ("tensor", "dp"), axis=0, tiled=True)
    block = block.reshape(2, D, flat.shape[1])
    at_down = 2 * ff_tiles
    at_in = 3 * ff_tiles
    at_out = at_in + 3 * width // TILE
    g_p = Run(links.gather(flat_patch))
    g_m = Run(links.gather_rows(flat_map))
    s_p, s_a, s_e, s_s, rows_run = (Run() for _ in range(5))
    line = links.size // 4
    part = 8 * map_rows

    n_up = len(links.upper)

    order_d = spread([reverse_bits(i, links.bits) for i in range(links.size)], me, D // links.size)
    to_own = order_matrix(D, order_d)
    from_own = to_own.T
    this_pair = pair.reshape(1)
    places = []
    for i in range(2 * links.size):
        place = 0
        for bit, step in enumerate(links.upper):
            place |= ((i >> bit) & 1) << (step + 1)
        place |= ((i >> n_up) & 1) << 2
        place |= (i >> (n_up + 1)) & 1
        place |= ((i >> (n_up + 2)) & 1) << 1
        places.append(place)
    order_p = spread(places, own_place, map_rows)
    to_own_p = order_matrix(PD, order_p)

    sigma, radius, _ = noise_terms(levels)
    chosen = jnp.where(dropped == 1, CLASSES - 1, labels)
    sig = jnp.repeat(sigma, SEQ)[:, None]
    rad = jnp.repeat(radius, SEQ)[:, None]
    clean_float = dot_f32(clean_images.reshape(rows, PD), to_own_p)
    noise_float = dot_f32(noise_draw.reshape(rows, PD), to_own_p)
    inputs = ((clean_float + sig * noise_float) / rad).astype(LOW)
    target = (sig * clean_float - SIGMA_DATA * SIGMA_DATA * noise_float) / (SIGMA_DATA * rad)
    counts = jnp.sum((groups[:, None] == groups[None, :]).astype(F32), axis=1)
    weight = 1.0 / (GROUPS * counts)

    coef = jnp.broadcast_to((2.0 * weight / (SEQ * PD))[:, None], (images, 128))


    def in_order(values, axis):
        found = []
        for i in range(line):
            index = links.index(i ^ (me // 4))
            found.append(sum(jnp.where(index == j, v, 0) for j, v in enumerate(values)))
        return jnp.concatenate(found, axis=axis)

    def cut_for_line(value):
        return [
            lax.dynamic_slice_in_dim(value, ((me // 4) ^ links.place(i)) * part, part, axis=1)
            for i in range(line)
        ]

    def seen(values):
        shape = (line, images, -1)
        return sum(
            links.seen_from_here(value.reshape(shape), i) for i, value in enumerate(values)
        ).reshape(line * images, -1)

    def run_names():
        names = jnp.stack([chosen, levels], axis=1)
        have.names = links.along([turn(names)] * line)

    def run_cond():
        names = jnp.concatenate(have.names, axis=0)
        have.chosen, have.levels = names[:, 0], names[:, 1]
        have.feats_low = noise_terms(have.levels)[2].astype(LOW)
        onehot = (have.chosen[:, None] == jnp.arange(TABLE)[None, :]).astype(LOW)
        known = jnp.concatenate([onehot, have.feats_low], axis=1)
        places = [((i & 1) << 2) | ((i >> 1) & 1) | ((i >> 2) << 1) for i in range(8)]
        order_m = order_matrix(part, spread(places, own_place % 8, map_rows))
        map_part = dot_f32(order_m, g_m.finish()).astype(LOW)
        have.map_in = map_part[:, TABLE + FOUR : TABLE + FOUR + CD]
        have.map_out = map_part[:, TABLE + FOUR + CD :]
        have.cond_zero = dot_nt(known, map_part[:, : TABLE + FOUR])
        squares = jnp.sum(have.cond_zero * have.cond_zero, axis=1, keepdims=True)
        squares = turn(jnp.broadcast_to(squares, (line * images, 128)))
        have.squares = links.along([squares] * line)

    def run_inner():
        squares = seen(turn(*have.squares))[:, :1]
        have.root = lax.rsqrt(squares * (1.0 / CD) + NORM_EPS)
        have.normed = (have.cond_zero * have.root).astype(LOW)
        have.inners = links.along(turn(*cut_for_line(dot_f32(have.normed, have.map_in))))

    def run_scales():
        have.inner = seen(turn(*have.inners))
        have.cond_low = (have.cond_zero + jax.nn.gelu(have.inner)).astype(LOW)
        scales = dot_f32(have.cond_low, have.map_out)
        scales = turn(*(scales[i * images : (i + 1) * images] for i in range(line)))
        have.scale_parts = links.along(scales)

    def run_map():
        scales = 1.0 + sum(turn(*have.scale_parts))
        have.scales = scales.reshape(images, 3, D)

    def run_patch():
        have.patch_all = assemble(g_p.finish())
        have.resid_zero = dot_f32(inputs, have.patch_all[:, :D])

    def run_in():
        rows_zero = rms_norm(have.resid_zero) * jnp.repeat(have.scales[:, 0], SEQ, axis=0)
        have.rows_zero = rows_zero.astype(LOW)
        have.project = rows_matmul(have.rows_zero, block, 3 * width, at_in)

    def run_mix():
        have.mixed = turn(attention_forward(have.project, width))

    def run_out():
        have.resid_one, have.rows_one = cols_forward(
            have.mixed, block, TILE, at_out, have.resid_zero, have.scales[:, 1]
        )

    def run_up():
        have.gated, have.hidden = expand_forward(have.rows_one, block, 2 * ff_width)

    def run_down():
        have.resid_two, have.last = cols_forward(
            have.hidden, block, TILE, at_down, have.resid_one, have.scales[:, 2]
        )

    def run_loss():
        have.squared, have.grad_low, have.grad_two, have.rows_two, have.scale_two = loss_kernel(
            have.last, have.patch_all[:, D:], target, coef, have.resid_two, have.scales[:, 2]
        )

    def start(run, parts):
        run.begin(links.reduce(*parts))

    def patch_grad(left, right):
        half, part = PD // 2, PD // 8
        own = dot_tn(left[:, :half], right).astype(LOW).reshape(2, half // 2, D)
        other = dot_tn(left[:, half:], right).astype(LOW)
        return [own] + [other[i * part : (i + 1) * part] for i in range(4)]

    def grad_down():
        start(s_s, weight_grads(from_own, this_pair, (have.rows_two, have.hidden)))

    def back_down():
        have.gated_grad = shrink_backward(have.rows_two, block, at_down, have.gated)

    def grad_up():
        start(s_e, weight_grads(from_own, this_pair, (have.rows_one, have.gated_grad)))

    def back_up():
        have.scale_one, have.grad_one, have.rows_grad = cols_backward(
            have.gated_grad, block, 2 * TILE, 0, have.resid_one, have.scales[:, 1],
            have.grad_two, (F32, LOW),
        )

    def back_out():
        have.grad_mixed = rows_matmul(have.rows_grad, block, width, at_out)

    def back_mix():
        have.grad_project = attention_backward(have.project, have.grad_mixed, width)

    def grad_in():
        start(
            s_a,
            weight_grads(
                from_own, this_pair,
                (have.rows_zero, have.grad_project), (have.rows_grad, have.mixed),
            ),
        )

    def back_in():
        have.scale_zero, have.grad_zero = cols_backward(
            have.grad_project, block, TILE, at_in, have.resid_zero, have.scales[:, 0],
            have.grad_one, (LOW,),
        )

    def grad_patch():
        parts = zip(patch_grad(inputs, have.grad_zero), patch_grad(have.grad_low, have.last))
        start(s_p, [jnp.concatenate(part, axis=-1) for part in parts])

    def back_map():
        grad_scales = jnp.stack([have.scale_zero, have.scale_one, have.scale_two], axis=1)
        scales_low = grad_scales.reshape(images, 3 * D).astype(LOW)
        have.scale_grads = links.along([turn(scales_low)] * line)

    def back_scales():
        have.scales_low = jnp.concatenate(turn(*have.scale_grads), axis=0)
        have.grad_cond = dot_nt(have.scales_low, have.map_out)
        _, pull_gelu = jax.vjp(jax.nn.gelu, have.inner)
        (grad_inner,) = pull_gelu(have.grad_cond)
        low = grad_inner.astype(LOW)
        inner = jnp.sum(low.astype(F32) * have.inner, axis=1, keepdims=True)
        have.inner_grads = links.along([low] * line)
        have.sums = links.along([jnp.broadcast_to(inner, (line * images, 128))] * line)

    def back_cond():
        grads = [
            links.seen_from_here(grad.reshape(line, images, part), i)
            for i, grad in enumerate(have.inner_grads)
        ]
        have.inner_low = in_order(grads, 2).reshape(line * images, CD)
        grad_normed = dot_nt(have.inner_low, have.map_in)
        mean = seen(have.sums)[:, :1] * (1.0 / CD)
        zero = have.root * (grad_normed - have.cond_zero * have.root * mean) + have.grad_cond
        code = jnp.stack([have.chosen // 32, have.chosen % 32], axis=1).astype(LOW)
        code = jnp.pad(code, ((0, 0), (0, 126)))
        sent = (
            have.scales_low, have.inner_low, have.feats_low, code,
            zero.astype(LOW), have.normed, have.cond_low,
        )
        rows_run.begin(links.gather_rows(jnp.concatenate(sent, axis=1)[None]))

    def grad_map():
        all_rows = rows_run.finish()
        all_rows = all_rows.reshape(-1, all_rows.shape[2])
        starts = [0]
        for size in (3 * D, CD, FOUR, 128, part, part, part):
            starts.append(starts[-1] + size)
        scales_all, inner_all, feats_all, code_all, zero_all, normed_all, cond_all = (
            all_rows[:, a:b] for a, b in zip(starts[:-1], starts[1:])
        )
        first = (own_place % 8) * map_rows
        pick = jnp.arange(part)[:, None] == first + jnp.arange(map_rows)[None, :]
        pick = pick.astype(LOW)
        zero_own = dot_f32(zero_all, pick).astype(LOW)
        normed_own = dot_f32(normed_all, pick).astype(LOW)
        cond_own = dot_f32(cond_all, pick).astype(LOW)
        code_all = code_all.astype(jnp.int32)
        chosen_all = code_all[:, 0] * 32 + code_all[:, 1]
        onehot_all = (chosen_all[:, None] == jnp.arange(CLASSES)[None, :]).astype(LOW)
        have.table_grad = dot_tn(onehot_all, zero_own)
        have.mapping_grad = jnp.concatenate(
            [
                dot_tn(zero_own, feats_all),
                dot_tn(normed_own, inner_all),
                dot_tn(cond_own, scales_all),
            ],
            axis=1,
        )

    for runs, works, held in (
        ((g_p, g_m), (run_names,), ()),
        ((g_p, g_m), (), ()),
        ((g_p, g_m), (), ()),
        ((g_p,), (run_cond,), ()),
        ((), (run_inner, run_patch), ()),
        ((), (run_scales,), ()),
        ((), (run_map,), ()),
        ((), (run_in,), ()),
        ((), (run_mix,), ()),
        ((), (run_out,), ()),
        ((), (run_up,), ()),
        ((), (run_down,), ()),
        ((), (run_loss,), ()),
        ((), (grad_down,), ()),
        ((s_s,), (back_down,), ()),
        ((s_s,), (grad_up,), ()),
        ((s_s, s_e), (back_up, back_out), ()),
        ((s_e, s_s), (back_mix, grad_in), ()),
        ((s_e, s_a), (back_in, back_map, grad_patch), (s_s,)),
        ((s_a, s_p), (back_scales,), (s_e,)),
        ((s_e, s_a, s_p), (back_cond,), ()),
        ((s_a, s_p, rows_run), (), (s_e,)),
        ((s_p, rows_run), (), (s_a,)),
        ((rows_run,), (), (s_p,)),
        ((s_a, s_p, s_e, s_s), (grad_map,), ()),
    ):
        rounds(runs, works, held)
    patch_grads = s_p.finish()
    attn_grads = s_a.finish()
    up_grad = s_e.finish().reshape(-1, ff_tiles, 2, TILE).transpose(0, 2, 1, 3)
    grads = (
        attn_grads[:, : 3 * width].reshape(inward.shape),
        attn_grads[:, 3 * width :].T,
        up_grad.reshape(expand.shape),
        s_s.finish().T,
        jnp.stack([patch_grads[:, :D], patch_grads[:, D:]]),
        have.table_grad,
        have.mapping_grad,
    )
    squares = sum((jnp.sum(grad * grad) for grad in grads))
    local_loss = jnp.sum(weight * have.squared[:, 0]) / (SEQ * PD)
    sums = links.total(jnp.stack([local_loss, squares]))
    sums = sums + rounds.token[0, :2]
    total_loss = sums[0]
    grad_norm = jnp.sqrt(sums[1])
    factor = CLIP / (grad_norm + NORM_EPS)
    count = step_count[0].astype(F32)
    fix_one = 1.0 - jnp.power(BETA_ONE, count)
    fix_two = 1.0 - jnp.power(BETA_TWO, count)
    results = [total_loss, grad_norm]
    for master, first, second, grad in zip(masters, firsts, seconds, grads):
        clipped = grad * factor
        moment = BETA_ONE * first + (1.0 - BETA_ONE) * clipped
        square = BETA_TWO * second + (1.0 - BETA_TWO) * clipped * clipped
        step_size = moment / fix_one / (jnp.sqrt(square / fix_two) + ADAM_EPS)
        results.extend([master - LEARN_RATE * (step_size + DECAY * master), moment, square])
    return tuple(results)


def solution(mesh):
    in_specs = (
        P(("dp", "tensor"), None, None),
        P(("dp", "tensor"), None, None),
        P(("dp", "tensor")),
        P(("dp", "tensor")),
        P(("dp", "tensor")),
        P(("dp", "tensor")),
        P(),
        P("dp", None, "tensor"),
        P("dp", None, "tensor"),
        P("dp", None, "tensor"),
        P("tensor", "dp"),
        P("tensor", "dp"),
        P("tensor", "dp"),
        P("dp", None, "tensor"),
        P("dp", None, "tensor"),
        P("dp", None, "tensor"),
        P("tensor", "dp"),
        P("tensor", "dp"),
        P("tensor", "dp"),
        P(None, ("dp", "tensor"), None),
        P(None, ("dp", "tensor"), None),
        P(None, ("dp", "tensor"), None),
        P(None, ("dp", "tensor")),
        P(None, ("dp", "tensor")),
        P(None, ("dp", "tensor")),
        P(("dp", "tensor"), None),
        P(("dp", "tensor"), None),
        P(("dp", "tensor"), None),
    )
    out_specs = (
        P(),
        P(),
        P("dp", None, "tensor"),
        P("dp", None, "tensor"),
        P("dp", None, "tensor"),
        P("tensor", "dp"),
        P("tensor", "dp"),
        P("tensor", "dp"),
        P("dp", None, "tensor"),
        P("dp", None, "tensor"),
        P("dp", None, "tensor"),
        P("tensor", "dp"),
        P("tensor", "dp"),
        P("tensor", "dp"),
        P(None, ("dp", "tensor"), None),
        P(None, ("dp", "tensor"), None),
        P(None, ("dp", "tensor"), None),
        P(None, ("dp", "tensor")),
        P(None, ("dp", "tensor")),
        P(None, ("dp", "tensor")),
        P(("dp", "tensor"), None),
        P(("dp", "tensor"), None),
        P(("dp", "tensor"), None),
    )
    return jax.shard_map(body, mesh=mesh, in_specs=in_specs, out_specs=out_specs, check_vma=False)
```

time: 1680 us -> 586 us (0.35)
  waiting for transfers between devices: 1360 us -> 239 us
  Pallas kernels: 0 us -> 138 us
  matrix products: 143 us -> 16.8 us
  starting transfers between devices: 2.17 us -> 80.9 us
  blocking collectives: 40.2 us -> 0 us
  other arithmetic: 62.7 us -> 35.5 us
    reduce_scatter x11 -> x0, waiting for transfers between devices: 892 us -> none  [the longest x4 176 us: pair_sum(): return lax.psum_scatter(value, 'tensor', scatter_dimension=0, tiled=True)]
    all_gather x11 -> x1, waiting for transfers between devices: 466 us -> 82.4 us  [body(): block = lax.all_gather(flat, ('tensor', 'dp'), axis=0, tiled=True)]
    ppermute x0 -> x88, waiting for transfers between devices: none -> 156 us  [the longest x75 115 us: swap(): return lax.ppermute(value, 'dp', [(i, i ^ mask) for i in range(self.size)])]
    pallas_call x0 -> x27, Pallas kernels: none -> 138 us  [the longest x3 28.9 us: weight_grads(): pl.pallas_call(kernel, grid=(columns // TILE,), in_specs=[whole(from_own....]
    dot_general x33 -> x18, matrix products: 143 us -> 16.8 us  [the longest x8 8.57 us: dot_tn(): lax.dot_general(left, right, (((0,), (0,)), ((), ())), preferred_element_...]
    ppermute x0 -> x88, starting transfers between devices: none -> 80.9 us  [the longest x75 65.1 us: swap(): return lax.ppermute(value, 'dp', [(i, i ^ mask) for i in range(self.size)])]
    psum x1 -> x0, blocking collectives: 40.2 us -> none  [body(): total_loss = lax.psum(local_loss, ('dp', 'tensor'))]
    convert_element_type x12 -> x7, other arithmetic: 21.4 us -> 4.39 us  [the longest x1 1.76 us: order_matrix(): return (jnp.arange(size)[:, None] == order[None, :]).astype(LOW)]
  transfers between devices with their start and end apart: 22 -> 89, of which waited for: 22 -> 34; matrix products, arithmetic and copies ran while one was open for 8% -> 7% of each run, Pallas kernels for 0% -> 16%
where the time goes in v2:
time: 586 us; the launch traced here: 580 us
  waiting for transfers between devices  239 us (41%)
  Pallas kernels  138 us (24%)
  starting transfers between devices  80.9 us (14%)
  local copies, waits for them, and re-layouts  46.6 us (8%)
  other arithmetic  35.5 us (6%)
  between operations  24.1 us (4%)
  matrix products  16.8 us (3%)
    ppermute x75, waiting for transfers between devices, swap(): return lax.ppermute(value, 'dp', [(i, i ^ mask) for i in range(self.size)])  115 us
    all_gather x1, waiting for transfers between devices, body(): block = lax.all_gather(flat, ('tensor', 'dp'), axis=0, tiled=True)  82.4 us
    ppermute x75, starting transfers between devices, swap(): return lax.ppermute(value, 'dp', [(i, i ^ mask) for i in range(self.size)])  65.1 us
    ppermute x13, waiting for transfers between devices, flip_pair(): return lax.ppermute(value, 'tensor', [(0, 1), (1, 0)])  41.7 us
    unnamed x265, local copies, waits for them, and re-layouts  38.1 us
    pallas_call x3, Pallas kernels, weight_grads(): pl.pallas_call(kernel, grid=(columns // TILE,), in_specs=[whole(from_own....  28.9 us
    pallas_call x12, Pallas kernels, simple(): pl.pallas_call(kernel, grid=(columns // width,), in_specs=[spec(width) fo...  24.8 us
    pallas_call x2, Pallas kernels, cols_backward(): pl.pallas_call(kernel, grid=(steps,), in_specs=[both_spec(rows, width), w...  17.6 us
  transfers between devices with their start and end apart: 89, of which 34 were waited for; matrix products, arithmetic and copies ran while one was open for 7% of the time, Pallas kernels for 16%

profile of v2, /device:TPU:0, one launch (start us, length us, event | category | flops | bytes accessed | tf_op | source)
XLA Modules:
  0.0 580.3 jit_solution(3478742721581105185)
XLA Ops:
  12.9 5.1 collective-permute-start.2
  31.5 10.5 %collective-permute-done = s32[2,2]{0,1:T(2,128)S(1)} collective-permute-done((s32[2,2]{0,1:T(2,128)S(1)}, s32[2,2]{0,1:T(2,128)S(1)}, u32[]{:S(2)}, u32[]{:S(2)}) %collective-permute-start) | collective-permute-done | bytes 48 | tf_op jit(solution)/shard_map/ppermute | solution.py:216
  45.7 10.6 %collective-permute-done.9 = bf16[48,5120]{1,0:T(8,128)(2,1)S(1)} collective-permute-done((bf16[48,5120]{1,0:T(8,128)(2,1)S(1)}, bf16[48,5120]{1,0:T(8,128)(2,1)S(1)}, u32[]{:S(2)}, u32[]{:S(2)}) %collective-permute-start.9) | collective-permute-done | bytes 491552 | tf_op jit(solution)/shard_map/ppermute | solution.py:228
  56.3 12.7 %collective-permute-done.8.first_ref.refs_2_ = bf16[96,2048]{1,0:T(8,128)(2,1)S(1)} collective-permute-done((bf16[96,2048]{1,0:T(8,128)(2,1)S(1)}, bf16[96,2048]{1,0:T(8,128)(2,1)S(1)}, u32[]{:S(2)}, u32[]{:S(2)}) %collective-permute-start.8) | collective-permute-done | bytes 393248 | tf_op jit(solution)/shard_map/ppermute | solution.py:228
  72.3 9.1 %collective-permute-done.14.refs_3_ = bf16[48,2048]{1,0:T(8,128)(2,1)S(1)} collective-permute-done((bf16[48,2048]{1,0:T(8,128)(2,1)S(1)}, bf16[48,2048]{1,0:T(8,128)(2,1)S(1)}, u32[]{:S(2)}, u32[]{:S(2)}) %collective-permute-start.14) | collective-permute-done | bytes 196640 | tf_op jit(solution)/shard_map/ppermute | solution.py:216
  107.3 82.4 %all-gather.2.cloned.1.call-done = bf16[2048,6656]{1,0:T(8,128)(2,1)} async-done(((bf16[64,6656]{1,0:T(8,128)(2,1)}), bf16[2048,6656]{1,0:T(8,128)(2,1)}) %all-gather.2.cloned.1.call-update) | async-done | bytes 27262992 | tf_op jit(solution)/shard_map/all_gather | solution.py:789
  190.9 5.8 %shard_map.472.q_ref.k_ref.v_ref = bf16[2,512,1536]{2,1,0:T(8,128)(2,1)S(1)} custom-call(bf16[512,1024]{1,0:T(8,128)(2,1)S(1)} %copy-done.21, bf16[2,1024,6656]{2,1,0:T(8,128)(2,1)} %bitcast.256), custom_call_target="tpu_custom_call" | custom-call | flops 1 | bytes 1 | tf_op jit(solution)/shard_map/pallas_call | solution.py:385
  196.8 10.0 %shard_map.473.value_ref.refs_5_ = bf16[2,512,512]{2,1,0:T(8,128)(2,1)S(1)} custom-call(bf16[2,512,1536]{2,1,0:T(8,128)(2,1)S(1)} %shard_map.472.q_ref.k_ref.v_ref, bf16[2,512,1536]{2,1,0:T(8,128)(2,1)S(1)} %shard_map.472.q_ref.k_ref.v_ref, bf16[2,512,1536]{2,1,0:T(8,128)(2,1)S(1)} %shard_map.472.q_ref.k_ref.v_ref), custom_call_target="tpu_custom_call" | custom-call | flops 1 | bytes 1 | tf_op jit(solution)/shard_map/pallas_call | solution.py:635
  210.3 10.8 %shard_map.475 = (bf16[2,512,3072]{2,1,0:T(8,128)(2,1)S(1)}, bf16[2,512,1536]{2,1,0:T(8,128)(2,1)S(1)}) custom-call(bf16[512,1024]{1,0:T(8,128)(2,1)S(1)} %get-tuple-element.329.x_ref.refs_2_, bf16[2,1024,6656]{2,1,0:T(8,128)(2,1)} %bitcast.258), custom_call_target="tpu_custom_call" | custom-call | flops 1 | bytes 1 | tf_op jit(solution)/shard_map/pallas_call | solution.py:407
  223.8 8.3 %shard_map.476 = (f32[512,1024]{1,0:T(8,128)S(1)}, bf16[512,1024]{1,0:T(8,128)(2,1)S(1)}) custom-call(bf16[2,512,1536]{2,1,0:T(8,128)(2,1)S(1)} %get-tuple-element.333.value_ref.refs_3_, f32[512,1024]{1,0:T(8,128)S(1)} %get-tuple-element.334.resid_ref, f32[2,1024]{1,0:T(2,128)S(1)} %get-tuple-element.693.scale_ref, bf16[2,1024,6656]{2,1,0:T(8,128)(2,1)} %bitcast.259), custom_call_target="tpu_custom_call" | custom-call | flops 1 | bytes 1 | tf_op jit(solution)/shard_map/pallas_call | solution.py:491
  238.2 6.6 %shard_map.479 = (bf16[2,512,1536]{2,1,0:T(8,128)(2,1)S(1)}, bf16[256,1536]{1,0:T(8,128)(2,1)}, bf16[256,1536]{1,0:T(8,128)(2,1)}, bf16[256,1536]{1,0:T(8,128)(2,1)}, bf16[256,1536]{1,0:T(8,128)(2,1)}) custom-call(bf16[1024,1024]{1,0:T(8,128)(2,1)S(1)} %copy-done.12, s32[1]{0:T(128)} %bitcast.54.refs_1_, ...), custom_call_target="tpu_custom_call" | custom-call | flops 1 | bytes 1 | tf_op jit(solution)/shard_map/pallas_call | solution.py:591
  248.7 9.8 %shard_map.478.value_ref.refs_3_ = bf16[2,512,3072]{2,1,0:T(8,128)(2,1)S(1)} custom-call(bf16[512,1024]{1,0:T(8,128)(2,1)S(1)} %get-tuple-element.348.x_ref.refs_2_, bf16[2,512,3072]{2,1,0:T(8,128)(2,1)S(1)} %copy-done.28, bf16[2,1024,6656]{2,1,0:T(8,128)(2,1)} %bitcast.260), custom_call_target="tpu_custom_call" | custom-call | flops 1 | bytes 1 | tf_op jit(solution)/shard_map/pallas_call | solution.py:444
  263.6 12.8 %shard_map.483 = (bf16[2,512,3072]{2,1,0:T(8,128)(2,1)}, bf16[256,3072]{1,0:T(8,128)(2,1)}, bf16[256,3072]{1,0:T(8,128)(2,1)S(1)}, bf16[256,3072]{1,0:T(8,128)(2,1)}, bf16[256,3072]{1,0:T(8,128)(2,1)}) custom-call(bf16[1024,1024]{1,0:T(8,128)(2,1)S(1)} %copy-done.12, s32[1]{0:T(128)} %bitcast.54.refs_1_, ...), custom_call_target="tpu_custom_call" | custom-call | flops 1 | bytes 1 | tf_op jit(solution)/shard_map/pallas_call | solution.py:591
  298.2 10.8 %shard_map.480 = (f32[2,1024]{1,0:T(2,128)S(1)}, f32[512,1024]{1,0:T(8,128)S(1)}, bf16[512,1024]{1,0:T(8,128)(2,1)S(1)}) custom-call(bf16[2,512,3072]{2,1,0:T(8,128)(2,1)S(1)} %copy-done.5, f32[512,1024]{1,0:T(8,128)S(1)} %copy-done.24, f32[2,1024]{1,0:T(2,128)S(1)} %get-tuple-element.694.scale_ref, f32[512,1024]{1,0:T(8,128)S(1)} %copy-done.33, ...), custom_call_target="tpu_custom_call" | custom-call | flops 1 | bytes 1 | tf_op jit(solution)/shard_map/pallas_call | solution.py:537
  309.0 4.0 shard_map.481.grad_ref
  313.6 3.7 shard_map.486
  324.3 10.8 %shard_map.485.refs_4_.value_ref = bf16[2,512,1536]{2,1,0:T(8,128)(2,1)S(1)} custom-call(bf16[2,512,1536]{2,1,0:T(8,128)(2,1)S(1)} %shard_map.472.q_ref.k_ref.v_ref, bf16[2,512,1536]{2,1,0:T(8,128)(2,1)S(1)} %shard_map.472.q_ref.k_ref.v_ref, bf16[2,512,1536]{2,1,0:T(8,128)(2,1)S(1)} %shard_map.472.q_ref.k_ref.v_ref, bf16[2,512,512]{2,1,0:T(8,128)(2,1)S(1)} %shard_map.481.grad_ref), custom_call_target="tpu_custom_call" | custom-call | flops 1 | bytes 1 | tf_op jit(solution)/shard_map/pallas_call | solution.py:665
  341.5 9.5 %shard_map.487 = (bf16[2,512,2048]{2,1,0:T(8,128)(2,1)}, bf16[256,2048]{1,0:T(8,128)(2,1)}, bf16[256,2048]{1,0:T(8,128)(2,1)S(1)}, bf16[256,2048]{1,0:T(8,128)(2,1)S(1)}, bf16[256,2048]{1,0:T(8,128)(2,1)}) custom-call(bf16[1024,1024]{1,0:T(8,128)(2,1)S(1)} %copy-done.13, s32[1]{0:T(128)} %bitcast.54.refs_1_, bf16[512,1024]{1,0:T(8,128)(2,1)S(1)} %copy-done.22, ...), custom_call_target="tpu_custom_call" | custom-call | flops 1 | bytes 1 | tf_op jit(solution)/shard_map/pallas_call | solution.py:591
  354.9 4.1 collective-permute-done.41
  359.0 5.2 collective-permute-done.42
  364.9 5.7 shard_map.490
  372.6 6.9 %shard_map.489 = (f32[2,1024]{1,0:T(2,128)S(1)}, bf16[512,1024]{1,0:T(8,128)(2,1)S(1)}) custom-call(bf16[2,512,1536]{2,1,0:T(8,128)(2,1)S(1)} %copy-done.16, f32[512,1024]{1,0:T(8,128)S(1)} %copy-done.11, f32[2,1024]{1,0:T(2,128)S(1)} %get-tuple-element.695.scale_ref, f32[512,1024]{1,0:T(8,128)S(1)} %copy-done.35, bf16[2,1024,6656]{2,1,0:T(8,128)(2,1)} %bitcast.263), custom_call_target="tpu_custom_call" | custom-call | flops 1 | bytes 1 | tf_op jit(solution)/shard_map/pallas_call | solution.py:537
  385.9 3.8 collective-permute-done.43
  391.3 15.2 %collective-permute-done.48.refs_2_ = bf16[256,3072]{1,0:T(8,128)(2,1)S(1)} collective-permute-done((bf16[256,3072]{1,0:T(8,128)(2,1)}, bf16[256,3072]{1,0:T(8,128)(2,1)S(1)}, u32[]{:S(2)}, u32[]{:S(2)}) %collective-permute-start.48) | collective-permute-done | bytes 1572896 | tf_op jit(solution)/shard_map/ppermute | solution.py:228
  424.3 5.3 collective-permute-done.57.x_ref
  434.2 3.8 shard_map.494
  442.7 19.2 %collective-permute-done.65.x_ref = bf16[48,2048]{1,0:T(8,128)(2,1)S(1)} collective-permute-done((bf16[48,2048]{1,0:T(8,128)(2,1)S(1)}, bf16[48,2048]{1,0:T(8,128)(2,1)S(1)}, u32[]{:S(2)}, u32[]{:S(2)}) %collective-permute-start.65) | collective-permute-done | bytes 196640 | tf_op jit(solution)/shard_map/ppermute | solution.py:216
  468.0 5.4 collective-permute-done.70
  473.3 7.3 %collective-permute-done.71 = bf16[64,3072]{1,0:T(8,128)(2,1)} collective-permute-done((bf16[64,3072]{1,0:T(8,128)(2,1)}, bf16[64,3072]{1,0:T(8,128)(2,1)}, u32[]{:S(2)}, u32[]{:S(2)}) %collective-permute-start.71) | collective-permute-done | bytes 393248 | tf_op jit(solution)/shard_map/ppermute | solution.py:216
  495.0 14.3 %collective-permute-done.75 = bf16[64,2048]{1,0:T(8,128)(2,1)S(1)} collective-permute-done((bf16[64,2048]{1,0:T(8,128)(2,1)S(1)}, bf16[64,2048]{1,0:T(8,128)(2,1)S(1)}, u32[]{:S(2)}, u32[]{:S(2)}) %collective-permute-start.75) | collective-permute-done | bytes 262176 | tf_op jit(solution)/shard_map/ppermute | solution.py:216
  545.5 3.5 collective-permute-done.86
  549.1 4.4 collective-permute-done.87
  (601 shorter events, 218.8 us)
Async XLA Ops:
  7.2 182.5 %all-gather.2.cloned.1.call-start = ((), (), s32[]{:S(2)}) async-start(), calls=%async_computation | async-start | bytes 28114944 | tf_op jit(solution)/shard_map/all_gather | solution.py:789
  18.2 23.8 %collective-permute-start.5 = (bf16[24,2048]{1,0:T(8,128)(2,1)S(1)}, bf16[24,2048]{1,0:T(8,128)(2,1)S(1)}, u32[]{:S(2)}, u32[]{:S(2)}) collective-permute-start(bf16[24,2048]{1,0:T(8,128)(2,1)S(1)} %pad_maximum_fusion.12), channel_id=1, source_target_pairs={{0,24},{2,26},{4,28},{6,30},{8,16},{10,18},{12,20},{14,22},{16,8},... | collective-permute-start | bytes 294920 | tf_op jit(solution)/shard_map/ppermute | solution.py:216
  19.1 22.9 %collective-permute-start.4 = (bf16[24,2048]{1,0:T(8,128)(2,1)S(1)}, bf16[24,2048]{1,0:T(8,128)(2,1)S(1)}, u32[]{:S(2)}, u32[]{:S(2)}) collective-permute-start(bf16[24,2048]{1,0:T(8,128)(2,1)S(1)} %pad_maximum_fusion.12), channel_id=1, source_target_pairs={{0,8},{2,10},{4,12},{6,14},{8,0},{10,2},{12,4},{14,6},{16,24},{18,... | collective-permute-start | bytes 294920 | tf_op jit(solution)/shard_map/ppermute | solution.py:216
  43.6 25.4 %collective-permute-start.8 = (bf16[96,2048]{1,0:T(8,128)(2,1)S(1)}, bf16[96,2048]{1,0:T(8,128)(2,1)S(1)}, u32[]{:S(2)}, u32[]{:S(2)}) collective-permute-start(bf16[96,2048]{1,0:T(8,128)(2,1)S(1)} %constant_dynamic-update-slice_fusion.refs_0_), channel_id=1, source_target_pairs={{0,1},{1,0},{2,3},{3,2},{4,5},{5,4},{6,7},{7,6},{8,9},{9,8},{10,11... | collective-permute-start | bytes 1179656 | tf_op jit(solution)/shard_map/ppermute | solution.py:228
  44.2 24.8 %collective-permute-start.7 = (bf16[96,2048]{1,0:T(8,128)(2,1)S(1)}, bf16[96,2048]{1,0:T(8,128)(2,1)S(1)}, u32[]{:S(2)}, u32[]{:S(2)}) collective-permute-start(bf16[96,2048]{1,0:T(8,128)(2,1)S(1)} %constant_dynamic-update-slice_fusion.refs_0_), channel_id=1, source_target_pairs={{0,4},{2,6},{4,0},{6,2},{8,12},{10,14},{12,8},{14,10},{16,20},{18,... | collective-permute-start | bytes 1179656 | tf_op jit(solution)/shard_map/ppermute | solution.py:216
  245.2 31.3 %collective-permute-start.30 = (bf16[256,1536]{1,0:T(8,128)(2,1)}, bf16[256,1536]{1,0:T(8,128)(2,1)}, u32[]{:S(2)}, u32[]{:S(2)}) collective-permute-start(bf16[256,1536]{1,0:T(8,128)(2,1)} %get-tuple-element.366), channel_id=1, source_target_pairs={{0,2},{2,0},{4,6},{6,4},{8,10},{10,8},{12,14},{14,12},{16,18},{18,... | collective-permute-start | bytes 2359304 | tf_op jit(solution)/shard_map/ppermute | solution.py:216
  245.4 31.0 %collective-permute-start.31 = (bf16[256,1536]{1,0:T(8,128)(2,1)}, bf16[256,1536]{1,0:T(8,128)(2,1)}, u32[]{:S(2)}, u32[]{:S(2)}) collective-permute-start(bf16[256,1536]{1,0:T(8,128)(2,1)} %get-tuple-element.367), channel_id=1, source_target_pairs={{0,2},{2,0},{4,6},{6,4},{8,10},{10,8},{12,14},{14,12},{16,18},{18,... | collective-permute-start | bytes 2359304 | tf_op jit(solution)/shard_map/ppermute | solution.py:216
  263.6 24.1 %collective-permute-start.33 = (bf16[256,1536]{1,0:T(8,128)(2,1)}, bf16[256,1536]{1,0:T(8,128)(2,1)}, u32[]{:S(2)}, u32[]{:S(2)}) collective-permute-start(bf16[256,1536]{1,0:T(8,128)(2,1)} %get-tuple-element.374), channel_id=1, source_target_pairs={{0,2},{2,0},{4,6},{6,4},{8,10},{10,8},{12,14},{14,12},{16,18},{18,... | collective-permute-start | bytes 2359304 | tf_op jit(solution)/shard_map/ppermute | solution.py:216
  278.3 34.7 %collective-permute-start.32 = (bf16[256,3072]{1,0:T(8,128)(2,1)}, bf16[256,3072]{1,0:T(8,128)(2,1)}, u32[]{:S(2)}, u32[]{:S(2)}) collective-permute-start(bf16[256,3072]{1,0:T(8,128)(2,1)} %get-tuple-element.373), channel_id=1, source_target_pairs={{0,2},{2,0},{4,6},{6,4},{8,10},{10,8},{12,14},{14,12},{16,18},{18,... | collective-permute-start | bytes 4718600 | tf_op jit(solution)/shard_map/ppermute | solution.py:216
  278.8 43.9 %collective-permute-start.38 = (bf16[256,3072]{1,0:T(8,128)(2,1)}, bf16[256,3072]{1,0:T(8,128)(2,1)}, u32[]{:S(2)}, u32[]{:S(2)}) collective-permute-start(bf16[256,3072]{1,0:T(8,128)(2,1)} %get-tuple-element.387), channel_id=1, source_target_pairs={{0,2},{2,0},{4,6},{6,4},{8,10},{10,8},{12,14},{14,12},{16,18},{18,... | collective-permute-start | bytes 4718600 | tf_op jit(solution)/shard_map/ppermute | solution.py:216
  279.5 72.4 %collective-permute-start.39 = (bf16[256,3072]{1,0:T(8,128)(2,1)}, bf16[256,3072]{1,0:T(8,128)(2,1)}, u32[]{:S(2)}, u32[]{:S(2)}) collective-permute-start(bf16[256,3072]{1,0:T(8,128)(2,1)} %copy-done.50), channel_id=1, source_target_pairs={{0,2},{2,0},{4,6},{6,4},{8,10},{10,8},{12,14},{14,12},{16,18},{18,... | collective-permute-start | bytes 4718600 | tf_op jit(solution)/shard_map/ppermute | solution.py:216
  286.2 26.8 %collective-permute-start.34 = (bf16[256,1536]{1,0:T(8,128)(2,1)}, bf16[256,1536]{1,0:T(8,128)(2,1)}, u32[]{:S(2)}, u32[]{:S(2)}) collective-permute-start(bf16[256,1536]{1,0:T(8,128)(2,1)} %get-tuple-element.379), channel_id=1, source_target_pairs={{0,1},{1,0},{2,3},{3,2},{4,5},{5,4},{6,7},{7,6},{8,9},{9,8},{10,11... | collective-permute-start | bytes 2359304 | tf_op jit(solution)/shard_map/ppermute | solution.py:228
  287.7 25.4 %collective-permute-start.35 = (bf16[256,1536]{1,0:T(8,128)(2,1)}, bf16[256,1536]{1,0:T(8,128)(2,1)}, u32[]{:S(2)}, u32[]{:S(2)}) collective-permute-start(bf16[256,1536]{1,0:T(8,128)(2,1)} %get-tuple-element.380), channel_id=1, source_target_pairs={{0,4},{2,6},{4,0},{6,2},{8,12},{10,14},{12,8},{14,10},{16,20},{18,... | collective-permute-start | bytes 2359304 | tf_op jit(solution)/shard_map/ppermute | solution.py:216
  317.3 46.9 %collective-permute-start.36 = (bf16[128,3072]{1,0:T(8,128)(2,1)}, bf16[128,3072]{1,0:T(8,128)(2,1)}, u32[]{:S(2)}, u32[]{:S(2)}) collective-permute-start(bf16[128,3072]{1,0:T(8,128)(2,1)} %get-tuple-element.385), channel_id=1, source_target_pairs={{0,4},{2,6},{4,0},{6,2},{8,12},{10,14},{12,8},{14,10},{16,20},{18,... | collective-permute-start | bytes 2359304 | tf_op jit(solution)/shard_map/ppermute | solution.py:216
  318.7 45.5 %collective-permute-start.37 = (bf16[128,3072]{1,0:T(8,128)(2,1)S(1)}, bf16[128,3072]{1,0:T(8,128)(2,1)}, u32[]{:S(2)}, u32[]{:S(2)}) collective-permute-start(bf16[128,3072]{1,0:T(8,128)(2,1)S(1)} %get-tuple-element.386), channel_id=1, source_target_pairs={{0,1},{1,0},{2,3},{3,2},{4,5},{5,4},{6,7},{7,6},{8,9},{9,8},{10,11... | collective-permute-start | bytes 2359304 | tf_op jit(solution)/shard_map/ppermute | solution.py:228
  320.2 61.8 %collective-permute-start.47 = (bf16[256,3072]{1,0:T(8,128)(2,1)}, bf16[256,3072]{1,0:T(8,128)(2,1)}, u32[]{:S(2)}, u32[]{:S(2)}) collective-permute-start(bf16[256,3072]{1,0:T(8,128)(2,1)} %get-tuple-element.412), channel_id=1, source_target_pairs={{0,2},{2,0},{4,6},{6,4},{8,10},{10,8},{12,14},{14,12},{16,18},{18,... | collective-permute-start | bytes 4718600 | tf_op jit(solution)/shard_map/ppermute | solution.py:216
  322.7 29.7 %collective-permute-start.40 = (bf16[64,1536]{1,0:T(8,128)(2,1)S(1)}, bf16[64,1536]{1,0:T(8,128)(2,1)S(1)}, u32[]{:S(2)}, u32[]{:S(2)}) collective-permute-start(bf16[64,1536]{1,0:T(8,128)(2,1)S(1)} %get-tuple-element.400), channel_id=1, source_target_pairs={{0,16},{2,18},{4,20},{6,22},{8,24},{10,26},{12,28},{14,30},{16,0},... | collective-permute-start | bytes 589832 | tf_op jit(solution)/shard_map/ppermute | solution.py:216
  370.6 35.9 %collective-permute-start.48 = (bf16[256,3072]{1,0:T(8,128)(2,1)}, bf16[256,3072]{1,0:T(8,128)(2,1)S(1)}, u32[]{:S(2)}, u32[]{:S(2)}) collective-permute-start(bf16[256,3072]{1,0:T(8,128)(2,1)} %get-tuple-element.417), channel_id=1, source_target_pairs={{0,1},{1,0},{2,3},{3,2},{4,5},{5,4},{6,7},{7,6},{8,9},{9,8},{10,11... | collective-permute-start | bytes 4718600 | tf_op jit(solution)/shard_map/ppermute | solution.py:228
  372.0 35.6 %collective-permute-start.49 = (bf16[256,3072]{1,0:T(8,128)(2,1)}, bf16[256,3072]{1,0:T(8,128)(2,1)S(1)}, u32[]{:S(2)}, u32[]{:S(2)}) collective-permute-start(bf16[256,3072]{1,0:T(8,128)(2,1)} %get-tuple-element.418), channel_id=1, source_target_pairs={{0,4},{2,6},{4,0},{6,2},{8,12},{10,14},{12,8},{14,10},{16,20},{18,... | collective-permute-start | bytes 4718600 | tf_op jit(solution)/shard_map/ppermute | solution.py:216
  385.9 27.9 %collective-permute-start.59 = (bf16[256,2048]{1,0:T(8,128)(2,1)S(1)}, bf16[256,2048]{1,0:T(8,128)(2,1)S(1)}, u32[]{:S(2)}, u32[]{:S(2)}) collective-permute-start(bf16[256,2048]{1,0:T(8,128)(2,1)S(1)} %copy-done.52), channel_id=1, source_target_pairs={{0,2},{2,0},{4,6},{6,4},{8,10},{10,8},{12,14},{14,12},{16,18},{18,... | collective-permute-start | bytes 3145736 | tf_op jit(solution)/shard_map/ppermute | solution.py:216
  389.7 25.6 %collective-permute-start.60 = (bf16[256,2048]{1,0:T(8,128)(2,1)S(1)}, bf16[256,2048]{1,0:T(8,128)(2,1)S(1)}, u32[]{:S(2)}, u32[]{:S(2)}) collective-permute-start(bf16[256,2048]{1,0:T(8,128)(2,1)S(1)} %get-tuple-element.435), channel_id=1, source_target_pairs={{0,2},{2,0},{4,6},{6,4},{8,10},{10,8},{12,14},{14,12},{16,18},{18,... | collective-permute-start | bytes 3145736 | tf_op jit(solution)/shard_map/ppermute | solution.py:216
  423.8 18.4 %collective-permute-start.68 = (bf16[96,2048]{1,0:T(8,128)(2,1)}, bf16[96,2048]{1,0:T(8,128)(2,1)}, u32[]{:S(2)}, u32[]{:S(2)}) collective-permute-start(bf16[96,2048]{1,0:T(8,128)(2,1)} %pad_maximum_fusion.5), channel_id=1, source_target_pairs={{0,2},{2,0},{4,6},{6,4},{8,10},{10,8},{12,14},{14,12},{16,18},{18,... | collective-permute-start | bytes 1179656 | tf_op jit(solution)/shard_map/ppermute | solution.py:216
  432.0 48.7 %collective-permute-start.63 = (bf16[256,2048]{1,0:T(8,128)(2,1)}, bf16[256,2048]{1,0:T(8,128)(2,1)}, u32[]{:S(2)}, u32[]{:S(2)}) collective-permute-start(bf16[256,2048]{1,0:T(8,128)(2,1)} %get-tuple-element.447), channel_id=1, source_target_pairs={{0,1},{1,0},{2,3},{3,2},{4,5},{5,4},{6,7},{7,6},{8,9},{9,8},{10,11... | collective-permute-start | bytes 3145736 | tf_op jit(solution)/shard_map/ppermute | solution.py:228
  433.4 47.3 %collective-permute-start.64 = (bf16[256,2048]{1,0:T(8,128)(2,1)}, bf16[256,2048]{1,0:T(8,128)(2,1)}, u32[]{:S(2)}, u32[]{:S(2)}) collective-permute-start(bf16[256,2048]{1,0:T(8,128)(2,1)} %get-tuple-element.448), channel_id=1, source_target_pairs={{0,4},{2,6},{4,0},{6,2},{8,12},{10,14},{12,8},{14,10},{16,20},{18,... | collective-permute-start | bytes 3145736 | tf_op jit(solution)/shard_map/ppermute | solution.py:216
  438.9 26.2 %collective-permute-start.69 = (bf16[64,3072]{1,0:T(8,128)(2,1)}, bf16[64,3072]{1,0:T(8,128)(2,1)}, u32[]{:S(2)}, u32[]{:S(2)}) collective-permute-start(bf16[64,3072]{1,0:T(8,128)(2,1)} %copy-done.56), channel_id=1, source_target_pairs={{0,16},{2,18},{4,20},{6,22},{8,24},{10,26},{12,28},{14,30},{16,0},... | collective-permute-start | bytes 1179656 | tf_op jit(solution)/shard_map/ppermute | solution.py:216
  440.6 21.3 %collective-permute-start.65 = (bf16[48,2048]{1,0:T(8,128)(2,1)S(1)}, bf16[48,2048]{1,0:T(8,128)(2,1)S(1)}, u32[]{:S(2)}, u32[]{:S(2)}) collective-permute-start(bf16[48,2048]{1,0:T(8,128)(2,1)S(1)} %get-tuple-element.450), channel_id=1, source_target_pairs={{0,4},{2,6},{4,0},{6,2},{8,12},{10,14},{12,8},{14,10},{16,20},{18,... | collective-permute-start | bytes 589832 | tf_op jit(solution)/shard_map/ppermute | solution.py:216
  442.2 19.8 %collective-permute-start.66 = (bf16[48,2048]{1,0:T(8,128)(2,1)S(1)}, bf16[48,2048]{1,0:T(8,128)(2,1)S(1)}, u32[]{:S(2)}, u32[]{:S(2)}) collective-permute-start(bf16[48,2048]{1,0:T(8,128)(2,1)S(1)} %get-tuple-element.451), channel_id=1, source_target_pairs={{0,1},{1,0},{2,3},{3,2},{4,5},{5,4},{6,7},{7,6},{8,9},{9,8},{10,11... | collective-permute-start | bytes 589832 | tf_op jit(solution)/shard_map/ppermute | solution.py:228
  462.7 18.0 %collective-permute-start.71 = (bf16[64,3072]{1,0:T(8,128)(2,1)}, bf16[64,3072]{1,0:T(8,128)(2,1)}, u32[]{:S(2)}, u32[]{:S(2)}) collective-permute-start(bf16[64,3072]{1,0:T(8,128)(2,1)} %get-tuple-element.472), channel_id=1, source_target_pairs={{0,24},{2,26},{4,28},{6,30},{8,16},{10,18},{12,20},{14,22},{16,8},... | collective-permute-start | bytes 1179656 | tf_op jit(solution)/shard_map/ppermute | solution.py:216
  465.1 27.2 %collective-permute-start.50 = (bf16[96,2048]{1,0:T(8,128)(2,1)}, bf16[96,2048]{1,0:T(8,128)(2,1)}, u32[]{:S(2)}, u32[]{:S(2)}) collective-permute-start(bf16[96,2048]{1,0:T(8,128)(2,1)} %pad_maximum_fusion.4), channel_id=1, source_target_pairs={{0,2},{2,0},{4,6},{6,4},{8,10},{10,8},{12,14},{14,12},{16,18},{18,... | collective-permute-start | bytes 1179656 | tf_op jit(solution)/shard_map/ppermute | solution.py:216
  485.8 23.6 %collective-permute-start.72 = (bf16[96,2048]{1,0:T(8,128)(2,1)S(1)}, bf16[96,2048]{1,0:T(8,128)(2,1)S(1)}, u32[]{:S(2)}, u32[]{:S(2)}) collective-permute-start(bf16[96,2048]{1,0:T(8,128)(2,1)S(1)} %get-tuple-element.478), channel_id=1, source_target_pairs={{0,1},{1,0},{2,3},{3,2},{4,5},{5,4},{6,7},{7,6},{8,9},{9,8},{10,11... | collective-permute-start | bytes 1179656 | tf_op jit(solution)/shard_map/ppermute | solution.py:228
  487.1 22.2 %collective-permute-start.73 = (bf16[96,2048]{1,0:T(8,128)(2,1)S(1)}, bf16[96,2048]{1,0:T(8,128)(2,1)S(1)}, u32[]{:S(2)}, u32[]{:S(2)}) collective-permute-start(bf16[96,2048]{1,0:T(8,128)(2,1)S(1)} %get-tuple-element.479), channel_id=1, source_target_pairs={{0,4},{2,6},{4,0},{6,2},{8,12},{10,14},{12,8},{14,10},{16,20},{18,... | collective-permute-start | bytes 1179656 | tf_op jit(solution)/shard_map/ppermute | solution.py:216
  489.7 19.6 %collective-permute-start.75 = (bf16[64,2048]{1,0:T(8,128)(2,1)S(1)}, bf16[64,2048]{1,0:T(8,128)(2,1)S(1)}, u32[]{:S(2)}, u32[]{:S(2)}) collective-permute-start(bf16[64,2048]{1,0:T(8,128)(2,1)S(1)} %get-tuple-element.486), channel_id=1, source_target_pairs={{0,16},{2,18},{4,20},{6,22},{8,24},{10,26},{12,28},{14,30},{16,0},... | collective-permute-start | bytes 786440 | tf_op jit(solution)/shard_map/ppermute | solution.py:216
  (185 other events, 1345.0 us)
Sparse Core Ops, SparseCore 0:
  13.0 176.7 all-gather.1

commit v3 on v2

--- a/solution.py
+++ b/solution.py
@@ -81,7 +81,7 @@
             work()
 
 
-def params(vmem=40):
+def params(vmem=50):
     return pltpu.CompilerParams(vmem_limit_bytes=vmem * MIB)
 
 
@@ -249,11 +249,12 @@
         pieces = list(pieces)
         return pieces + [self.flip(piece, 0) for piece in pieces]
 
-    def gather_rows(self, value):
-        for bit in (1, None, 0):
+    def gather_rows(self, value, *groups):
+        for group in groups:
             (value,) = yield (value,)
-            other = self.flip_pair(value) if bit is None else self.flip(value, bit)
-            value = jnp.concatenate([value, other], axis=0)
+            for bit in group:
+                other = self.flip_pair(value) if bit is None else self.flip(value, bit)
+                value = jnp.concatenate([value, other], axis=0)
         return value
 
 
@@ -273,7 +274,7 @@
         order = [i ^ index for i in range(value.shape[0])]
         return jnp.concatenate([value[i : i + 1] for i in order], axis=0)
 
-    def reduce(self, own, *others):
+    def reduce(self, groups, own, *others):
         others = yield others
         corner, side, across, kept = (self.flip(others[i], 0) for i in (3, 2, 1, 0))
         (corner,) = yield (corner,)
@@ -286,7 +287,11 @@
         if self.far():
             terms = yield terms
             kept, *sent = add_parts(4, *terms)
-            terms = (kept, *(self.swap(part, mask) for part, mask in zip(sent, self.far())))
+            terms = [kept]
+            for group in groups:
+                terms = [*terms] + [self.swap(sent[i], self.far()[i]) for i in group]
+                if group != groups[-1]:
+                    terms = yield tuple(terms)
         else:
             for bit in reversed(self.upper):
                 terms = yield terms
@@ -295,10 +300,18 @@
         terms = yield terms
         return sum(term.astype(F32) for term in terms)
 
+    def swap_corner(self, value):
+        pairs = [(2 * i + j, 2 * (i ^ 2) + (j ^ 1)) for i in range(self.size) for j in range(2)]
+        return lax.ppermute(value, ("dp", "tensor"), pairs)
+
     def total(self, value):
         value = value + self.flip(value, 0)
-        value = value + self.flip_pair(value)
-        for bit in [1] + self.upper[::-1]:
+        by_x, by_pair, corner = self.flip(value, 1), self.flip_pair(value), self.swap_corner(value)
+        value = (value + by_pair) + (by_x + corner)
+        if self.far():
+            first, second, both = (self.swap(value, mask) for mask in self.far())
+            return (value + first) + (second + both)
+        for bit in reversed(self.upper):
             value = value + self.flip(value, bit)
         return value
 
@@ -312,7 +325,8 @@
     def begin(self, steps):
         self.steps, self.waiting = steps, next(steps)
 
-    def go_on(self, values):
+    def go_on(self, values=None):
+        values = self.waiting if values is None else values
         assert self.result is None
         try:
             self.waiting = self.steps.send(values)
@@ -602,6 +616,31 @@
         compiler_params=params(),
         cost_estimate=cost(),
     )(from_own, first, *(x for x, _ in pairs), *(value for _, value in pairs))
+
+
+def patch_weight_grads(*pairs):
+    depth, columns = pairs[0][0].shape[1], pairs[0][1].shape[1]
+    size = depth // 8
+
+    def kernel(*refs):
+        lefts, rights = refs[: len(pairs)], refs[len(pairs) : 2 * len(pairs)]
+        own_ref, *parts = refs[2 * len(pairs) :]
+        for i in range(len(pairs)):
+            grad = dot_tn(lefts[i][...], rights[i][...]).astype(LOW)
+            span = slice(i * columns, (i + 1) * columns)
+            own_ref[0, :, span] = grad[: 2 * size]
+            own_ref[1, :, span] = grad[2 * size : 4 * size]
+            for j, part in enumerate(parts):
+                part[:, span] = grad[(4 + j) * size : (5 + j) * size]
+
+    width = len(pairs) * columns
+    return pl.pallas_call(
+        kernel,
+        out_shape=[jax.ShapeDtypeStruct((2, 2 * size, width), LOW)]
+        + [jax.ShapeDtypeStruct((size, width), LOW)] * 4,
+        compiler_params=params(),
+        cost_estimate=cost(),
+    )(*(left for left, _ in pairs), *(right for _, right in pairs))
 
 
 def head_part(ref, part):
@@ -792,7 +831,7 @@
     at_in = 3 * ff_tiles
     at_out = at_in + 3 * width // TILE
     g_p = Run(links.gather(flat_patch))
-    g_m = Run(links.gather_rows(flat_map))
+    g_m = Run(links.gather_rows(flat_map, (1,), (None,), (0,)))
     s_p, s_a, s_e, s_s, rows_run = (Run() for _ in range(5))
     line = links.size // 4
     part = 8 * map_rows
@@ -915,14 +954,8 @@
             have.last, have.patch_all[:, D:], target, coef, have.resid_two, have.scales[:, 2]
         )
 
-    def start(run, parts):
-        run.begin(links.reduce(*parts))
-
-    def patch_grad(left, right):
-        half, part = PD // 2, PD // 8
-        own = dot_tn(left[:, :half], right).astype(LOW).reshape(2, half // 2, D)
-        other = dot_tn(left[:, half:], right).astype(LOW)
-        return [own] + [other[i * part : (i + 1) * part] for i in range(4)]
+    def start(run, parts, groups=((0, 1, 2),)):
+        run.begin(links.reduce(groups, *parts))
 
     def grad_down():
         start(s_s, weight_grads(from_own, this_pair, (have.rows_two, have.hidden)))
@@ -931,7 +964,8 @@
         have.gated_grad = shrink_backward(have.rows_two, block, at_down, have.gated)
 
     def grad_up():
-        start(s_e, weight_grads(from_own, this_pair, (have.rows_one, have.gated_grad)))
+        parts = weight_grads(from_own, this_pair, (have.rows_one, have.gated_grad))
+        start(s_e, parts, ((0,), (1, 2)))
 
     def back_up():
         have.scale_one, have.grad_one, have.rows_grad = cols_backward(
@@ -961,8 +995,8 @@
         )
 
     def grad_patch():
-        parts = zip(patch_grad(inputs, have.grad_zero), patch_grad(have.grad_low, have.last))
-        start(s_p, [jnp.concatenate(part, axis=-1) for part in parts])
+        pairs = ((inputs, have.grad_zero), (have.grad_low, have.last))
+        start(s_p, patch_weight_grads(*pairs))
 
     def back_map():
         grad_scales = jnp.stack([have.scale_zero, have.scale_one, have.scale_two], axis=1)
@@ -994,7 +1028,7 @@
             have.scales_low, have.inner_low, have.feats_low, code,
             zero.astype(LOW), have.normed, have.cond_low,
         )
-        rows_run.begin(links.gather_rows(jnp.concatenate(sent, axis=1)[None]))
+        rows_run.begin(links.gather_rows(jnp.concatenate(sent, axis=1)[None], (0, 1), (None,)))
 
     def grad_map():
         all_rows = rows_run.finish()
@@ -1024,6 +1058,12 @@
             axis=1,
         )
 
+    def more_p():
+        s_p.go_on()
+
+    def more_r():
+        rows_run.go_on()
+
     for runs, works, held in (
         ((g_p, g_m), (run_names,), ()),
         ((g_p, g_m), (), ()),
@@ -1042,13 +1082,12 @@
         ((s_s,), (back_down,), ()),
         ((s_s,), (grad_up,), ()),
         ((s_s, s_e), (back_up, back_out), ()),
-        ((s_e, s_s), (back_mix, grad_in), ()),
-        ((s_e, s_a), (back_in, back_map, grad_patch), (s_s,)),
-        ((s_a, s_p), (back_scales,), (s_e,)),
-        ((s_e, s_a, s_p), (back_cond,), ()),
-        ((s_a, s_p, rows_run), (), (s_e,)),
-        ((s_p, rows_run), (), (s_a,)),
-        ((rows_run,), (), (s_p,)),
+        ((s_e,), (back_mix, grad_in), ()),
+        ((s_e, s_a, s_s), (back_in, back_map, grad_patch), ()),
+        ((s_a, s_p, s_e), (back_scales, more_p), (s_s,)),
+        ((s_a, s_e, s_p), (), ()),
+        ((s_a, s_p), (back_cond, more_r), (s_e,)),
+        ((rows_run,), (), ()),
         ((s_a, s_p, s_e, s_s), (grad_map,), ()),
     ):
         rounds(runs, works, held)

time: 586 us -> 567 us (0.968)
  Pallas kernels: 138 us -> 169 us
  waiting for transfers between devices: 239 us -> 208 us
  local copies, waits for them, and re-layouts: 46.6 us -> 26 us
  starting transfers between devices: 80.9 us -> 87.5 us
    ppermute x75 -> x76, waiting for transfers between devices: 115 us -> 90.3 us  [swap(): return lax.ppermute(value, 'dp', [(i, i ^ mask) for i in range(self.size)])]
    unnamed x265 -> x263, local copies, waits for them, and re-layouts: 38.1 us -> 16 us
    dot_general x8 -> x4, matrix products: 8.57 us -> 2.31 us  [dot_tn(): lax.dot_general(left, right, (((0,), (0,)), ((), ())), preferred_element_...]
    ppermute x75 -> x76, starting transfers between devices: 65.1 us -> 70.5 us  [swap(): return lax.ppermute(value, 'dp', [(i, i ^ mask) for i in range(self.size)])]
  transfers between devices with their start and end apart: 89 -> 91, of which waited for: 34 -> 29; matrix products, arithmetic and copies ran while one was open for 7% -> 6% of each run, Pallas kernels for 16% -> 20%
where the time goes in v3:
time: 567 us; the launch traced here: 561 us
  waiting for transfers between devices  208 us (37%)
  Pallas kernels  169 us (30%)
  starting transfers between devices  87.5 us (15%)
  other arithmetic  35 us (6%)
  local copies, waits for them, and re-layouts  26 us (5%)
  between operations  24.3 us (4%)
  matrix products  11.7 us (2%)
    ppermute x76, waiting for transfers between devices, swap(): return lax.ppermute(value, 'dp', [(i, i ^ mask) for i in range(self.size)])  90.3 us
    all_gather x1, waiting for transfers between devices, body(): block = lax.all_gather(flat, ('tensor', 'dp'), axis=0, tiled=True)  79.8 us
    ppermute x76, starting transfers between devices, swap(): return lax.ppermute(value, 'dp', [(i, i ^ mask) for i in range(self.size)])  70.5 us
    ppermute x13, waiting for transfers between devices, flip_pair(): return lax.ppermute(value, 'tensor', [(0, 1), (1, 0)])  36.5 us
    pallas_call x3, Pallas kernels, weight_grads(): pl.pallas_call(kernel, grid=(columns // TILE,), in_specs=[whole(from_own....  34.5 us
    pallas_call x12, Pallas kernels, simple(): pl.pallas_call(kernel, grid=(columns // width,), in_specs=[spec(width) fo...  29 us
    pallas_call x2, Pallas kernels, cols_backward(): pl.pallas_call(kernel, grid=(steps,), in_specs=[both_spec(rows, width), w...  20.9 us
    unnamed x263, local copies, waits for them, and re-layouts  16 us
  transfers between devices with their start and end apart: 91, of which 29 were waited for; matrix products, arithmetic and copies ran while one was open for 6% of the time, Pallas kernels for 20%

profile of v3, /device:TPU:0, one launch (start us, length us, event | category | flops | bytes accessed | tf_op | source)
XLA Modules:
  0.0 560.8 jit_solution(14428511618440754416)
XLA Ops:
  13.0 5.1 collective-permute-start.2
  31.5 10.5 %collective-permute-done = s32[2,2]{0,1:T(2,128)S(1)} collective-permute-done((s32[2,2]{0,1:T(2,128)S(1)}, s32[2,2]{0,1:T(2,128)S(1)}, u32[]{:S(2)}, u32[]{:S(2)}) %collective-permute-start) | collective-permute-done | bytes 48 | tf_op jit(solution)/shard_map/ppermute | solution.py:216
  45.7 10.6 %collective-permute-done.9 = bf16[48,5120]{1,0:T(8,128)(2,1)S(1)} collective-permute-done((bf16[48,5120]{1,0:T(8,128)(2,1)S(1)}, bf16[48,5120]{1,0:T(8,128)(2,1)S(1)}, u32[]{:S(2)}, u32[]{:S(2)}) %collective-permute-start.9) | collective-permute-done | bytes 491552 | tf_op jit(solution)/shard_map/ppermute | solution.py:228
  56.3 12.7 %collective-permute-done.8.first_ref.refs_2_ = bf16[96,2048]{1,0:T(8,128)(2,1)S(1)} collective-permute-done((bf16[96,2048]{1,0:T(8,128)(2,1)S(1)}, bf16[96,2048]{1,0:T(8,128)(2,1)S(1)}, u32[]{:S(2)}, u32[]{:S(2)}) %collective-permute-start.8) | collective-permute-done | bytes 393248 | tf_op jit(solution)/shard_map/ppermute | solution.py:228
  72.3 9.1 %collective-permute-done.14.refs_3_ = bf16[48,2048]{1,0:T(8,128)(2,1)S(1)} collective-permute-done((bf16[48,2048]{1,0:T(8,128)(2,1)S(1)}, bf16[48,2048]{1,0:T(8,128)(2,1)S(1)}, u32[]{:S(2)}, u32[]{:S(2)}) %collective-permute-start.14) | collective-permute-done | bytes 196640 | tf_op jit(solution)/shard_map/ppermute | solution.py:216
  109.5 79.8 %all-gather.2.cloned.1.call-done = bf16[2048,6656]{1,0:T(8,128)(2,1)} async-done(((bf16[64,6656]{1,0:T(8,128)(2,1)}), bf16[2048,6656]{1,0:T(8,128)(2,1)}) %all-gather.2.cloned.1.call-update) | async-done | bytes 27262992 | tf_op jit(solution)/shard_map/all_gather | solution.py:828
  189.3 7.1 %shard_map.472.q_ref.k_ref.v_ref = bf16[2,512,1536]{2,1,0:T(8,128)(2,1)} custom-call(bf16[512,1024]{1,0:T(8,128)(2,1)S(1)} %fusion.3.x_ref.refs_2_, bf16[2,1024,6656]{2,1,0:T(8,128)(2,1)} %bitcast.249), custom_call_target="tpu_custom_call" | custom-call | flops 1 | bytes 1 | tf_op jit(solution)/shard_map/pallas_call | solution.py:399
  196.4 10.5 %shard_map.473.value_ref.refs_5_ = bf16[2,512,512]{2,1,0:T(8,128)(2,1)S(1)} custom-call(bf16[2,512,1536]{2,1,0:T(8,128)(2,1)} %shard_map.472.q_ref.k_ref.v_ref, bf16[2,512,1536]{2,1,0:T(8,128)(2,1)} %shard_map.472.q_ref.k_ref.v_ref, bf16[2,512,1536]{2,1,0:T(8,128)(2,1)} %shard_map.472.q_ref.k_ref.v_ref), custom_call_target="tpu_custom_call" | custom-call | flops 1 | bytes 1 | tf_op jit(solution)/shard_map/pallas_call | solution.py:674
  207.0 5.2 shard_map.474
  212.2 12.0 %shard_map.475 = (bf16[2,512,3072]{2,1,0:T(8,128)(2,1)}, bf16[2,512,1536]{2,1,0:T(8,128)(2,1)}) custom-call(bf16[512,1024]{1,0:T(8,128)(2,1)S(1)} %get-tuple-element.320.x_ref.refs_2_, bf16[2,1024,6656]{2,1,0:T(8,128)(2,1)} %bitcast.251), custom_call_target="tpu_custom_call" | custom-call | flops 1 | bytes 1 | tf_op jit(solution)/shard_map/pallas_call | solution.py:421
  224.2 8.1 %shard_map.476 = (f32[512,1024]{1,0:T(8,128)S(1)}, bf16[512,1024]{1,0:T(8,128)(2,1)S(1)}) custom-call(bf16[2,512,1536]{2,1,0:T(8,128)(2,1)} %get-tuple-element.324.value_ref.refs_3_, f32[512,1024]{1,0:T(8,128)} %get-tuple-element.325.resid_ref, f32[2,1024]{1,0:T(2,128)S(1)} %get-tuple-element.667.scale_ref, bf16[2,1024,6656]{2,1,0:T(8,128)(2,1)} %bitcast.252), custom_call_target="tpu_custom_call" | custom-call | flops 1 | bytes 1 | tf_op jit(solution)/shard_map/pallas_call | solution.py:505
  233.8 6.6 %shard_map.477 = (f32[2,128]{1,0:T(2,128)S(1)}, bf16[512,768]{1,0:T(8,128)(2,1)S(1)}, f32[512,1024]{1,0:T(8,128)}, bf16[512,1024]{1,0:T(8,128)(2,1)S(1)}, f32[2,1024]{1,0:T(2,128)S(1)}) custom-call(bf16[512,1024]{1,0:T(8,128)(2,1)S(1)} %get-tuple-element.329.last_ref.refs_3_, bf16[768,1024]{1,0:T(8,128)(2,1)} %slice.631.out_ref, ...), custom_call_target="tpu_custom_call" | custom-call | flops 1 | bytes 1 | tf_op jit(solution)/shard_map/pallas_call | solution.py:736
  241.3 8.8 %shard_map.479 = (bf16[2,512,1536]{2,1,0:T(8,128)(2,1)}, bf16[256,1536]{1,0:T(8,128)(2,1)S(1)}, bf16[256,1536]{1,0:T(8,128)(2,1)S(1)}, bf16[256,1536]{1,0:T(8,128)(2,1)S(1)}, bf16[256,1536]{1,0:T(8,128)(2,1)S(1)}) custom-call(bf16[1024,1024]{1,0:T(8,128)(2,1)} %fusion.refs_0_, s32[1]{0:T(128)} %bitcast.53.refs_1_, bf16[512,1024]{1,0:T(8,128)(2,1)} %copy-done.8, ...), custom_call_target="tpu_custom_call" | custom-call | flops 1 | bytes 1 | tf_op jit(solution)/shard_map/pallas_call | solution.py:605
  250.9 11.6 %shard_map.478.value_ref.refs_3_ = bf16[2,512,3072]{2,1,0:T(8,128)(2,1)} custom-call(bf16[512,1024]{1,0:T(8,128)(2,1)S(1)} %copy-done.9, bf16[2,512,3072]{2,1,0:T(8,128)(2,1)} %get-tuple-element.341.gated_ref, bf16[2,1024,6656]{2,1,0:T(8,128)(2,1)} %bitcast.253), custom_call_target="tpu_custom_call" | custom-call | flops 1 | bytes 1 | tf_op jit(solution)/shard_map/pallas_call | solution.py:458
  265.8 13.6 %shard_map.483 = (bf16[2,512,3072]{2,1,0:T(8,128)(2,1)}, bf16[256,3072]{1,0:T(8,128)(2,1)S(1)}, bf16[256,3072]{1,0:T(8,128)(2,1)}, bf16[256,3072]{1,0:T(8,128)(2,1)}, bf16[256,3072]{1,0:T(8,128)(2,1)}) custom-call(bf16[1024,1024]{1,0:T(8,128)(2,1)} %fusion.refs_0_, s32[1]{0:T(128)} %bitcast.53.refs_1_, ...), custom_call_target="tpu_custom_call" | custom-call | flops 1 | bytes 1 | tf_op jit(solution)/shard_map/pallas_call | solution.py:605
  285.8 12.8 %shard_map.480 = (f32[2,1024]{1,0:T(2,128)S(1)}, f32[512,1024]{1,0:T(8,128)S(1)}, bf16[512,1024]{1,0:T(8,128)(2,1)S(1)}) custom-call(bf16[2,512,3072]{2,1,0:T(8,128)(2,1)} %shard_map.478.value_ref.refs_3_, f32[512,1024]{1,0:T(8,128)} %get-tuple-element.325.resid_ref, f32[2,1024]{1,0:T(2,128)S(1)} %get-tuple-element.668.scale_ref, ...), custom_call_target="tpu_custom_call" | custom-call | flops 1 | bytes 1 | tf_op jit(solution)/shard_map/pallas_call | solution.py:551
  298.6 4.0 shard_map.481.grad_ref
  308.2 12.7 %shard_map.484.refs_4_.value_ref = bf16[2,512,1536]{2,1,0:T(8,128)(2,1)} custom-call(bf16[2,512,1536]{2,1,0:T(8,128)(2,1)} %shard_map.472.q_ref.k_ref.v_ref, bf16[2,512,1536]{2,1,0:T(8,128)(2,1)} %shard_map.472.q_ref.k_ref.v_ref, bf16[2,512,1536]{2,1,0:T(8,128)(2,1)} %shard_map.472.q_ref.k_ref.v_ref, bf16[2,512,512]{2,1,0:T(8,128)(2,1)S(1)} %shard_map.481.grad_ref), custom_call_target="tpu_custom_call" | custom-call | flops 1 | bytes 1 | tf_op jit(solution)/shard_map/pallas_call | solution.py:704
  320.9 12.1 %shard_map.485 = (bf16[2,512,2048]{2,1,0:T(8,128)(2,1)}, bf16[256,2048]{1,0:T(8,128)(2,1)S(1)}, bf16[256,2048]{1,0:T(8,128)(2,1)S(1)}, bf16[256,2048]{1,0:T(8,128)(2,1)S(1)}, bf16[256,2048]{1,0:T(8,128)(2,1)}) custom-call(bf16[1024,1024]{1,0:T(8,128)(2,1)} %fusion.refs_0_, s32[1]{0:T(128)} %bitcast.53.refs_1_, bf16[512,1024]{1,0:T(8,128)(2,1)} %copy-done.6, ...), custom_call_target="tpu_custom_call" | custom-call | flops 1 | bytes 1 | tf_op jit(solution)/shard_map/pallas_call | solution.py:605
  335.0 5.5 shard_map.490
  346.5 8.1 %shard_map.488 = (f32[2,1024]{1,0:T(2,128)S(1)}, bf16[512,1024]{1,0:T(8,128)(2,1)S(1)}) custom-call(bf16[2,512,1536]{2,1,0:T(8,128)(2,1)} %shard_map.484.refs_4_.value_ref, f32[512,1024]{1,0:T(8,128)S(1)} %copy-done.3, f32[2,1024]{1,0:T(2,128)S(1)} %get-tuple-element.669.scale_ref, f32[512,1024]{1,0:T(8,128)} %copy-done.11, bf16[2,1024,6656]{2,1,0:T(8,128)(2,1)} %bitcast.256), custom_call_target="tpu_custom_call" | custom-call | flops 1 | bytes 1 | tf_op jit(solution)/shard_map/pallas_call | solution.py:551
  356.4 4.8 collective-permute-done.43
  361.2 3.7 collective-permute-done.42
  364.9 4.6 collective-permute-done.41
  370.9 7.1 %collective-permute-done.49 = bf16[64,1536]{1,0:T(8,128)(2,1)S(1)} collective-permute-done((bf16[64,1536]{1,0:T(8,128)(2,1)S(1)}, bf16[64,1536]{1,0:T(8,128)(2,1)S(1)}, u32[]{:S(2)}, u32[]{:S(2)}) %collective-permute-start.49) | collective-permute-done | bytes 196640 | tf_op jit(solution)/shard_map/ppermute | solution.py:216
  378.6 4.5 shard_map.489
  400.4 4.4 shard_map.493
  412.8 13.1 %collective-permute-done.61 = bf16[64,3072]{1,0:T(8,128)(2,1)} collective-permute-done((bf16[64,3072]{1,0:T(8,128)(2,1)}, bf16[64,3072]{1,0:T(8,128)(2,1)}, u32[]{:S(2)}, u32[]{:S(2)}) %collective-permute-start.61) | collective-permute-done | bytes 393248 | tf_op jit(solution)/shard_map/ppermute | solution.py:216
  446.0 8.6 %collective-permute-done.73 = bf16[64,3072]{1,0:T(8,128)(2,1)S(1)} collective-permute-done((bf16[64,3072]{1,0:T(8,128)(2,1)S(1)}, bf16[64,3072]{1,0:T(8,128)(2,1)S(1)}, u32[]{:S(2)}, u32[]{:S(2)}) %collective-permute-start.73) | collective-permute-done | bytes 393248 | tf_op jit(solution)/shard_map/ppermute | solution.py:216
  455.4 12.1 %collective-permute-done.70 = bf16[96,2048]{1,0:T(8,128)(2,1)S(1)} collective-permute-done((bf16[96,2048]{1,0:T(8,128)(2,1)S(1)}, bf16[96,2048]{1,0:T(8,128)(2,1)S(1)}, u32[]{:S(2)}, u32[]{:S(2)}) %collective-permute-start.70) | collective-permute-done | bytes 393248 | tf_op jit(solution)/shard_map/ppermute | solution.py:228
  484.9 10.9 %collective-permute-done.78 = bf16[24,2048]{1,0:T(8,128)(2,1)S(1)} collective-permute-done((bf16[24,2048]{1,0:T(8,128)(2,1)S(1)}, bf16[24,2048]{1,0:T(8,128)(2,1)S(1)}, u32[]{:S(2)}, u32[]{:S(2)}) %collective-permute-start.78) | collective-permute-done | bytes 98336 | tf_op jit(solution)/shard_map/ppermute | solution.py:216
  497.0 8.2 %collective-permute-done.77 = bf16[24,2048]{1,0:T(8,128)(2,1)S(1)} collective-permute-done((bf16[24,2048]{1,0:T(8,128)(2,1)S(1)}, bf16[24,2048]{1,0:T(8,128)(2,1)S(1)}, u32[]{:S(2)}, u32[]{:S(2)}) %collective-permute-start.77) | collective-permute-done | bytes 98336 | tf_op jit(solution)/shard_map/ppermute | solution.py:216
  (590 shorter events, 188.0 us)
Async XLA Ops:
  7.2 182.1 %all-gather.2.cloned.1.call-start = ((), (), s32[]{:S(2)}) async-start(), calls=%async_computation | async-start | bytes 28114944 | tf_op jit(solution)/shard_map/all_gather | solution.py:828
  18.2 23.8 %collective-permute-start.5 = (bf16[24,2048]{1,0:T(8,128)(2,1)S(1)}, bf16[24,2048]{1,0:T(8,128)(2,1)S(1)}, u32[]{:S(2)}, u32[]{:S(2)}) collective-permute-start(bf16[24,2048]{1,0:T(8,128)(2,1)S(1)} %pad_maximum_fusion.7), channel_id=1, source_target_pairs={{0,24},{2,26},{4,28},{6,30},{8,16},{10,18},{12,20},{14,22},{16,8},... | collective-permute-start | bytes 294920 | tf_op jit(solution)/shard_map/ppermute | solution.py:216
  19.2 22.8 %collective-permute-start.4 = (bf16[24,2048]{1,0:T(8,128)(2,1)S(1)}, bf16[24,2048]{1,0:T(8,128)(2,1)S(1)}, u32[]{:S(2)}, u32[]{:S(2)}) collective-permute-start(bf16[24,2048]{1,0:T(8,128)(2,1)S(1)} %pad_maximum_fusion.7), channel_id=1, source_target_pairs={{0,8},{2,10},{4,12},{6,14},{8,0},{10,2},{12,4},{14,6},{16,24},{18,... | collective-permute-start | bytes 294920 | tf_op jit(solution)/shard_map/ppermute | solution.py:216
  43.5 25.4 %collective-permute-start.8 = (bf16[96,2048]{1,0:T(8,128)(2,1)S(1)}, bf16[96,2048]{1,0:T(8,128)(2,1)S(1)}, u32[]{:S(2)}, u32[]{:S(2)}) collective-permute-start(bf16[96,2048]{1,0:T(8,128)(2,1)S(1)} %constant_dynamic-update-slice_fusion.refs_0_), channel_id=1, source_target_pairs={{0,1},{1,0},{2,3},{3,2},{4,5},{5,4},{6,7},{7,6},{8,9},{9,8},{10,11... | collective-permute-start | bytes 1179656 | tf_op jit(solution)/shard_map/ppermute | solution.py:228
  44.2 24.7 %collective-permute-start.7 = (bf16[96,2048]{1,0:T(8,128)(2,1)S(1)}, bf16[96,2048]{1,0:T(8,128)(2,1)S(1)}, u32[]{:S(2)}, u32[]{:S(2)}) collective-permute-start(bf16[96,2048]{1,0:T(8,128)(2,1)S(1)} %constant_dynamic-update-slice_fusion.refs_0_), channel_id=1, source_target_pairs={{0,4},{2,6},{4,0},{6,2},{8,12},{10,14},{12,8},{14,10},{16,20},{18,... | collective-permute-start | bytes 1179656 | tf_op jit(solution)/shard_map/ppermute | solution.py:216
  250.4 29.1 %collective-permute-start.30 = (bf16[256,1536]{1,0:T(8,128)(2,1)S(1)}, bf16[256,1536]{1,0:T(8,128)(2,1)S(1)}, u32[]{:S(2)}, u32[]{:S(2)}) collective-permute-start(bf16[256,1536]{1,0:T(8,128)(2,1)S(1)} %get-tuple-element.358), channel_id=1, source_target_pairs={{0,2},{2,0},{4,6},{6,4},{8,10},{10,8},{12,14},{14,12},{16,18},{18,... | collective-permute-start | bytes 2359304 | tf_op jit(solution)/shard_map/ppermute | solution.py:216
  250.6 28.8 %collective-permute-start.31 = (bf16[256,1536]{1,0:T(8,128)(2,1)S(1)}, bf16[256,1536]{1,0:T(8,128)(2,1)S(1)}, u32[]{:S(2)}, u32[]{:S(2)}) collective-permute-start(bf16[256,1536]{1,0:T(8,128)(2,1)S(1)} %get-tuple-element.359), channel_id=1, source_target_pairs={{0,2},{2,0},{4,6},{6,4},{8,10},{10,8},{12,14},{14,12},{16,18},{18,... | collective-permute-start | bytes 2359304 | tf_op jit(solution)/shard_map/ppermute | solution.py:216
  279.5 26.7 %collective-permute-start.37 = (bf16[256,1536]{1,0:T(8,128)(2,1)S(1)}, bf16[256,1536]{1,0:T(8,128)(2,1)S(1)}, u32[]{:S(2)}, u32[]{:S(2)}) collective-permute-start(bf16[256,1536]{1,0:T(8,128)(2,1)S(1)} %get-tuple-element.380), channel_id=1, source_target_pairs={{0,2},{2,0},{4,6},{6,4},{8,10},{10,8},{12,14},{14,12},{16,18},{18,... | collective-permute-start | bytes 2359304 | tf_op jit(solution)/shard_map/ppermute | solution.py:216
  282.3 24.5 %collective-permute-start.38 = (bf16[256,1536]{1,0:T(8,128)(2,1)}, bf16[256,1536]{1,0:T(8,128)(2,1)S(1)}, u32[]{:S(2)}, u32[]{:S(2)}) collective-permute-start(bf16[256,1536]{1,0:T(8,128)(2,1)} %get-tuple-element.385), channel_id=1, source_target_pairs={{0,1},{1,0},{2,3},{3,2},{4,5},{5,4},{6,7},{7,6},{8,9},{9,8},{10,11... | collective-permute-start | bytes 2359304 | tf_op jit(solution)/shard_map/ppermute | solution.py:228
  283.8 51.3 %collective-permute-start.35 = (bf16[256,3072]{1,0:T(8,128)(2,1)}, bf16[256,3072]{1,0:T(8,128)(2,1)}, u32[]{:S(2)}, u32[]{:S(2)}) collective-permute-start(bf16[256,3072]{1,0:T(8,128)(2,1)} %get-tuple-element.374), channel_id=1, source_target_pairs={{0,2},{2,0},{4,6},{6,4},{8,10},{10,8},{12,14},{14,12},{16,18},{18,... | collective-permute-start | bytes 4718600 | tf_op jit(solution)/shard_map/ppermute | solution.py:216
  283.8 51.3 %collective-permute-start.36 = (bf16[256,3072]{1,0:T(8,128)(2,1)}, bf16[256,3072]{1,0:T(8,128)(2,1)}, u32[]{:S(2)}, u32[]{:S(2)}) collective-permute-start(bf16[256,3072]{1,0:T(8,128)(2,1)} %get-tuple-element.375), channel_id=1, source_target_pairs={{0,2},{2,0},{4,6},{6,4},{8,10},{10,8},{12,14},{14,12},{16,18},{18,... | collective-permute-start | bytes 4718600 | tf_op jit(solution)/shard_map/ppermute | solution.py:216
  284.3 24.0 %collective-permute-start.39 = (bf16[256,1536]{1,0:T(8,128)(2,1)S(1)}, bf16[256,1536]{1,0:T(8,128)(2,1)S(1)}, u32[]{:S(2)}, u32[]{:S(2)}) collective-permute-start(bf16[256,1536]{1,0:T(8,128)(2,1)S(1)} %get-tuple-element.386), channel_id=1, source_target_pairs={{0,4},{2,6},{4,0},{6,2},{8,12},{10,14},{12,8},{14,10},{16,20},{18,... | collective-permute-start | bytes 2359304 | tf_op jit(solution)/shard_map/ppermute | solution.py:216
  306.3 28.8 %collective-permute-start.33 = (bf16[128,3072]{1,0:T(8,128)(2,1)}, bf16[128,3072]{1,0:T(8,128)(2,1)S(1)}, u32[]{:S(2)}, u32[]{:S(2)}) collective-permute-start(bf16[128,3072]{1,0:T(8,128)(2,1)} %get-tuple-element.372), channel_id=1, source_target_pairs={{0,4},{2,6},{4,0},{6,2},{8,12},{10,14},{12,8},{14,10},{16,20},{18,... | collective-permute-start | bytes 2359304 | tf_op jit(solution)/shard_map/ppermute | solution.py:216
  306.8 28.2 %collective-permute-start.34 = (bf16[128,3072]{1,0:T(8,128)(2,1)}, bf16[128,3072]{1,0:T(8,128)(2,1)S(1)}, u32[]{:S(2)}, u32[]{:S(2)}) collective-permute-start(bf16[128,3072]{1,0:T(8,128)(2,1)} %get-tuple-element.373), channel_id=1, source_target_pairs={{0,1},{1,0},{2,3},{3,2},{4,5},{5,4},{6,7},{7,6},{8,9},{9,8},{10,11... | collective-permute-start | bytes 2359304 | tf_op jit(solution)/shard_map/ppermute | solution.py:228
  308.2 47.4 %collective-permute-start.45 = (bf16[256,3072]{1,0:T(8,128)(2,1)S(1)}, bf16[256,3072]{1,0:T(8,128)(2,1)S(1)}, u32[]{:S(2)}, u32[]{:S(2)}) collective-permute-start(bf16[256,3072]{1,0:T(8,128)(2,1)S(1)} %get-tuple-element.401), channel_id=1, source_target_pairs={{0,2},{2,0},{4,6},{6,4},{8,10},{10,8},{12,14},{14,12},{16,18},{18,... | collective-permute-start | bytes 4718600 | tf_op jit(solution)/shard_map/ppermute | solution.py:216
  340.5 42.6 %collective-permute-start.46 = (bf16[256,3072]{1,0:T(8,128)(2,1)}, bf16[256,3072]{1,0:T(8,128)(2,1)}, u32[]{:S(2)}, u32[]{:S(2)}) collective-permute-start(bf16[256,3072]{1,0:T(8,128)(2,1)} %get-tuple-element.406), channel_id=1, source_target_pairs={{0,1},{1,0},{2,3},{3,2},{4,5},{5,4},{6,7},{7,6},{8,9},{9,8},{10,11... | collective-permute-start | bytes 4718600 | tf_op jit(solution)/shard_map/ppermute | solution.py:228
  341.1 42.0 %collective-permute-start.47 = (bf16[256,3072]{1,0:T(8,128)(2,1)}, bf16[256,3072]{1,0:T(8,128)(2,1)}, u32[]{:S(2)}, u32[]{:S(2)}) collective-permute-start(bf16[256,3072]{1,0:T(8,128)(2,1)} %get-tuple-element.407), channel_id=1, source_target_pairs={{0,4},{2,6},{4,0},{6,2},{8,12},{10,14},{12,8},{14,10},{16,20},{18,... | collective-permute-start | bytes 4718600 | tf_op jit(solution)/shard_map/ppermute | solution.py:216
  345.0 24.5 %collective-permute-start.48 = (bf16[64,1536]{1,0:T(8,128)(2,1)S(1)}, bf16[64,1536]{1,0:T(8,128)(2,1)S(1)}, u32[]{:S(2)}, u32[]{:S(2)}) collective-permute-start(bf16[64,1536]{1,0:T(8,128)(2,1)S(1)} %get-tuple-element.413), channel_id=1, source_target_pairs={{0,16},{2,18},{4,20},{6,22},{8,24},{10,26},{12,28},{14,30},{16,0},... | collective-permute-start | bytes 589832 | tf_op jit(solution)/shard_map/ppermute | solution.py:216
  346.4 36.7 %collective-permute-start.44 = (bf16[256,2048]{1,0:T(8,128)(2,1)}, bf16[256,2048]{1,0:T(8,128)(2,1)S(1)}, u32[]{:S(2)}, u32[]{:S(2)}) collective-permute-start(bf16[256,2048]{1,0:T(8,128)(2,1)} %get-tuple-element.395), channel_id=1, source_target_pairs={{0,2},{2,0},{4,6},{6,4},{8,10},{10,8},{12,14},{14,12},{16,18},{18,... | collective-permute-start | bytes 3145736 | tf_op jit(solution)/shard_map/ppermute | solution.py:216
  383.1 22.5 %collective-permute-start.62 = (bf16[96,2048]{1,0:T(8,128)(2,1)}, bf16[96,2048]{1,0:T(8,128)(2,1)}, u32[]{:S(2)}, u32[]{:S(2)}) collective-permute-start(bf16[96,2048]{1,0:T(8,128)(2,1)} %get-tuple-element.434), channel_id=1, source_target_pairs={{0,2},{2,0},{4,6},{6,4},{8,10},{10,8},{12,14},{14,12},{16,18},{18,... | collective-permute-start | bytes 1179656 | tf_op jit(solution)/shard_map/ppermute | solution.py:216
  398.3 27.6 %collective-permute-start.57 = (bf16[128,2048]{1,0:T(8,128)(2,1)}, bf16[128,2048]{1,0:T(8,128)(2,1)}, u32[]{:S(2)}, u32[]{:S(2)}) collective-permute-start(bf16[128,2048]{1,0:T(8,128)(2,1)} %get-tuple-element.423), channel_id=1, source_target_pairs={{0,4},{2,6},{4,0},{6,2},{8,12},{10,14},{12,8},{14,10},{16,20},{18,... | collective-permute-start | bytes 1572872 | tf_op jit(solution)/shard_map/ppermute | solution.py:216
  398.9 27.5 %collective-permute-start.58 = (bf16[128,2048]{1,0:T(8,128)(2,1)}, bf16[128,2048]{1,0:T(8,128)(2,1)}, u32[]{:S(2)}, u32[]{:S(2)}) collective-permute-start(bf16[128,2048]{1,0:T(8,128)(2,1)} %get-tuple-element.424), channel_id=1, source_target_pairs={{0,1},{1,0},{2,3},{3,2},{4,5},{5,4},{6,7},{7,6},{8,9},{9,8},{10,11... | collective-permute-start | bytes 1572872 | tf_op jit(solution)/shard_map/ppermute | solution.py:228
  405.6 20.2 %collective-permute-start.61 = (bf16[64,3072]{1,0:T(8,128)(2,1)}, bf16[64,3072]{1,0:T(8,128)(2,1)}, u32[]{:S(2)}, u32[]{:S(2)}) collective-permute-start(bf16[64,3072]{1,0:T(8,128)(2,1)} %get-tuple-element.432), channel_id=1, source_target_pairs={{0,16},{2,18},{4,20},{6,22},{8,24},{10,26},{12,28},{14,30},{16,0},... | collective-permute-start | bytes 1179656 | tf_op jit(solution)/shard_map/ppermute | solution.py:216
  433.6 35.6 %collective-permute-start.67 = (bf16[256,2048]{1,0:T(8,128)(2,1)}, bf16[256,2048]{1,0:T(8,128)(2,1)}, u32[]{:S(2)}, u32[]{:S(2)}) collective-permute-start(bf16[256,2048]{1,0:T(8,128)(2,1)} %copy-done.24), channel_id=1, source_target_pairs={{0,1},{1,0},{2,3},{3,2},{4,5},{5,4},{6,7},{7,6},{8,9},{9,8},{10,11... | collective-permute-start | bytes 3145736 | tf_op jit(solution)/shard_map/ppermute | solution.py:228
  434.6 34.7 %collective-permute-start.68 = (bf16[256,2048]{1,0:T(8,128)(2,1)}, bf16[256,2048]{1,0:T(8,128)(2,1)}, u32[]{:S(2)}, u32[]{:S(2)}) collective-permute-start(bf16[256,2048]{1,0:T(8,128)(2,1)} %copy-done.23), channel_id=1, source_target_pairs={{0,4},{2,6},{4,0},{6,2},{8,12},{10,14},{12,8},{14,10},{16,20},{18,... | collective-permute-start | bytes 3145736 | tf_op jit(solution)/shard_map/ppermute | solution.py:216
  443.3 24.2 %collective-permute-start.70 = (bf16[96,2048]{1,0:T(8,128)(2,1)S(1)}, bf16[96,2048]{1,0:T(8,128)(2,1)S(1)}, u32[]{:S(2)}, u32[]{:S(2)}) collective-permute-start(bf16[96,2048]{1,0:T(8,128)(2,1)S(1)} %get-tuple-element.451), channel_id=1, source_target_pairs={{0,1},{1,0},{2,3},{3,2},{4,5},{5,4},{6,7},{7,6},{8,9},{9,8},{10,11... | collective-permute-start | bytes 1179656 | tf_op jit(solution)/shard_map/ppermute | solution.py:228
  444.2 25.1 %collective-permute-start.71 = (bf16[96,2048]{1,0:T(8,128)(2,1)S(1)}, bf16[96,2048]{1,0:T(8,128)(2,1)S(1)}, u32[]{:S(2)}, u32[]{:S(2)}) collective-permute-start(bf16[96,2048]{1,0:T(8,128)(2,1)S(1)} %get-tuple-element.452), channel_id=1, source_target_pairs={{0,4},{2,6},{4,0},{6,2},{8,12},{10,14},{12,8},{14,10},{16,20},{18,... | collective-permute-start | bytes 1179656 | tf_op jit(solution)/shard_map/ppermute | solution.py:216
  454.6 27.0 %collective-permute-start.81 = (bf16[2,8,4800]{2,1,0:T(8,128)(2,1)}, bf16[2,8,4800]{2,1,0:T(8,128)(2,1)}, u32[]{:S(2)}, u32[]{:S(2)}) collective-permute-start(bf16[2,8,4800]{2,1,0:T(8,128)(2,1)} %pad_maximum_fusion.6), channel_id=1, source_target_pairs={{0,4},{2,6},{4,0},{6,2},{8,12},{10,14},{12,8},{14,10},{16,20},{18,... | collective-permute-start | bytes 460808 | tf_op jit(solution)/shard_map/ppermute | solution.py:216
  477.2 28.1 %collective-permute-start.74 = (bf16[64,2048]{1,0:T(8,128)(2,1)S(1)}, bf16[64,2048]{1,0:T(8,128)(2,1)S(1)}, u32[]{:S(2)}, u32[]{:S(2)}) collective-permute-start(bf16[64,2048]{1,0:T(8,128)(2,1)S(1)} %get-tuple-element.463), channel_id=1, source_target_pairs={{0,16},{2,18},{4,20},{6,22},{8,24},{10,26},{12,28},{14,30},{16,0},... | collective-permute-start | bytes 786440 | tf_op jit(solution)/shard_map/ppermute | solution.py:216
  478.6 26.7 %collective-permute-start.75 = (bf16[64,2048]{1,0:T(8,128)(2,1)S(1)}, bf16[64,2048]{1,0:T(8,128)(2,1)S(1)}, u32[]{:S(2)}, u32[]{:S(2)}) collective-permute-start(bf16[64,2048]{1,0:T(8,128)(2,1)S(1)} %get-tuple-element.464), channel_id=1, source_target_pairs={{0,8},{2,10},{4,12},{6,14},{8,0},{10,2},{12,4},{14,6},{16,24},{18,... | collective-permute-start | bytes 786440 | tf_op jit(solution)/shard_map/ppermute | solution.py:216
  479.5 25.8 %collective-permute-start.76 = (bf16[64,2048]{1,0:T(8,128)(2,1)S(1)}, bf16[64,2048]{1,0:T(8,128)(2,1)S(1)}, u32[]{:S(2)}, u32[]{:S(2)}) collective-permute-start(bf16[64,2048]{1,0:T(8,128)(2,1)S(1)} %get-tuple-element.465), channel_id=1, source_target_pairs={{0,24},{2,26},{4,28},{6,30},{8,16},{10,18},{12,20},{14,22},{16,8},... | collective-permute-start | bytes 786440 | tf_op jit(solution)/shard_map/ppermute | solution.py:216
  481.9 23.4 %collective-permute-start.77 = (bf16[24,2048]{1,0:T(8,128)(2,1)S(1)}, bf16[24,2048]{1,0:T(8,128)(2,1)S(1)}, u32[]{:S(2)}, u32[]{:S(2)}) collective-permute-start(bf16[24,2048]{1,0:T(8,128)(2,1)S(1)} %copy-done.80), channel_id=1, source_target_pairs={{0,16},{2,18},{4,20},{6,22},{8,24},{10,26},{12,28},{14,30},{16,0},... | collective-permute-start | bytes 294920 | tf_op jit(solution)/shard_map/ppermute | solution.py:216
  (186 other events, 1753.9 us)
Sparse Core Ops, SparseCore 0:
  13.0 176.2 all-gather.1

commit v4 on v3

--- a/solution.py
+++ b/solution.py
@@ -81,7 +81,7 @@
             work()
 
 
-def params(vmem=50):
+def params(vmem=48):
     return pltpu.CompilerParams(vmem_limit_bytes=vmem * MIB)
 
 

time: 567 us -> 559 us (0.986)
  Pallas kernels: 169 us -> 157 us
    unnamed x263 -> x293, local copies, waits for them, and re-layouts: 16 us -> 21.5 us
  transfers between devices with their start and end apart: 91 -> 91, of which waited for: 29 -> 27; matrix products, arithmetic and copies ran while one was open for 6% -> 6% of each run, Pallas kernels for 20% -> 19%
where the time goes in v4:
time: 559 us; the launch traced here: 553 us
  waiting for transfers between devices  208 us (37%)
  Pallas kernels  157 us (28%)
  starting transfers between devices  88 us (16%)
  other arithmetic  32.5 us (6%)
  local copies, waits for them, and re-layouts  31.5 us (6%)
  between operations  24.4 us (4%)
  matrix products  11.8 us (2%)
    ppermute x76, waiting for transfers between devices, swap(): return lax.ppermute(value, 'dp', [(i, i ^ mask) for i in range(self.size)])  90.9 us
    all_gather x1, waiting for transfers between devices, body(): block = lax.all_gather(flat, ('tensor', 'dp'), axis=0, tiled=True)  79.9 us
    ppermute x76, starting transfers between devices, swap(): return lax.ppermute(value, 'dp', [(i, i ^ mask) for i in range(self.size)])  72.1 us
    ppermute x13, waiting for transfers between devices, flip_pair(): return lax.ppermute(value, 'tensor', [(0, 1), (1, 0)])  35.8 us
    pallas_call x3, Pallas kernels, weight_grads(): pl.pallas_call(kernel, grid=(columns // TILE,), in_specs=[whole(from_own....  34.7 us
    pallas_call x12, Pallas kernels, simple(): pl.pallas_call(kernel, grid=(columns // width,), in_specs=[spec(width) fo...  26.3 us
    unnamed x293, local copies, waits for them, and re-layouts  21.5 us
    pallas_call x2, Pallas kernels, cols_backward(): pl.pallas_call(kernel, grid=(steps,), in_specs=[both_spec(rows, width), w...  19.7 us
  transfers between devices with their start and end apart: 91, of which 27 were waited for; matrix products, arithmetic and copies ran while one was open for 6% of the time, Pallas kernels for 19%

profile of v4, /device:TPU:0, one launch (start us, length us, event | category | flops | bytes accessed | tf_op | source)
XLA Modules:
  0.0 553.0 jit_solution(16006977012524821607)
XLA Ops:
  12.9 5.1 collective-permute-start.2
  31.5 10.5 %collective-permute-done = s32[2,2]{0,1:T(2,128)S(1)} collective-permute-done((s32[2,2]{0,1:T(2,128)S(1)}, s32[2,2]{0,1:T(2,128)S(1)}, u32[]{:S(2)}, u32[]{:S(2)}) %collective-permute-start) | collective-permute-done | bytes 48 | tf_op jit(solution)/shard_map/ppermute | solution.py:216
  45.7 10.5 %collective-permute-done.9 = bf16[48,5120]{1,0:T(8,128)(2,1)S(1)} collective-permute-done((bf16[48,5120]{1,0:T(8,128)(2,1)S(1)}, bf16[48,5120]{1,0:T(8,128)(2,1)S(1)}, u32[]{:S(2)}, u32[]{:S(2)}) %collective-permute-start.9) | collective-permute-done | bytes 491552 | tf_op jit(solution)/shard_map/ppermute | solution.py:228
  56.3 12.7 %collective-permute-done.8.first_ref.refs_2_ = bf16[96,2048]{1,0:T(8,128)(2,1)S(1)} collective-permute-done((bf16[96,2048]{1,0:T(8,128)(2,1)S(1)}, bf16[96,2048]{1,0:T(8,128)(2,1)S(1)}, u32[]{:S(2)}, u32[]{:S(2)}) %collective-permute-start.8) | collective-permute-done | bytes 393248 | tf_op jit(solution)/shard_map/ppermute | solution.py:228
  72.3 9.1 %collective-permute-done.14.refs_3_ = bf16[48,2048]{1,0:T(8,128)(2,1)S(1)} collective-permute-done((bf16[48,2048]{1,0:T(8,128)(2,1)S(1)}, bf16[48,2048]{1,0:T(8,128)(2,1)S(1)}, u32[]{:S(2)}, u32[]{:S(2)}) %collective-permute-start.14) | collective-permute-done | bytes 196640 | tf_op jit(solution)/shard_map/ppermute | solution.py:216
  109.6 79.9 %all-gather.2.cloned.1.call-done = bf16[2048,6656]{1,0:T(8,128)(2,1)} async-done(((bf16[64,6656]{1,0:T(8,128)(2,1)}), bf16[2048,6656]{1,0:T(8,128)(2,1)}) %all-gather.2.cloned.1.call-update) | async-done | bytes 27262992 | tf_op jit(solution)/shard_map/all_gather | solution.py:828
  189.5 5.8 %shard_map.472.q_ref.k_ref.v_ref = bf16[2,512,1536]{2,1,0:T(8,128)(2,1)S(1)} custom-call(bf16[512,1024]{1,0:T(8,128)(2,1)S(1)} %fusion.3.x_ref.refs_2_, bf16[2,1024,6656]{2,1,0:T(8,128)(2,1)} %bitcast.249), custom_call_target="tpu_custom_call" | custom-call | flops 1 | bytes 1 | tf_op jit(solution)/shard_map/pallas_call | solution.py:399
  195.3 10.0 %shard_map.473.value_ref.refs_5_ = bf16[2,512,512]{2,1,0:T(8,128)(2,1)S(1)} custom-call(bf16[2,512,1536]{2,1,0:T(8,128)(2,1)S(1)} %shard_map.472.q_ref.k_ref.v_ref, bf16[2,512,1536]{2,1,0:T(8,128)(2,1)S(1)} %shard_map.472.q_ref.k_ref.v_ref, bf16[2,512,1536]{2,1,0:T(8,128)(2,1)S(1)} %shard_map.472.q_ref.k_ref.v_ref), custom_call_target="tpu_custom_call" | custom-call | flops 1 | bytes 1 | tf_op jit(solution)/shard_map/pallas_call | solution.py:674
  205.4 4.1 shard_map.474
  209.5 11.3 %shard_map.475 = (bf16[2,512,3072]{2,1,0:T(8,128)(2,1)}, bf16[2,512,1536]{2,1,0:T(8,128)(2,1)S(1)}) custom-call(bf16[512,1024]{1,0:T(8,128)(2,1)S(1)} %get-tuple-element.320.x_ref.refs_2_, bf16[2,1024,6656]{2,1,0:T(8,128)(2,1)} %bitcast.251), custom_call_target="tpu_custom_call" | custom-call | flops 1 | bytes 1 | tf_op jit(solution)/shard_map/pallas_call | solution.py:421
  222.4 7.6 %shard_map.476 = (f32[512,1024]{1,0:T(8,128)S(1)}, bf16[512,1024]{1,0:T(8,128)(2,1)S(1)}) custom-call(bf16[2,512,1536]{2,1,0:T(8,128)(2,1)} %copy-done.8, f32[512,1024]{1,0:T(8,128)S(1)} %get-tuple-element.325.resid_ref, f32[2,1024]{1,0:T(2,128)S(1)} %get-tuple-element.667.scale_ref, bf16[2,1024,6656]{2,1,0:T(8,128)(2,1)} %bitcast.252), custom_call_target="tpu_custom_call" | custom-call | flops 1 | bytes 1 | tf_op jit(solution)/shard_map/pallas_call | solution.py:505
  231.5 5.7 %shard_map.477 = (f32[2,128]{1,0:T(2,128)S(1)}, bf16[512,768]{1,0:T(8,128)(2,1)S(1)}, f32[512,1024]{1,0:T(8,128)}, bf16[512,1024]{1,0:T(8,128)(2,1)S(1)}, f32[2,1024]{1,0:T(2,128)S(1)}) custom-call(bf16[512,1024]{1,0:T(8,128)(2,1)S(1)} %get-tuple-element.329.last_ref.refs_3_, bf16[768,1024]{1,0:T(8,128)(2,1)S(1)} %copy-done.10, f32[512,768]{1,0:T(8,128)S(1)} %copy-done.15, ...), custom_call_target="tpu_custom_call" | custom-call | flops 1 | bytes 1 | tf_op jit(solution)/shard_map/pallas_call | solution.py:736
  237.2 9.0 %shard_map.479 = (bf16[2,512,1536]{2,1,0:T(8,128)(2,1)}, bf16[256,1536]{1,0:T(8,128)(2,1)}, bf16[256,1536]{1,0:T(8,128)(2,1)}, bf16[256,1536]{1,0:T(8,128)(2,1)S(1)}, bf16[256,1536]{1,0:T(8,128)(2,1)S(1)}) custom-call(bf16[1024,1024]{1,0:T(8,128)(2,1)} %fusion.refs_0_, s32[1]{0:T(128)} %bitcast.53.refs_1_, ...), custom_call_target="tpu_custom_call" | custom-call | flops 1 | bytes 1 | tf_op jit(solution)/shard_map/pallas_call | solution.py:605
  247.0 11.8 %shard_map.478.value_ref.refs_3_ = bf16[2,512,3072]{2,1,0:T(8,128)(2,1)} custom-call(bf16[512,1024]{1,0:T(8,128)(2,1)S(1)} %get-tuple-element.340.x_ref.refs_2_, bf16[2,512,3072]{2,1,0:T(8,128)(2,1)} %get-tuple-element.341.gated_ref, bf16[2,1024,6656]{2,1,0:T(8,128)(2,1)} %bitcast.253), custom_call_target="tpu_custom_call" | custom-call | flops 1 | bytes 1 | tf_op jit(solution)/shard_map/pallas_call | solution.py:458
  261.3 13.7 %shard_map.483 = (bf16[2,512,3072]{2,1,0:T(8,128)(2,1)}, bf16[256,3072]{1,0:T(8,128)(2,1)}, bf16[256,3072]{1,0:T(8,128)(2,1)S(1)}, bf16[256,3072]{1,0:T(8,128)(2,1)}, bf16[256,3072]{1,0:T(8,128)(2,1)}) custom-call(bf16[1024,1024]{1,0:T(8,128)(2,1)} %fusion.refs_0_, s32[1]{0:T(128)} %bitcast.53.refs_1_, ...), custom_call_target="tpu_custom_call" | custom-call | flops 1 | bytes 1 | tf_op jit(solution)/shard_map/pallas_call | solution.py:605
  280.5 12.3 %shard_map.480 = (f32[2,1024]{1,0:T(2,128)S(1)}, f32[512,1024]{1,0:T(8,128)S(1)}, bf16[512,1024]{1,0:T(8,128)(2,1)S(1)}) custom-call(bf16[2,512,3072]{2,1,0:T(8,128)(2,1)} %shard_map.478.value_ref.refs_3_, f32[512,1024]{1,0:T(8,128)S(1)} %get-tuple-element.325.resid_ref, f32[2,1024]{1,0:T(2,128)S(1)} %get-tuple-element.668.scale_ref, ...), custom_call_target="tpu_custom_call" | custom-call | flops 1 | bytes 1 | tf_op jit(solution)/shard_map/pallas_call | solution.py:551
  292.8 3.2 shard_map.481.grad_ref
  303.2 11.7 %shard_map.484.refs_4_.value_ref = bf16[2,512,1536]{2,1,0:T(8,128)(2,1)S(1)} custom-call(bf16[2,512,1536]{2,1,0:T(8,128)(2,1)} %copy-done.2, bf16[2,512,1536]{2,1,0:T(8,128)(2,1)} %copy-done.2, bf16[2,512,1536]{2,1,0:T(8,128)(2,1)} %copy-done.2, bf16[2,512,512]{2,1,0:T(8,128)(2,1)S(1)} %shard_map.481.grad_ref), custom_call_target="tpu_custom_call" | custom-call | flops 1 | bytes 1 | tf_op jit(solution)/shard_map/pallas_call | solution.py:704
  316.5 12.1 %shard_map.485 = (bf16[2,512,2048]{2,1,0:T(8,128)(2,1)}, bf16[256,2048]{1,0:T(8,128)(2,1)S(1)}, bf16[256,2048]{1,0:T(8,128)(2,1)}, bf16[256,2048]{1,0:T(8,128)(2,1)}, bf16[256,2048]{1,0:T(8,128)(2,1)}) custom-call(bf16[1024,1024]{1,0:T(8,128)(2,1)} %fusion.refs_0_, s32[1]{0:T(128)} %bitcast.53.refs_1_, bf16[512,1024]{1,0:T(8,128)(2,1)S(1)} %fusion.3.x_ref.refs_2_, ...), custom_call_target="tpu_custom_call" | custom-call | flops 1 | bytes 1 | tf_op jit(solution)/shard_map/pallas_call | solution.py:605
  329.6 5.4 shard_map.490
  340.9 7.4 %shard_map.488 = (f32[2,1024]{1,0:T(2,128)S(1)}, bf16[512,1024]{1,0:T(8,128)(2,1)S(1)}) custom-call(bf16[2,512,1536]{2,1,0:T(8,128)(2,1)} %copy-done.6, f32[512,1024]{1,0:T(8,128)S(1)} %copy-done.5, f32[2,1024]{1,0:T(2,128)S(1)} %get-tuple-element.669.scale_ref, f32[512,1024]{1,0:T(8,128)S(1)} %get-tuple-element.390.grad_ref, bf16[2,1024,6656]{2,1,0:T(8,128)(2,1)} %bitcast.256), custom_call_target="tpu_custom_call" | custom-call | flops 1 | bytes 1 | tf_op jit(solution)/shard_map/pallas_call | solution.py:551
  349.2 4.8 collective-permute-done.43
  354.0 3.7 collective-permute-done.42
  357.7 4.6 collective-permute-done.41
  363.8 7.1 %collective-permute-done.49 = bf16[64,1536]{1,0:T(8,128)(2,1)S(1)} collective-permute-done((bf16[64,1536]{1,0:T(8,128)(2,1)S(1)}, bf16[64,1536]{1,0:T(8,128)(2,1)S(1)}, u32[]{:S(2)}, u32[]{:S(2)}) %collective-permute-start.49) | collective-permute-done | bytes 196640 | tf_op jit(solution)/shard_map/ppermute | solution.py:216
  371.4 3.3 shard_map.489
  392.6 4.2 shard_map.493
  404.4 13.6 %collective-permute-done.61 = bf16[64,3072]{1,0:T(8,128)(2,1)} collective-permute-done((bf16[64,3072]{1,0:T(8,128)(2,1)}, bf16[64,3072]{1,0:T(8,128)(2,1)}, u32[]{:S(2)}, u32[]{:S(2)}) %collective-permute-start.61) | collective-permute-done | bytes 393248 | tf_op jit(solution)/shard_map/ppermute | solution.py:216
  440.0 8.7 %collective-permute-done.73 = bf16[64,3072]{1,0:T(8,128)(2,1)S(1)} collective-permute-done((bf16[64,3072]{1,0:T(8,128)(2,1)S(1)}, bf16[64,3072]{1,0:T(8,128)(2,1)S(1)}, u32[]{:S(2)}, u32[]{:S(2)}) %collective-permute-start.73) | collective-permute-done | bytes 393248 | tf_op jit(solution)/shard_map/ppermute | solution.py:216
  449.8 11.7 %collective-permute-done.70 = bf16[96,2048]{1,0:T(8,128)(2,1)S(1)} collective-permute-done((bf16[96,2048]{1,0:T(8,128)(2,1)S(1)}, bf16[96,2048]{1,0:T(8,128)(2,1)S(1)}, u32[]{:S(2)}, u32[]{:S(2)}) %collective-permute-start.70) | collective-permute-done | bytes 393248 | tf_op jit(solution)/shard_map/ppermute | solution.py:228
  479.3 10.8 %collective-permute-done.78 = bf16[24,2048]{1,0:T(8,128)(2,1)S(1)} collective-permute-done((bf16[24,2048]{1,0:T(8,128)(2,1)S(1)}, bf16[24,2048]{1,0:T(8,128)(2,1)S(1)}, u32[]{:S(2)}, u32[]{:S(2)}) %collective-permute-start.78) | collective-permute-done | bytes 98336 | tf_op jit(solution)/shard_map/ppermute | solution.py:216
  491.0 8.7 %collective-permute-done.77 = bf16[24,2048]{1,0:T(8,128)(2,1)S(1)} collective-permute-done((bf16[24,2048]{1,0:T(8,128)(2,1)S(1)}, bf16[24,2048]{1,0:T(8,128)(2,1)S(1)}, u32[]{:S(2)}, u32[]{:S(2)}) %collective-permute-start.77) | collective-permute-done | bytes 98336 | tf_op jit(solution)/shard_map/ppermute | solution.py:216
  (620 shorter events, 188.4 us)
Async XLA Ops:
  7.2 182.3 %all-gather.2.cloned.1.call-start = ((), (), s32[]{:S(2)}) async-start(), calls=%async_computation | async-start | bytes 28114944 | tf_op jit(solution)/shard_map/all_gather | solution.py:828
  18.2 23.8 %collective-permute-start.5 = (bf16[24,2048]{1,0:T(8,128)(2,1)S(1)}, bf16[24,2048]{1,0:T(8,128)(2,1)S(1)}, u32[]{:S(2)}, u32[]{:S(2)}) collective-permute-start(bf16[24,2048]{1,0:T(8,128)(2,1)S(1)} %pad_maximum_fusion.7), channel_id=1, source_target_pairs={{0,24},{2,26},{4,28},{6,30},{8,16},{10,18},{12,20},{14,22},{16,8},... | collective-permute-start | bytes 294920 | tf_op jit(solution)/shard_map/ppermute | solution.py:216
  19.2 22.9 %collective-permute-start.4 = (bf16[24,2048]{1,0:T(8,128)(2,1)S(1)}, bf16[24,2048]{1,0:T(8,128)(2,1)S(1)}, u32[]{:S(2)}, u32[]{:S(2)}) collective-permute-start(bf16[24,2048]{1,0:T(8,128)(2,1)S(1)} %pad_maximum_fusion.7), channel_id=1, source_target_pairs={{0,8},{2,10},{4,12},{6,14},{8,0},{10,2},{12,4},{14,6},{16,24},{18,... | collective-permute-start | bytes 294920 | tf_op jit(solution)/shard_map/ppermute | solution.py:216
  43.6 25.4 %collective-permute-start.8 = (bf16[96,2048]{1,0:T(8,128)(2,1)S(1)}, bf16[96,2048]{1,0:T(8,128)(2,1)S(1)}, u32[]{:S(2)}, u32[]{:S(2)}) collective-permute-start(bf16[96,2048]{1,0:T(8,128)(2,1)S(1)} %constant_dynamic-update-slice_fusion.refs_0_), channel_id=1, source_target_pairs={{0,1},{1,0},{2,3},{3,2},{4,5},{5,4},{6,7},{7,6},{8,9},{9,8},{10,11... | collective-permute-start | bytes 1179656 | tf_op jit(solution)/shard_map/ppermute | solution.py:228
  44.3 24.8 %collective-permute-start.7 = (bf16[96,2048]{1,0:T(8,128)(2,1)S(1)}, bf16[96,2048]{1,0:T(8,128)(2,1)S(1)}, u32[]{:S(2)}, u32[]{:S(2)}) collective-permute-start(bf16[96,2048]{1,0:T(8,128)(2,1)S(1)} %constant_dynamic-update-slice_fusion.refs_0_), channel_id=1, source_target_pairs={{0,4},{2,6},{4,0},{6,2},{8,12},{10,14},{12,8},{14,10},{16,20},{18,... | collective-permute-start | bytes 1179656 | tf_op jit(solution)/shard_map/ppermute | solution.py:216
  246.5 28.5 %collective-permute-start.30 = (bf16[256,1536]{1,0:T(8,128)(2,1)S(1)}, bf16[256,1536]{1,0:T(8,128)(2,1)S(1)}, u32[]{:S(2)}, u32[]{:S(2)}) collective-permute-start(bf16[256,1536]{1,0:T(8,128)(2,1)S(1)} %get-tuple-element.358), channel_id=1, source_target_pairs={{0,2},{2,0},{4,6},{6,4},{8,10},{10,8},{12,14},{14,12},{16,18},{18,... | collective-permute-start | bytes 2359304 | tf_op jit(solution)/shard_map/ppermute | solution.py:216
  246.7 28.2 %collective-permute-start.31 = (bf16[256,1536]{1,0:T(8,128)(2,1)}, bf16[256,1536]{1,0:T(8,128)(2,1)S(1)}, u32[]{:S(2)}, u32[]{:S(2)}) collective-permute-start(bf16[256,1536]{1,0:T(8,128)(2,1)} %get-tuple-element.359), channel_id=1, source_target_pairs={{0,2},{2,0},{4,6},{6,4},{8,10},{10,8},{12,14},{14,12},{16,18},{18,... | collective-permute-start | bytes 2359304 | tf_op jit(solution)/shard_map/ppermute | solution.py:216
  275.1 23.4 %collective-permute-start.37 = (bf16[256,1536]{1,0:T(8,128)(2,1)}, bf16[256,1536]{1,0:T(8,128)(2,1)S(1)}, u32[]{:S(2)}, u32[]{:S(2)}) collective-permute-start(bf16[256,1536]{1,0:T(8,128)(2,1)} %get-tuple-element.380), channel_id=1, source_target_pairs={{0,2},{2,0},{4,6},{6,4},{8,10},{10,8},{12,14},{14,12},{16,18},{18,... | collective-permute-start | bytes 2359304 | tf_op jit(solution)/shard_map/ppermute | solution.py:216
  277.9 22.8 %collective-permute-start.38 = (bf16[256,1536]{1,0:T(8,128)(2,1)S(1)}, bf16[256,1536]{1,0:T(8,128)(2,1)S(1)}, u32[]{:S(2)}, u32[]{:S(2)}) collective-permute-start(bf16[256,1536]{1,0:T(8,128)(2,1)S(1)} %get-tuple-element.385), channel_id=1, source_target_pairs={{0,1},{1,0},{2,3},{3,2},{4,5},{5,4},{6,7},{7,6},{8,9},{9,8},{10,11... | collective-permute-start | bytes 2359304 | tf_op jit(solution)/shard_map/ppermute | solution.py:228
  279.4 49.3 %collective-permute-start.35 = (bf16[256,3072]{1,0:T(8,128)(2,1)}, bf16[256,3072]{1,0:T(8,128)(2,1)}, u32[]{:S(2)}, u32[]{:S(2)}) collective-permute-start(bf16[256,3072]{1,0:T(8,128)(2,1)} %get-tuple-element.374), channel_id=1, source_target_pairs={{0,2},{2,0},{4,6},{6,4},{8,10},{10,8},{12,14},{14,12},{16,18},{18,... | collective-permute-start | bytes 4718600 | tf_op jit(solution)/shard_map/ppermute | solution.py:216
  279.4 49.3 %collective-permute-start.36 = (bf16[256,3072]{1,0:T(8,128)(2,1)S(1)}, bf16[256,3072]{1,0:T(8,128)(2,1)}, u32[]{:S(2)}, u32[]{:S(2)}) collective-permute-start(bf16[256,3072]{1,0:T(8,128)(2,1)S(1)} %get-tuple-element.375), channel_id=1, source_target_pairs={{0,2},{2,0},{4,6},{6,4},{8,10},{10,8},{12,14},{14,12},{16,18},{18,... | collective-permute-start | bytes 4718600 | tf_op jit(solution)/shard_map/ppermute | solution.py:216
  279.9 22.4 %collective-permute-start.39 = (bf16[256,1536]{1,0:T(8,128)(2,1)}, bf16[256,1536]{1,0:T(8,128)(2,1)S(1)}, u32[]{:S(2)}, u32[]{:S(2)}) collective-permute-start(bf16[256,1536]{1,0:T(8,128)(2,1)} %get-tuple-element.386), channel_id=1, source_target_pairs={{0,4},{2,6},{4,0},{6,2},{8,12},{10,14},{12,8},{14,10},{16,20},{18,... | collective-permute-start | bytes 2359304 | tf_op jit(solution)/shard_map/ppermute | solution.py:216
  299.4 29.3 %collective-permute-start.33 = (bf16[128,3072]{1,0:T(8,128)(2,1)S(1)}, bf16[128,3072]{1,0:T(8,128)(2,1)S(1)}, u32[]{:S(2)}, u32[]{:S(2)}) collective-permute-start(bf16[128,3072]{1,0:T(8,128)(2,1)S(1)} %get-tuple-element.372), channel_id=1, source_target_pairs={{0,4},{2,6},{4,0},{6,2},{8,12},{10,14},{12,8},{14,10},{16,20},{18,... | collective-permute-start | bytes 2359304 | tf_op jit(solution)/shard_map/ppermute | solution.py:216
  301.7 27.0 %collective-permute-start.34 = (bf16[128,3072]{1,0:T(8,128)(2,1)S(1)}, bf16[128,3072]{1,0:T(8,128)(2,1)S(1)}, u32[]{:S(2)}, u32[]{:S(2)}) collective-permute-start(bf16[128,3072]{1,0:T(8,128)(2,1)S(1)} %get-tuple-element.373), channel_id=1, source_target_pairs={{0,1},{1,0},{2,3},{3,2},{4,5},{5,4},{6,7},{7,6},{8,9},{9,8},{10,11... | collective-permute-start | bytes 2359304 | tf_op jit(solution)/shard_map/ppermute | solution.py:228
  303.2 45.2 %collective-permute-start.45 = (bf16[256,3072]{1,0:T(8,128)(2,1)}, bf16[256,3072]{1,0:T(8,128)(2,1)S(1)}, u32[]{:S(2)}, u32[]{:S(2)}) collective-permute-start(bf16[256,3072]{1,0:T(8,128)(2,1)} %get-tuple-element.401), channel_id=1, source_target_pairs={{0,2},{2,0},{4,6},{6,4},{8,10},{10,8},{12,14},{14,12},{16,18},{18,... | collective-permute-start | bytes 4718600 | tf_op jit(solution)/shard_map/ppermute | solution.py:216
  335.0 39.6 %collective-permute-start.46 = (bf16[256,3072]{1,0:T(8,128)(2,1)}, bf16[256,3072]{1,0:T(8,128)(2,1)S(1)}, u32[]{:S(2)}, u32[]{:S(2)}) collective-permute-start(bf16[256,3072]{1,0:T(8,128)(2,1)} %get-tuple-element.406), channel_id=1, source_target_pairs={{0,1},{1,0},{2,3},{3,2},{4,5},{5,4},{6,7},{7,6},{8,9},{9,8},{10,11... | collective-permute-start | bytes 4718600 | tf_op jit(solution)/shard_map/ppermute | solution.py:228
  336.5 38.2 %collective-permute-start.47 = (bf16[256,3072]{1,0:T(8,128)(2,1)}, bf16[256,3072]{1,0:T(8,128)(2,1)}, u32[]{:S(2)}, u32[]{:S(2)}) collective-permute-start(bf16[256,3072]{1,0:T(8,128)(2,1)} %get-tuple-element.407), channel_id=1, source_target_pairs={{0,4},{2,6},{4,0},{6,2},{8,12},{10,14},{12,8},{14,10},{16,20},{18,... | collective-permute-start | bytes 4718600 | tf_op jit(solution)/shard_map/ppermute | solution.py:216
  339.4 22.9 %collective-permute-start.48 = (bf16[64,1536]{1,0:T(8,128)(2,1)S(1)}, bf16[64,1536]{1,0:T(8,128)(2,1)S(1)}, u32[]{:S(2)}, u32[]{:S(2)}) collective-permute-start(bf16[64,1536]{1,0:T(8,128)(2,1)S(1)} %get-tuple-element.413), channel_id=1, source_target_pairs={{0,16},{2,18},{4,20},{6,22},{8,24},{10,26},{12,28},{14,30},{16,0},... | collective-permute-start | bytes 589832 | tf_op jit(solution)/shard_map/ppermute | solution.py:216
  340.9 33.7 %collective-permute-start.44 = (bf16[256,2048]{1,0:T(8,128)(2,1)}, bf16[256,2048]{1,0:T(8,128)(2,1)S(1)}, u32[]{:S(2)}, u32[]{:S(2)}) collective-permute-start(bf16[256,2048]{1,0:T(8,128)(2,1)} %get-tuple-element.395), channel_id=1, source_target_pairs={{0,2},{2,0},{4,6},{6,4},{8,10},{10,8},{12,14},{14,12},{16,18},{18,... | collective-permute-start | bytes 3145736 | tf_op jit(solution)/shard_map/ppermute | solution.py:216
  374.7 22.9 %collective-permute-start.62 = (bf16[96,2048]{1,0:T(8,128)(2,1)}, bf16[96,2048]{1,0:T(8,128)(2,1)}, u32[]{:S(2)}, u32[]{:S(2)}) collective-permute-start(bf16[96,2048]{1,0:T(8,128)(2,1)} %get-tuple-element.434), channel_id=1, source_target_pairs={{0,2},{2,0},{4,6},{6,4},{8,10},{10,8},{12,14},{14,12},{16,18},{18,... | collective-permute-start | bytes 1179656 | tf_op jit(solution)/shard_map/ppermute | solution.py:216
  390.4 27.6 %collective-permute-start.57 = (bf16[128,2048]{1,0:T(8,128)(2,1)}, bf16[128,2048]{1,0:T(8,128)(2,1)}, u32[]{:S(2)}, u32[]{:S(2)}) collective-permute-start(bf16[128,2048]{1,0:T(8,128)(2,1)} %get-tuple-element.423), channel_id=1, source_target_pairs={{0,4},{2,6},{4,0},{6,2},{8,12},{10,14},{12,8},{14,10},{16,20},{18,... | collective-permute-start | bytes 1572872 | tf_op jit(solution)/shard_map/ppermute | solution.py:216
  391.9 26.7 %collective-permute-start.58 = (bf16[128,2048]{1,0:T(8,128)(2,1)}, bf16[128,2048]{1,0:T(8,128)(2,1)}, u32[]{:S(2)}, u32[]{:S(2)}) collective-permute-start(bf16[128,2048]{1,0:T(8,128)(2,1)} %get-tuple-element.424), channel_id=1, source_target_pairs={{0,1},{1,0},{2,3},{3,2},{4,5},{5,4},{6,7},{7,6},{8,9},{9,8},{10,11... | collective-permute-start | bytes 1572872 | tf_op jit(solution)/shard_map/ppermute | solution.py:228
  397.6 20.5 %collective-permute-start.61 = (bf16[64,3072]{1,0:T(8,128)(2,1)}, bf16[64,3072]{1,0:T(8,128)(2,1)}, u32[]{:S(2)}, u32[]{:S(2)}) collective-permute-start(bf16[64,3072]{1,0:T(8,128)(2,1)} %get-tuple-element.432), channel_id=1, source_target_pairs={{0,16},{2,18},{4,20},{6,22},{8,24},{10,26},{12,28},{14,30},{16,0},... | collective-permute-start | bytes 1179656 | tf_op jit(solution)/shard_map/ppermute | solution.py:216
  427.7 35.9 %collective-permute-start.67 = (bf16[256,2048]{1,0:T(8,128)(2,1)}, bf16[256,2048]{1,0:T(8,128)(2,1)}, u32[]{:S(2)}, u32[]{:S(2)}) collective-permute-start(bf16[256,2048]{1,0:T(8,128)(2,1)} %copy-done.36), channel_id=1, source_target_pairs={{0,1},{1,0},{2,3},{3,2},{4,5},{5,4},{6,7},{7,6},{8,9},{9,8},{10,11... | collective-permute-start | bytes 3145736 | tf_op jit(solution)/shard_map/ppermute | solution.py:228
  428.9 34.7 %collective-permute-start.68 = (bf16[256,2048]{1,0:T(8,128)(2,1)}, bf16[256,2048]{1,0:T(8,128)(2,1)}, u32[]{:S(2)}, u32[]{:S(2)}) collective-permute-start(bf16[256,2048]{1,0:T(8,128)(2,1)} %copy-done.35), channel_id=1, source_target_pairs={{0,4},{2,6},{4,0},{6,2},{8,12},{10,14},{12,8},{14,10},{16,20},{18,... | collective-permute-start | bytes 3145736 | tf_op jit(solution)/shard_map/ppermute | solution.py:216
  437.3 24.2 %collective-permute-start.70 = (bf16[96,2048]{1,0:T(8,128)(2,1)S(1)}, bf16[96,2048]{1,0:T(8,128)(2,1)S(1)}, u32[]{:S(2)}, u32[]{:S(2)}) collective-permute-start(bf16[96,2048]{1,0:T(8,128)(2,1)S(1)} %get-tuple-element.451), channel_id=1, source_target_pairs={{0,1},{1,0},{2,3},{3,2},{4,5},{5,4},{6,7},{7,6},{8,9},{9,8},{10,11... | collective-permute-start | bytes 1179656 | tf_op jit(solution)/shard_map/ppermute | solution.py:228
  438.5 25.1 %collective-permute-start.71 = (bf16[96,2048]{1,0:T(8,128)(2,1)S(1)}, bf16[96,2048]{1,0:T(8,128)(2,1)S(1)}, u32[]{:S(2)}, u32[]{:S(2)}) collective-permute-start(bf16[96,2048]{1,0:T(8,128)(2,1)S(1)} %get-tuple-element.452), channel_id=1, source_target_pairs={{0,4},{2,6},{4,0},{6,2},{8,12},{10,14},{12,8},{14,10},{16,20},{18,... | collective-permute-start | bytes 1179656 | tf_op jit(solution)/shard_map/ppermute | solution.py:216
  448.7 27.2 %collective-permute-start.81 = (bf16[2,8,4800]{2,1,0:T(8,128)(2,1)}, bf16[2,8,4800]{2,1,0:T(8,128)(2,1)}, u32[]{:S(2)}, u32[]{:S(2)}) collective-permute-start(bf16[2,8,4800]{2,1,0:T(8,128)(2,1)} %pad_maximum_fusion.6), channel_id=1, source_target_pairs={{0,4},{2,6},{4,0},{6,2},{8,12},{10,14},{12,8},{14,10},{16,20},{18,... | collective-permute-start | bytes 460808 | tf_op jit(solution)/shard_map/ppermute | solution.py:216
  471.5 28.2 %collective-permute-start.74 = (bf16[64,2048]{1,0:T(8,128)(2,1)S(1)}, bf16[64,2048]{1,0:T(8,128)(2,1)S(1)}, u32[]{:S(2)}, u32[]{:S(2)}) collective-permute-start(bf16[64,2048]{1,0:T(8,128)(2,1)S(1)} %get-tuple-element.463), channel_id=1, source_target_pairs={{0,16},{2,18},{4,20},{6,22},{8,24},{10,26},{12,28},{14,30},{16,0},... | collective-permute-start | bytes 786440 | tf_op jit(solution)/shard_map/ppermute | solution.py:216
  473.0 26.6 %collective-permute-start.75 = (bf16[64,2048]{1,0:T(8,128)(2,1)S(1)}, bf16[64,2048]{1,0:T(8,128)(2,1)S(1)}, u32[]{:S(2)}, u32[]{:S(2)}) collective-permute-start(bf16[64,2048]{1,0:T(8,128)(2,1)S(1)} %get-tuple-element.464), channel_id=1, source_target_pairs={{0,8},{2,10},{4,12},{6,14},{8,0},{10,2},{12,4},{14,6},{16,24},{18,... | collective-permute-start | bytes 786440 | tf_op jit(solution)/shard_map/ppermute | solution.py:216
  473.9 25.8 %collective-permute-start.76 = (bf16[64,2048]{1,0:T(8,128)(2,1)S(1)}, bf16[64,2048]{1,0:T(8,128)(2,1)S(1)}, u32[]{:S(2)}, u32[]{:S(2)}) collective-permute-start(bf16[64,2048]{1,0:T(8,128)(2,1)S(1)} %get-tuple-element.465), channel_id=1, source_target_pairs={{0,24},{2,26},{4,28},{6,30},{8,16},{10,18},{12,20},{14,22},{16,8},... | collective-permute-start | bytes 786440 | tf_op jit(solution)/shard_map/ppermute | solution.py:216
  476.2 23.4 %collective-permute-start.77 = (bf16[24,2048]{1,0:T(8,128)(2,1)S(1)}, bf16[24,2048]{1,0:T(8,128)(2,1)S(1)}, u32[]{:S(2)}, u32[]{:S(2)}) collective-permute-start(bf16[24,2048]{1,0:T(8,128)(2,1)S(1)} %copy-done.91), channel_id=1, source_target_pairs={{0,16},{2,18},{4,20},{6,22},{8,24},{10,26},{12,28},{14,30},{16,0},... | collective-permute-start | bytes 294920 | tf_op jit(solution)/shard_map/ppermute | solution.py:216
  (201 other events, 1772.7 us)
Sparse Core Ops, SparseCore 0:
  13.0 176.4 all-gather.1
